TPU v7x, 32 devices: a whole 2x2x4 slice. The times are simulated.
32 devices in a mesh: seq: 8 (over z, y), tp: 4 (over x, core).
Axes of the slice: x: 2, y: 2, z: 4, core: 2. Of those that a mesh axis runs over, the one named last changes fastest.
Arguments:
- tokens: bfloat16 [1024, 1024], P('seq'), may hold values from -6 to 6
- norm_gain: float32 [1024], replicated, may hold values from 0.25 to 1.75
- w_qkv: bfloat16 [1024, 3, 1024], P(None, None, 'tp'), may hold values from -1 to 1
- w_out: bfloat16 [1024, 1024], P('tp'), may hold values from -0.1875 to 0.1875
- head_bias: float32 [2, 16], P(None, 'tp'), may hold values from -1.5 to 1.5
- kv_pool: bfloat16 [32, 128, 2, 1024], P('seq', None, None, 'tp'), may hold values from -6 to 6
- key_variate: int32 [32, 128], P('seq'), may hold values from 0 to 7
- page_table: int32 [8, 4], P('seq'), may hold values from 0 to 3, each once within a row
- node_len: int32 [8], P('seq'), may hold values from 1 to 512, 3072 in all
- path_nodes: int32 [1024, 3], P('seq'), may hold values from 0 to 7, all different within a row; in each aligned block of 128 rows (0 to 127, 128 to 255, ...) at most 128 rows name the same one
- query_variate: int32 [1024], P('seq'), may hold values from 0 to 7
Outputs:
- updated: bfloat16 [1024, 1024], P('seq')
Inputs may be any that keep to these rules, and one draw needn't show every extreme that they name: `path_nodes`: each row names three different nodes; the rows of one device name one node at most 128 times, a bound that some block reaches. `page_table`: each row is a permutation. `node_len`: some node holds exactly 512 tokens.
All inputs are finite; a program needn't handle non-finite values. No bound on the sum of `node_len` on one device may be relied on, other than what follows from the above.
Results may differ from a plain program's by a relative error of at most 0.0033.
The roundings to bfloat16 on the way count: a program that leaves them out, or rounds other values in their place, can miss the bound.
Values may be sent and summed in bfloat16 or wider, within the bound.
No kernel may reach another device: no remote copies, remote signals or barrier semaphores. Data moves between devices by JAX's collectives and lax.ppermute only.
A program may use at most 64 MiB of HBM per device.

v0:
```python
import jax
import jax.numpy as jnp
from jax import lax
from jax.sharding import PartitionSpec as P

HD = 64


def head_attend(qh, kh, vh, same, bias_same, bias_diff, valid):
    scores = jnp.dot(qh, kh.T, preferred_element_type=jnp.float32) * HD ** (-0.5)
    scores = scores + jnp.where(same, bias_same, bias_diff)
    scores = jnp.where(valid[None, :], scores, -1e30)
    peak = jnp.max(scores, axis=1)
    weights = jnp.exp(scores - peak[:, None])
    total = jnp.sum(weights, axis=1)
    mixed = (
        jnp.dot(weights.astype(jnp.bfloat16), vh, preferred_element_type=jnp.float32)
        / total[:, None]
    )
    mixed = lax.optimization_barrier(mixed.astype(jnp.bfloat16))
    return (mixed, peak, total)


def place_rows(dest, values, variates, owners, slots):
    onehot = (dest[:, None] == jnp.arange(owners, dtype=jnp.int32)[None, :]).astype(jnp.int32)
    before = jnp.cumsum(onehot, axis=0) - onehot
    slot = jnp.sum(before * onehot, axis=1)
    flat = dest * slots + slot
    width = values.shape[1]
    qbuf = (
        jnp.zeros((owners * slots, width), jnp.bfloat16)
        .at[flat]
        .set(values)
        .reshape(owners, slots, width)
    )
    vbuf = jnp.zeros((owners * slots,), jnp.int32).at[flat].set(variates).reshape(owners, slots)
    return (qbuf, vbuf, flat)


def body(
    tokens,
    norm_gain,
    w_qkv,
    w_out,
    head_bias,
    kv_pool,
    key_variate,
    page_table,
    node_len,
    path_nodes,
    query_variate,
):
    tok_rows, width = tokens.shape
    heads_here = w_qkv.shape[2] // HD
    owners = lax.axis_size("seq")
    slots = min(tok_rows, 8 * tok_rows // owners)
    xf = tokens.astype(jnp.float32)
    normed = (xf * lax.rsqrt(jnp.mean(xf * xf, axis=1, keepdims=True) + 1e-05) * norm_gain).astype(
        jnp.bfloat16
    )
    qkv = jnp.dot(
        normed, w_qkv.reshape(width, 3 * heads_here * HD), preferred_element_type=jnp.float32
    ).astype(jnp.bfloat16)
    qkv = qkv.reshape(tok_rows, 3, heads_here, HD)
    query, key, value = (qkv[:, 0], qkv[:, 1], qkv[:, 2])
    order = page_table[0]
    node_slots = kv_pool.shape[0] * kv_pool.shape[1]
    pages = kv_pool[order].reshape(node_slots, 2, heads_here, HD)
    node_keys = jnp.moveaxis(pages[:, 0], 1, 0)
    node_values = jnp.moveaxis(pages[:, 1], 1, 0)
    key_var = key_variate[order].reshape(node_slots)
    valid = jnp.arange(node_slots, dtype=jnp.int32) < node_len[0]
    qflat = query.reshape(tok_rows, heads_here * HD)
    out_list, peak_list, total_list = ([], [], [])
    for level in range(3):
        qbuf, vbuf, flat = place_rows(path_nodes[:, level], qflat, query_variate, owners, slots)
        owner_qbuf = lax.all_to_all(qbuf, "seq", split_axis=0, concat_axis=0, tiled=True)
        owner_vbuf = lax.all_to_all(vbuf, "seq", split_axis=0, concat_axis=0, tiled=True)
        sources, count, cols = owner_qbuf.shape
        rows = sources * count
        heads_q = jnp.moveaxis(owner_qbuf.reshape(rows, heads_here, HD), 1, 0)
        same = owner_vbuf.reshape(rows)[:, None] == key_var[None, :]

        def per_head(xs):
            return head_attend(xs[0], xs[1], xs[2], same, xs[3], xs[4], valid)

        mixed, peak, total = lax.map(
            per_head, (heads_q, node_keys, node_values, head_bias[1], head_bias[0])
        )
        mixed = jnp.moveaxis(mixed, 0, 1).reshape(sources, count, cols)
        peak = peak.T.reshape(sources, count, heads_here)
        total = total.T.reshape(sources, count, heads_here)
        mixed_back = lax.all_to_all(mixed, "seq", split_axis=0, concat_axis=0, tiled=True)
        peak_back = lax.all_to_all(peak, "seq", split_axis=0, concat_axis=0, tiled=True)
        total_back = lax.all_to_all(total, "seq", split_axis=0, concat_axis=0, tiled=True)
        mixed = mixed_back
        peak = peak_back
        total = total_back
        out_list.append(mixed.reshape(owners * slots, -1)[flat].reshape(tok_rows, heads_here, HD))
        peak_list.append(peak.reshape(owners * slots, heads_here)[flat])
        total_list.append(total.reshape(owners * slots, heads_here)[flat])
    outs = jnp.stack(out_list, axis=1)
    peaks = jnp.stack(peak_list, axis=1)
    totals = jnp.stack(total_list, axis=1)
    own_peak = (
        jnp.sum(query.astype(jnp.float32) * key.astype(jnp.float32), axis=2) * HD ** (-0.5)
        + head_bias[1][None, :]
    )
    all_o = jnp.concatenate([value.astype(jnp.float32)[:, None], outs.astype(jnp.float32)], axis=1)
    all_m = jnp.concatenate([own_peak[:, None], peaks], axis=1)
    all_l = jnp.concatenate([jnp.ones((tok_rows, 1, heads_here), jnp.float32), totals], axis=1)
    top = jnp.max(all_m, axis=1, keepdims=True)
    scale = all_l * jnp.exp(all_m - top)
    attn = (jnp.sum(scale[..., None] * all_o, axis=1) / jnp.sum(scale, axis=1)[..., None]).astype(
        jnp.bfloat16
    )
    partial_sum = jnp.dot(
        attn.reshape(tok_rows, heads_here * HD), w_out, preferred_element_type=jnp.float32
    )
    total_sum = lax.psum(partial_sum, "tp")
    return (xf + total_sum).astype(jnp.bfloat16)


def solution(mesh):
    in_specs = (
        P("seq", None),
        P(),
        P(None, None, "tp"),
        P("tp", None),
        P(None, "tp"),
        P("seq", None, None, "tp"),
        P("seq", None),
        P("seq", None),
        P("seq"),
        P("seq", None),
        P("seq"),
    )
    out_specs = P("seq", None)
    return jax.shard_map(body, mesh=mesh, in_specs=in_specs, out_specs=out_specs, check_vma=False)
```

profile of v0, /device:TPU:0, one launch (start us, length us, event | category | flops | bytes accessed | tf_op | source)
XLA Modules:
  0.0 328.2 jit_solution(2540543669957967379)
XLA Ops:
  10.0 1.7 scatter_custom_fusion.5
  11.7 7.3 %all-to-all-start.7 = ((s32[8,1,128]{2,1,0:T(1,128)}), s32[8,1,128]{2,1,0:T(1,128)S(1)}, u32[]{:S(2)}, u32[]{:S(2)}) async-start(s32[8,1,128]{2,1,0:T(1,128)} %bitcast.42), calls=%async_computation.7 | async-start | bytes 8192 | tf_op jit(solution)/shard_map/all_to_all | solution.py:78
  20.1 1.7 copy.125
  21.8 1.7 scatter_custom_fusion.3
  23.5 1.9 all-to-all-done.7
  25.4 4.1 %all-to-all-start.4 = ((s32[8,1,128]{2,1,0:T(1,128)}), s32[8,1,128]{2,1,0:T(1,128)S(1)}, u32[]{:S(2)}, u32[]{:S(2)}) async-start(s32[8,1,128]{2,1,0:T(1,128)} %bitcast.31), calls=%async_computation.4 | async-start | bytes 8192 | tf_op jit(solution)/shard_map/all_to_all | solution.py:78
  30.3 1.7 scatter_custom_fusion.1
  32.0 3.9 %all-to-all-done.4 = s32[8,1,128]{2,1,0:T(1,128)S(1)} async-done(((s32[8,1,128]{2,1,0:T(1,128)}), s32[8,1,128]{2,1,0:T(1,128)S(1)}, u32[]{:S(2)}, u32[]{:S(2)}) %all-to-all-start.4) | async-done | bytes 4128 | tf_op jit(solution)/shard_map/all_to_all | solution.py:78
  36.0 3.3 %all-to-all-start.1 = ((s32[8,1,128]{2,1,0:T(1,128)}), s32[8,1,128]{2,1,0:T(1,128)S(1)}, u32[]{:S(2)}, u32[]{:S(2)}) async-start(s32[8,1,128]{2,1,0:T(1,128)} %bitcast.18), calls=%async_computation.1 | async-start | bytes 8192 | tf_op jit(solution)/shard_map/all_to_all | solution.py:78
  41.6 4.0 %all-to-all-done.1 = s32[8,1,128]{2,1,0:T(1,128)S(1)} async-done(((s32[8,1,128]{2,1,0:T(1,128)}), s32[8,1,128]{2,1,0:T(1,128)S(1)}, u32[]{:S(2)}, u32[]{:S(2)}) %all-to-all-start.1) | async-done | bytes 4128 | tf_op jit(solution)/shard_map/all_to_all | solution.py:78
  45.6 3.5 %all-to-all-start.6 = ((bf16[8,128,256]{1,2,0:T(8,128)(2,1)}), bf16[8,128,256]{1,2,0:T(8,128)(2,1)S(1)}, u32[]{:S(2)}, u32[]{:S(2)}) async-start(bf16[8,128,256]{1,2,0:T(8,128)(2,1)} %copy.143), calls=%async_computation.6 | async-start | bytes 1048576 | tf_op jit(solution)/shard_map/all_to_all | solution.py:77
  51.4 9.3 %all-to-all-done.6 = bf16[8,128,256]{1,2,0:T(8,128)(2,1)S(1)} async-done(((bf16[8,128,256]{1,2,0:T(8,128)(2,1)}), bf16[8,128,256]{1,2,0:T(8,128)(2,1)S(1)}, u32[]{:S(2)}, u32[]{:S(2)}) %all-to-all-start.6) | async-done | bytes 524320 | tf_op jit(solution)/shard_map/all_to_all | solution.py:77
  60.6 3.7 %all-to-all-start.3 = ((bf16[8,128,256]{1,2,0:T(8,128)(2,1)}), bf16[8,128,256]{1,2,0:T(8,128)(2,1)S(1)}, u32[]{:S(2)}, u32[]{:S(2)}) async-start(bf16[8,128,256]{1,2,0:T(8,128)(2,1)} %copy.136), calls=%async_computation.3 | async-start | bytes 1048576 | tf_op jit(solution)/shard_map/all_to_all | solution.py:77
  64.3 1.6 gather_fusion
  72.5 5.1 %all-to-all-done.3 = bf16[8,128,256]{1,2,0:T(8,128)(2,1)S(1)} async-done(((bf16[8,128,256]{1,2,0:T(8,128)(2,1)}), bf16[8,128,256]{1,2,0:T(8,128)(2,1)S(1)}, u32[]{:S(2)}, u32[]{:S(2)}) %all-to-all-start.3) | async-done | bytes 524320 | tf_op jit(solution)/shard_map/all_to_all | solution.py:77
  77.5 3.7 %all-to-all-start = ((bf16[8,128,256]{1,2,0:T(8,128)(2,1)}), bf16[8,128,256]{1,2,0:T(8,128)(2,1)S(1)}, u32[]{:S(2)}, u32[]{:S(2)}) async-start(bf16[8,128,256]{1,2,0:T(8,128)(2,1)} %copy.128), calls=%async_computation | async-start | bytes 1048576 | tf_op jit(solution)/shard_map/all_to_all | solution.py:77
  81.9 31.1 %while.47 = (s32[]{:T(128)}, bf16[4,1024,64]{1,2,0:T(8,128)(2,1)S(1)}, f32[4,1024]{1,0:T(4,128)}, f32[4,1024]{1,0:T(4,128)S(1)}, bf16[4,1024,64]{1,2,0:T(8,128)(...) while((s32[]{:T(128)}, ...), condition=%wide.region_24.25_spmd.clone, body=%wide.region_21.24_spmd.clone.sunk | while | flops 139590144 | bytes 7124153 | solution.py:87
  83.8 2.7 fusion.114
  91.6 2.7 fusion.114
  94.6 1.4 fusion.116
  99.4 2.7 fusion.114
  107.1 2.7 fusion.114
  114.4 6.0 %all-to-all-start.11 = ((f32[8,128,4]{1,2,0:T(4,128)}), f32[8,128,4]{1,2,0:T(4,128)S(1)}, u32[]{:S(2)}, u32[]{:S(2)}) async-start(f32[8,128,4]{1,2,0:T(4,128)} %bitcast.58), calls=%async_computation.11 | async-start | bytes 32768 | tf_op jit(solution)/shard_map/all_to_all | solution.py:94
  121.1 31.5 %while.46 = (s32[]{:T(128)}, bf16[4,1024,64]{1,2,0:T(8,128)(2,1)S(1)}, f32[4,1024]{1,0:T(4,128)}, f32[4,1024]{1,0:T(4,128)S(1)}, bf16[4,1024,64]{1,2,0:T(8,128)(...) while((s32[]{:T(128)}, ...), condition=%wide.region_16.17_spmd.clone, body=%wide.region_13.16_spmd.clone.sunk | while | flops 139590144 | bytes 7124153 | solution.py:87
  123.0 2.8 fusion.109
  130.9 2.8 fusion.109
  138.7 2.8 fusion.109
  146.6 2.8 fusion.109
  153.9 6.0 %all-to-all-start.10 = ((f32[8,128,4]{1,2,0:T(4,128)}), f32[8,128,4]{1,2,0:T(4,128)S(1)}, u32[]{:S(2)}, u32[]{:S(2)}) async-start(f32[8,128,4]{1,2,0:T(4,128)} %bitcast.54), calls=%async_computation.10 | async-start | bytes 32768 | tf_op jit(solution)/shard_map/all_to_all | solution.py:94
  160.6 31.5 %while.45 = (s32[]{:T(128)}, bf16[4,1024,64]{1,2,0:T(8,128)(2,1)S(1)}, f32[4,1024]{1,0:T(4,128)S(1)}, f32[4,1024]{1,0:T(4,128)}, bf16[4,1024,64]{1,2,0:T(8,128)(...) while((s32[]{:T(128)}, ...), condition=%wide.region_8.9_spmd.clone, body=%wide.region_5.8_spmd.clone.sunk | while | flops 139590144 | bytes 7124153 | solution.py:87
  162.5 2.8 fusion.104
  170.4 2.8 fusion.104
  178.3 2.8 fusion.104
  186.2 2.8 fusion.104
  192.2 12.3 %all_to_all.87 = f32[8,128,4]{1,2,0:T(4,128)S(1)} all-to-all(f32[8,128,4]{1,2,0:T(4,128)S(1)} %bitcast.275), channel_id=1, replica_groups=mesh['seq'=8,'tp'=4] {'seq'}, dimensions={0} | all-to-all | bytes 32768 | tf_op jit(solution)/shard_map/all_to_all | solution.py:94
  204.5 8.9 %all_to_all.88 = f32[8,128,4]{1,2,0:T(4,128)S(1)} all-to-all(f32[8,128,4]{1,2,0:T(4,128)S(1)} %bitcast.276), channel_id=1, replica_groups=mesh['seq'=8,'tp'=4] {'seq'}, dimensions={0} | all-to-all | bytes 32768 | tf_op jit(solution)/shard_map/all_to_all | solution.py:95
  213.4 8.9 %all_to_all.89 = f32[8,128,4]{1,2,0:T(4,128)S(1)} all-to-all(f32[8,128,4]{1,2,0:T(4,128)S(1)} %bitcast.277), channel_id=1, replica_groups=mesh['seq'=8,'tp'=4] {'seq'}, dimensions={0} | all-to-all | bytes 32768 | tf_op jit(solution)/shard_map/all_to_all | solution.py:95
  222.4 3.3 %all-to-all-start.2 = ((f32[8,128,4]{1,2,0:T(4,128)}), f32[8,128,4]{1,2,0:T(4,128)S(1)}, u32[]{:S(2)}, u32[]{:S(2)}) async-start(f32[8,128,4]{1,2,0:T(4,128)} %bitcast.21), calls=%async_computation.2 | async-start | bytes 32768 | tf_op jit(solution)/shard_map/all_to_all | solution.py:95
  227.0 5.3 %all-to-all-done.2 = f32[8,128,4]{1,2,0:T(4,128)S(1)} async-done(((f32[8,128,4]{1,2,0:T(4,128)}), f32[8,128,4]{1,2,0:T(4,128)S(1)}, u32[]{:S(2)}, u32[]{:S(2)}) %all-to-all-start.2) | async-done | bytes 16416 | tf_op jit(solution)/shard_map/all_to_all | solution.py:95
  232.3 3.5 %all-to-all-start.14 = ((bf16[8,128,256]{2,1,0:T(8,128)(2,1)}), bf16[8,128,256]{2,1,0:T(8,128)(2,1)S(1)}, u32[]{:S(2)}, u32[]{:S(2)}) async-start(bf16[8,128,256]{2,1,0:T(8,128)(2,1)} %copy.165), calls=%async_computation.14 | async-start | bytes 1048576 | tf_op jit(solution)/shard_map/all_to_all | solution.py:93
  237.0 9.3 %all-to-all-done.14 = bf16[8,128,256]{2,1,0:T(8,128)(2,1)S(1)} async-done(((bf16[8,128,256]{2,1,0:T(8,128)(2,1)}), bf16[8,128,256]{2,1,0:T(8,128)(2,1)S(1)}, u32[]{:S(2)}, u32[]{:S(2)}) %all-to-all-start.14) | async-done | bytes 524320 | tf_op jit(solution)/shard_map/all_to_all | solution.py:93
  246.3 7.4 %all-to-all-start.13 = ((bf16[8,128,256]{2,1,0:T(8,128)(2,1)}), bf16[8,128,256]{2,1,0:T(8,128)(2,1)S(1)}, u32[]{:S(2)}, u32[]{:S(2)}) async-start(bf16[8,128,256]{2,1,0:T(8,128)(2,1)} %copy.163), calls=%async_computation.13 | async-start | bytes 1048576 | tf_op jit(solution)/shard_map/all_to_all | solution.py:93
  255.0 14.7 %all-to-all-done.13 = bf16[8,128,256]{2,1,0:T(8,128)(2,1)S(1)} async-done(((bf16[8,128,256]{2,1,0:T(8,128)(2,1)}), bf16[8,128,256]{2,1,0:T(8,128)(2,1)S(1)}, u32[]{:S(2)}, u32[]{:S(2)}) %all-to-all-start.13) | async-done | bytes 524320 | tf_op jit(solution)/shard_map/all_to_all | solution.py:93
  269.8 3.6 %all-to-all-start.12 = ((bf16[8,128,256]{2,1,0:T(8,128)(2,1)}), bf16[8,128,256]{2,1,0:T(8,128)(2,1)S(1)}, u32[]{:S(2)}, u32[]{:S(2)}) async-start(bf16[8,128,256]{2,1,0:T(8,128)(2,1)} %copy.161), calls=%async_computation.12 | async-start | bytes 1048576 | tf_op jit(solution)/shard_map/all_to_all | solution.py:93
  281.6 2.0 all-to-all-done.12
  284.7 2.1 fusion.83
  286.8 32.7 %all-reduce.2.cloned.1.call-done = f32[128,1024]{1,0:T(8,128)} async-done(((f32[128,1024]{1,0:T(8,128)}), f32[128,1024]{1,0:T(8,128)}) %all-reduce.2.cloned.1.call-update) | async-done | bytes 524304 | tf_op jit(solution)/shard_map/psum | solution.py:120
  319.6 1.8 fusion.54
  (202 shorter events, 93.2 us)
Async XLA Ops:
  6.5 57.8 %copy-start = (bf16[4,128,2,256]{3,2,1,0:T(2,128)(2,1)S(1)}, bf16[4,128,2,256]{3,2,1,0:T(2,128)(2,1)}, u32[]{:S(2)}) copy-start(bf16[4,128,2,256]{3,2,1,0:T(2,128)(2,1)} %param.22) | copy-start | bytes 1572868
  7.4 22.1 %copy-start.1 = (bf16[128,1024]{1,0:T(8,128)(2,1)S(1)}, bf16[128,1024]{1,0:T(8,128)(2,1)}, u32[]{:S(2)}) copy-start(bf16[128,1024]{1,0:T(8,128)(2,1)} %param.17) | copy-start | bytes 786436
  7.4 22.1 %copy-start.3 = (f32[1024]{0:T(1024)S(1)}, f32[1024]{0:T(1024)}, u32[]{:S(2)}) copy-start(f32[1024]{0:T(1024)} %param.18) | copy-start | bytes 12292
  11.7 13.7 %all-to-all-start.7 = ((s32[8,1,128]{2,1,0:T(1,128)}), s32[8,1,128]{2,1,0:T(1,128)S(1)}, u32[]{:S(2)}, u32[]{:S(2)}) async-start(s32[8,1,128]{2,1,0:T(1,128)} %bitcast.42), calls=%async_computation.7 | async-start | bytes 8192 | tf_op jit(solution)/shard_map/all_to_all | solution.py:78
  25.4 10.6 %all-to-all-start.4 = ((s32[8,1,128]{2,1,0:T(1,128)}), s32[8,1,128]{2,1,0:T(1,128)S(1)}, u32[]{:S(2)}, u32[]{:S(2)}) async-start(s32[8,1,128]{2,1,0:T(1,128)} %bitcast.31), calls=%async_computation.4 | async-start | bytes 8192 | tf_op jit(solution)/shard_map/all_to_all | solution.py:78
  36.0 9.6 %all-to-all-start.1 = ((s32[8,1,128]{2,1,0:T(1,128)}), s32[8,1,128]{2,1,0:T(1,128)S(1)}, u32[]{:S(2)}, u32[]{:S(2)}) async-start(s32[8,1,128]{2,1,0:T(1,128)} %bitcast.18), calls=%async_computation.1 | async-start | bytes 8192 | tf_op jit(solution)/shard_map/all_to_all | solution.py:78
  41.6 22.7 %copy-start.5 = (s32[1,4]{1,0:T(1,128)S(1)}, s32[1,4]{1,0:T(1,128)}, u32[]{:S(2)}) copy-start(s32[1,4]{1,0:T(1,128)} %param.24) | copy-start | bytes 52
  45.6 15.0 %all-to-all-start.6 = ((bf16[8,128,256]{1,2,0:T(8,128)(2,1)}), bf16[8,128,256]{1,2,0:T(8,128)(2,1)S(1)}, u32[]{:S(2)}, u32[]{:S(2)}) async-start(bf16[8,128,256]{1,2,0:T(8,128)(2,1)} %copy.143), calls=%async_computation.6 | async-start | bytes 1048576 | tf_op jit(solution)/shard_map/all_to_all | solution.py:77
  60.6 16.9 %all-to-all-start.3 = ((bf16[8,128,256]{1,2,0:T(8,128)(2,1)}), bf16[8,128,256]{1,2,0:T(8,128)(2,1)S(1)}, u32[]{:S(2)}, u32[]{:S(2)}) async-start(bf16[8,128,256]{1,2,0:T(8,128)(2,1)} %copy.136), calls=%async_computation.3 | async-start | bytes 1048576 | tf_op jit(solution)/shard_map/all_to_all | solution.py:77
  66.8 2.3 copy-start.2
  67.0 4.9 %copy-start.4 = (f32[2,4]{1,0:T(2,128)S(1)}, f32[2,4]{1,0:T(2,128)}, u32[]{:S(2)}) copy-start(f32[2,4]{1,0:T(2,128)} %param.21) | copy-start | bytes 100
  77.5 36.9 %all-to-all-start = ((bf16[8,128,256]{1,2,0:T(8,128)(2,1)}), bf16[8,128,256]{1,2,0:T(8,128)(2,1)S(1)}, u32[]{:S(2)}, u32[]{:S(2)}) async-start(bf16[8,128,256]{1,2,0:T(8,128)(2,1)} %copy.128), calls=%async_computation | async-start | bytes 1048576 | tf_op jit(solution)/shard_map/all_to_all | solution.py:77
  114.4 39.5 %all-to-all-start.11 = ((f32[8,128,4]{1,2,0:T(4,128)}), f32[8,128,4]{1,2,0:T(4,128)S(1)}, u32[]{:S(2)}, u32[]{:S(2)}) async-start(f32[8,128,4]{1,2,0:T(4,128)} %bitcast.58), calls=%async_computation.11 | async-start | bytes 32768 | tf_op jit(solution)/shard_map/all_to_all | solution.py:94
  153.9 38.2 %all-to-all-start.10 = ((f32[8,128,4]{1,2,0:T(4,128)}), f32[8,128,4]{1,2,0:T(4,128)S(1)}, u32[]{:S(2)}, u32[]{:S(2)}) async-start(f32[8,128,4]{1,2,0:T(4,128)} %bitcast.54), calls=%async_computation.10 | async-start | bytes 32768 | tf_op jit(solution)/shard_map/all_to_all | solution.py:94
  222.4 9.9 %all-to-all-start.2 = ((f32[8,128,4]{1,2,0:T(4,128)}), f32[8,128,4]{1,2,0:T(4,128)S(1)}, u32[]{:S(2)}, u32[]{:S(2)}) async-start(f32[8,128,4]{1,2,0:T(4,128)} %bitcast.21), calls=%async_computation.2 | async-start | bytes 32768 | tf_op jit(solution)/shard_map/all_to_all | solution.py:95
  232.3 14.0 %all-to-all-start.14 = ((bf16[8,128,256]{2,1,0:T(8,128)(2,1)}), bf16[8,128,256]{2,1,0:T(8,128)(2,1)S(1)}, u32[]{:S(2)}, u32[]{:S(2)}) async-start(bf16[8,128,256]{2,1,0:T(8,128)(2,1)} %copy.165), calls=%async_computation.14 | async-start | bytes 1048576 | tf_op jit(solution)/shard_map/all_to_all | solution.py:93
  246.3 23.4 %all-to-all-start.13 = ((bf16[8,128,256]{2,1,0:T(8,128)(2,1)}), bf16[8,128,256]{2,1,0:T(8,128)(2,1)S(1)}, u32[]{:S(2)}, u32[]{:S(2)}) async-start(bf16[8,128,256]{2,1,0:T(8,128)(2,1)} %copy.163), calls=%async_computation.13 | async-start | bytes 1048576 | tf_op jit(solution)/shard_map/all_to_all | solution.py:93
  269.8 13.9 %all-to-all-start.12 = ((bf16[8,128,256]{2,1,0:T(8,128)(2,1)}), bf16[8,128,256]{2,1,0:T(8,128)(2,1)S(1)}, u32[]{:S(2)}, u32[]{:S(2)}) async-start(bf16[8,128,256]{2,1,0:T(8,128)(2,1)} %copy.161), calls=%async_computation.12 | async-start | bytes 1048576 | tf_op jit(solution)/shard_map/all_to_all | solution.py:93
  273.3 46.2 %all-reduce.2.cloned.1.call-start = ((), (), s32[]{:S(2)}) async-start(), calls=%async_computation.15 | async-start | bytes 1048576 | tf_op jit(solution)/shard_map/psum | solution.py:120
Sparse Core Ops, SparseCore 0:
  286.9 32.5 all-reduce.1
where the time goes:
time: 331 us; the launch traced here: 328 us
  waiting for transfers between devices  88.2 us (27%)
  local copies, waits for them, and re-layouts  69.7 us (21%)
  starting transfers between devices  55.4 us (17%)
  matrix products  52.5 us (16%)
  blocking collectives  30.2 us (9%)
  other arithmetic  17.8 us (5%)
  between operations  13.9 us (4%)
    dot_general x12, matrix products, head_attend(): jnp.dot(qh, kh.T, preferred_element_type=jnp.float32) * HD ** (-0.5)  33.3 us
    psum x1, waiting for transfers between devices, body(): total_sum = lax.psum(partial_sum, 'tp')  32.7 us
    all_to_all x3, waiting for transfers between devices, body(): lax.all_to_all(mixed, 'seq', split_axis=0, concat_axis=0, tiled=True)  26 us
    all_to_all x2, blocking collectives, body(): lax.all_to_all(total, 'seq', split_axis=0, concat_axis=0, tiled=True)  17.9 us
    dynamic_update_slice x36, local copies, waits for them, and re-layouts, body(): lax.map(per_head, (heads_q, node_keys, node_values, head_bias[1], head_bi...  17.1 us
    dot_general x12, matrix products, head_attend(): jnp.dot(weights.astype(jnp.bfloat16), vh, preferred_element_type=jnp.floa...  16.4 us
    dynamic_slice x24, local copies, waits for them, and re-layouts, body(): lax.map(per_head, (heads_q, node_keys, node_values, head_bias[1], head_bi...  15 us
    all_to_all x3, starting transfers between devices, body(): lax.all_to_all(vbuf, 'seq', split_axis=0, concat_axis=0, tiled=True)  14.7 us
  transfers between devices with their start and end apart: 13, of which 10 were waited for; matrix products, arithmetic and copies ran while one was open for 40% of the time, Pallas kernels for 0%

commit v1 on v0

--- a/solution.py
+++ b/solution.py
@@ -1,6 +1,8 @@
 import jax
 import jax.numpy as jnp
 from jax import lax
+from jax.experimental import pallas as pl
+from jax.experimental.pallas import tpu as pltpu
 from jax.sharding import PartitionSpec as P
 
 HD = 64
@@ -37,7 +39,7 @@
     return (qbuf, vbuf, flat)
 
 
-def body(
+def routed_body(
     tokens,
     norm_gain,
     w_qkv,
@@ -121,6 +123,254 @@
     return (xf + total_sum).astype(jnp.bfloat16)
 
 
+BF16, F32, I32 = jnp.bfloat16, jnp.float32, jnp.int32
+AUX = 16
+FAR = -1e30
+VMEM = pl.BlockSpec(memory_space=pltpu.VMEM)
+
+
+def call(kernel, outs, *args, flops=1 << 20, scratch=()):
+    single = not isinstance(outs, (tuple, list))
+    moved = sum(a.size * a.dtype.itemsize for a in args)
+    return pl.pallas_call(
+        kernel,
+        out_shape=outs,
+        in_specs=[VMEM] * len(args),
+        out_specs=VMEM if single else [VMEM] * len(outs),
+        scratch_shapes=list(scratch),
+        compiler_params=pltpu.CompilerParams(vmem_limit_bytes=32 << 20),
+        cost_estimate=pl.CostEstimate(flops=flops, bytes_accessed=moved, transcendentals=0),
+    )(*args)
+
+
+def shape(*dims, dtype=BF16):
+    return jax.ShapeDtypeStruct(dims, dtype)
+
+
+def normalise(tok_ref, gain_ref):
+    x = tok_ref[...].astype(F32)
+    r = lax.rsqrt(jnp.mean(x * x, axis=1, keepdims=True) + 1e-05)
+    return (x * r * gain_ref[...]).astype(BF16)
+
+
+def query_kernel(tok_ref, gain_ref, w_ref, aux_ref, msg_ref, normed_ref):
+    normed = normalise(tok_ref, gain_ref)
+    normed_ref[...] = normed
+    q = jnp.dot(normed, w_ref[...], preferred_element_type=F32).astype(BF16)
+    cols = q.shape[1]
+    msg_ref[:cols, :] = (q.astype(F32) * HD ** (-0.5)).T.astype(BF16)
+    msg_ref[cols:, :] = aux_ref[...]
+
+
+def own_kernel(normed_ref, wk_ref, wv_ref, k_ref, v_ref):
+    normed = normed_ref[...]
+    for w_ref, out_ref in ((wk_ref, k_ref), (wv_ref, v_ref)):
+        out_ref[...] = jnp.dot(normed, w_ref[...], preferred_element_type=F32).astype(BF16).astype(F32).T.astype(BF16)
+
+
+def split3(x):
+    a = x.astype(BF16)
+    r = x - a.astype(F32)
+    b = r.astype(BF16)
+    c = (r - b.astype(F32)).astype(BF16)
+    return a, b, c
+
+
+def slot_terms(code_ref):
+    pages, page = code_ref.shape
+    blocks = []
+    lane = lax.broadcasted_iota(I32, (page, 128), 1)
+    for p in range(pages):
+        row = code_ref[p : p + 1, :]
+        sub = lax.broadcasted_iota(I32, (128, page), 0)
+        code = jnp.broadcast_to(row, (128, page))
+        hit = (code == sub % 8) & (sub < 24)
+        term = jnp.where(hit | ((sub >= 24) & (sub < 27)), 1.0, 0.0)
+        term = jnp.where((sub == 27) & (code == 8), FAR, term)
+        blocks.append(term.T.astype(BF16))
+    return jnp.concatenate(blocks, axis=0)
+
+
+def row_terms(bias_ref, head, variate):
+    same, other = bias_ref[1, head], bias_ref[0, head]
+    rows = variate.shape[1]
+    sub = lax.broadcasted_iota(I32, (128, rows), 0)
+    hit = (variate == sub % 8) & (sub < 24)
+    one = jnp.zeros((128, rows), F32)
+    d = split3(jnp.full((8, rows), same - other, F32))
+    o = split3(jnp.full((8, rows), other, F32))
+    picked = jnp.concatenate([d[0].astype(F32), d[1].astype(F32), d[2].astype(F32)], axis=0)
+    eight = sub[:8, :]
+    tail = jnp.where(eight == 0, o[0].astype(F32), jnp.where(eight == 1, o[1].astype(F32), jnp.where(eight == 2, o[2].astype(F32), jnp.where(eight == 3, 1.0, 0.0))))
+    top = jnp.where(hit[:24], picked, 0.0)
+    return jnp.concatenate([top.astype(BF16), tail.astype(BF16), jnp.zeros((96, rows), BF16)], axis=0)
+
+
+def attend(q, k_ref, vt_ref, terms, bias_ref, head, variate):
+    pair = head // 2
+    rows = q.shape[1]
+    zero = jnp.zeros((HD, rows), BF16)
+    q_head = q[head * HD : (head + 1) * HD, :]
+    both = [q_head, zero] if head % 2 == 0 else [zero, q_head]
+    q_cat = jnp.concatenate(both + [row_terms(bias_ref, head, variate)], axis=0)
+    k_cat = jnp.concatenate([k_ref[:, pair * 128 : (pair + 1) * 128], terms], axis=1)
+    scores = jnp.dot(k_cat, q_cat, preferred_element_type=F32)
+    peak = jnp.max(scores, axis=0, keepdims=True)
+    weights = jnp.exp(scores - peak)
+    total = jnp.sum(weights, axis=0, keepdims=True)
+    mixed = jnp.dot(vt_ref[head * HD : (head + 1) * HD, :], weights.astype(BF16), preferred_element_type=F32)
+    return (mixed / total).astype(BF16), peak + jnp.log(total)
+
+
+def first_kernel(code_ref, bias_ref, k_ref, vt_ref, *refs):
+    msgs, (o_ref, lse_ref) = refs[:-2], refs[-2:]
+    heads = k_ref.shape[1] // HD
+    cols = heads * HD
+    terms = slot_terms(code_ref)
+    for b, msg in enumerate(msgs):
+        variate = msg[cols : cols + AUX, :].astype(F32)[0:1, :].astype(I32)
+        q = msg[:cols, :]
+        for head in range(heads):
+            o, lse = attend(q, k_ref, vt_ref, terms, bias_ref, head, variate)
+            o_ref[b, head * HD : (head + 1) * HD, :] = o
+            lse_ref[b, head : head + 1, :] = lse
+
+
+def second_kernel(ids_ref, code_ref, bias_ref, k_ref, vt_ref, o_ref, lse_ref, *refs):
+    count = len(refs) // 2
+    msgs, outs = refs[:count], refs[count:]
+    heads = k_ref.shape[1] // HD
+    cols = heads * HD
+    terms = slot_terms(code_ref)
+    for b, (msg, out) in enumerate(zip(msgs, outs)):
+        aux = msg[cols : cols + AUX, :].astype(F32).astype(I32)
+        variate = aux[0:1, :]
+        paths = aux[1:4, :]
+        mine = jnp.max((paths == ids_ref[0]).astype(I32), axis=0, keepdims=True) > 0
+        theirs = jnp.max((paths == ids_ref[1]).astype(I32), axis=0, keepdims=True) > 0
+        q = msg[:cols, :]
+        merged = []
+        for head in range(heads):
+            o2, lse2 = attend(q, k_ref, vt_ref, terms, bias_ref, head, variate)
+            lse2 = jnp.where(theirs, lse2, FAR)
+            lse1 = jnp.where(mine, lse_ref[b, head : head + 1, :], FAR)
+            top = jnp.maximum(lse1, lse2)
+            w1, w2 = jnp.exp(lse1 - top), jnp.exp(lse2 - top)
+            o1 = o_ref[b, head * HD : (head + 1) * HD, :].astype(F32)
+            out[head * HD : (head + 1) * HD, :] = ((w1 * o1 + w2 * o2.astype(F32)) / (w1 + w2)).astype(BF16)
+            merged.append(top + jnp.log(w1 + w2))
+        pieces = [piece.astype(F32) for lse in merged for piece in split3(lse)]
+        pieces.append(jnp.zeros((AUX - 3 * heads, variate.shape[1]), F32))
+        out[cols:, :] = jnp.concatenate(pieces, axis=0).astype(BF16)
+
+
+def combine_kernel(bias_ref, q_ref, k_ref, v_ref, *refs):
+    parts, attn_ref = refs[:-1], refs[-1]
+    cols = k_ref.shape[0]
+    heads = cols // HD
+    auxes = [part[cols:, :].astype(F32) for part in parts]
+    done = []
+    for head in range(heads):
+        at = slice(head * HD, (head + 1) * HD)
+        q, k = q_ref[at, :].astype(F32), k_ref[at, :].astype(F32)
+        own = jnp.sum(q * k, axis=0, keepdims=True) + bias_ref[1, head]
+        lses = [sum(aux[3 * head + i : 3 * head + i + 1, :] for i in range(3)) for aux in auxes]
+        top = own
+        for lse in lses:
+            top = jnp.maximum(top, lse)
+        weight = jnp.exp(own - top)
+        whole = weight
+        acc = weight * v_ref[at, :].astype(F32)
+        for lse, part in zip(lses, parts):
+            weight = jnp.exp(lse - top)
+            whole = whole + weight
+            acc = acc + weight * part[at, :].astype(F32)
+        done.append(acc / whole)
+    attn_ref[...] = jnp.concatenate(done, axis=0).T.astype(BF16)
+
+
+def project_kernel(tok_ref, *refs):
+    out_ref = refs[-1]
+    half = (len(refs) - 1) // 2
+    total = tok_ref[...].astype(F32)
+    acc = None
+    for attn, w in zip(refs[:half], refs[half : 2 * half]):
+        term = jnp.dot(attn[...], w[...], preferred_element_type=F32)
+        acc = term if acc is None else acc + term
+    out_ref[...] = (total + acc).astype(BF16)
+
+
+def xor(axis, k):
+    return [(i, i ^ k) for i in range(lax.axis_size(axis))]
+
+
+def dense_body(
+    tokens,
+    norm_gain,
+    w_qkv,
+    w_out,
+    head_bias,
+    kv_pool,
+    key_variate,
+    page_table,
+    node_len,
+    path_nodes,
+    query_variate,
+):
+    rows, width = tokens.shape
+    cols = w_qkv.shape[2]
+    heads = cols // HD
+    pages, page = key_variate.shape
+    slots = pages * page
+    owners, parts = lax.axis_size("seq"), lax.axis_size("tp")
+    groups = [2 * k for k in range(owners // 2)]
+
+    place = jnp.sum(jnp.where(page_table[0][:, None] == jnp.arange(pages)[None, :], jnp.arange(pages)[:, None], 0), axis=0)
+    valid = place[:, None] * page + jnp.arange(page)[None, :] < node_len[0]
+    code = jnp.where(valid, key_variate, 8).astype(I32)
+    pool = kv_pool.reshape(slots, 2, cols)
+    keys = pool[:, 0]
+    values_t = pool[:, 1].T
+    keys2 = lax.ppermute(keys, "seq", xor("seq", 1))
+    values2 = lax.ppermute(values_t, "seq", xor("seq", 1))
+    code2 = lax.ppermute(code, "seq", xor("seq", 1))
+
+    aux = jnp.concatenate([query_variate[None], path_nodes.T, jnp.zeros((AUX - 4, rows), I32)], axis=0).astype(BF16)
+    msg, normed = call(
+        query_kernel,
+        [shape(cols + AUX, rows), shape(rows, width)],
+        tokens, norm_gain[None], w_qkv[:, 0], aux,
+        flops=2 * rows * width * cols,
+    )
+    msgs = [msg] + [lax.ppermute(msg, "seq", xor("seq", k)) for k in groups[1:]]
+
+    outs = [w_out]
+    outs.append(lax.ppermute(w_out, "tp", xor("tp", 2)))
+    outs += [lax.ppermute(w, "tp", xor("tp", 1)) for w in outs[:2]]
+
+    key, value = call(own_kernel, [shape(cols, rows)] * 2, normed, w_qkv[:, 1], w_qkv[:, 2], flops=4 * rows * width * cols)
+
+    work = 4 * len(groups) * rows * slots * cols
+    o1, lse1 = call(
+        first_kernel,
+        [shape(len(groups), cols, rows), shape(len(groups), heads, rows, dtype=F32)],
+        code, head_bias, keys, values_t, *msgs,
+        flops=work,
+    )
+    me = lax.axis_index("seq")
+    ids = jnp.stack([me, me ^ 1]).astype(I32)
+    merged = call(
+        second_kernel,
+        [shape(cols + AUX, rows)] * len(groups),
+        ids, code2, head_bias, keys2, values2, o1, lse1, *msgs,
+        flops=work,
+    )
+    back = [merged[0]] + [lax.ppermute(m, "seq", xor("seq", k)) for m, k in zip(merged[1:], groups[1:])]
+    attn = call(combine_kernel, shape(rows, cols), head_bias, msg, key, value, *back)
+    attns = [attn] + [lax.ppermute(attn, "tp", xor("tp", k)) for k in (2, 1, 3)]
+    return call(project_kernel, shape(rows, width), tokens, *attns, *outs, flops=2 * rows * width * width)
+
+
 def solution(mesh):
     in_specs = (
         P("seq", None),
@@ -136,4 +386,6 @@
         P("seq"),
     )
     out_specs = P("seq", None)
+    dense = mesh.shape["seq"] == 8 and mesh.shape["tp"] == 4
+    body = dense_body if dense else routed_body
     return jax.shard_map(body, mesh=mesh, in_specs=in_specs, out_specs=out_specs, check_vma=False)

time: 331 us -> 62.8 us (0.19)
  waiting for transfers between devices: 88.2 us -> 11 us
  local copies, waits for them, and re-layouts: 69.7 us -> 13.8 us
  matrix products: 52.5 us -> 0 us
  starting transfers between devices: 55.4 us -> 21.4 us
  blocking collectives: 30.2 us -> 0 us
  other arithmetic: 17.8 us -> 1.48 us
  Pallas kernels: 0 us -> 13.8 us
  between operations: 13.9 us -> 0.84 us
    all_to_all x12 -> x0, waiting for transfers between devices: 55.5 us -> none  [the longest x3 26 us: body(): lax.all_to_all(mixed, 'seq', split_axis=0, concat_axis=0, tiled=True)]
    all_to_all x12 -> x0, starting transfers between devices: 55.4 us -> none  [the longest x3 14.7 us: body(): lax.all_to_all(vbuf, 'seq', split_axis=0, concat_axis=0, tiled=True)]
    dot_general x26 -> x0, matrix products: 52.5 us -> none  [the longest x12 33.3 us: head_attend(): jnp.dot(qh, kh.T, preferred_element_type=jnp.float32) * HD ** (-0.5)]
    psum x1 -> x0, waiting for transfers between devices: 32.7 us -> none  [body(): total_sum = lax.psum(partial_sum, 'tp')]
    all_to_all x3 -> x0, blocking collectives: 30.2 us -> none  [the longest x2 17.9 us: body(): lax.all_to_all(total, 'seq', split_axis=0, concat_axis=0, tiled=True)]
    ppermute x0 -> x15, starting transfers between devices: none -> 21.4 us  [the longest x3 7.9 us: dense_body(): msgs = [msg] + [lax.ppermute(msg, 'seq', xor('seq', k)) for k in groups[1:]]]
    dynamic_update_slice x36 -> x0, local copies, waits for them, and re-layouts: 17.1 us -> none  [body(): lax.map(per_head, (heads_q, node_keys, node_values, head_bias[1], head_bi...]
    dynamic_slice x24 -> x0, local copies, waits for them, and re-layouts: 15 us -> none  [body(): lax.map(per_head, (heads_q, node_keys, node_values, head_bias[1], head_bi...]
  transfers between devices with their start and end apart: 13 -> 15, of which waited for: 10 -> 7; matrix products, arithmetic and copies ran while one was open for 40% -> 17% of each run, Pallas kernels for 0% -> 19%
where the time goes in v1:
time: 62.8 us; the launch traced here: 62.3 us
  starting transfers between devices  21.4 us (34%)
  local copies, waits for them, and re-layouts  13.8 us (22%)
  Pallas kernels  13.8 us (22%)
  waiting for transfers between devices  11 us (18%)
  other arithmetic  1.48 us (2%)
  between operations  0.84 us (1%)
    pallas_call x6, Pallas kernels, call(): pl.pallas_call(kernel, out_shape=outs, in_specs=[VMEM] * len(args), out_s...  13.8 us
    unnamed x32, local copies, waits for them, and re-layouts  8.36 us
    ppermute x3, starting transfers between devices, dense_body(): msgs = [msg] + [lax.ppermute(msg, 'seq', xor('seq', k)) for k in groups[1:]]  7.9 us
    ppermute x3, waiting for transfers between devices, dense_body(): lax.ppermute(m, 'seq', xor('seq', k))  5.32 us
    ppermute x3, starting transfers between devices, dense_body(): lax.ppermute(m, 'seq', xor('seq', k))  4.45 us
    ppermute x3, waiting for transfers between devices, dense_body(): attns = [attn] + [lax.ppermute(attn, 'tp', xor('tp', k)) for k in (2, 1, 3)]  3.1 us
    ppermute x1, starting transfers between devices, dense_body(): outs.append(lax.ppermute(w_out, 'tp', xor('tp', 2)))  3.02 us
    ppermute x3, starting transfers between devices, dense_body(): attns = [attn] + [lax.ppermute(attn, 'tp', xor('tp', k)) for k in (2, 1, 3)]  2.21 us
  transfers between devices with their start and end apart: 15, of which 7 were waited for; matrix products, arithmetic and copies ran while one was open for 17% of the time, Pallas kernels for 19%

profile of v1, /device:TPU:0, one launch (start us, length us, event | category | flops | bytes accessed | tf_op | source)
XLA Modules:
  0.0 62.3 jit_solution(4968192788568603651)
XLA Ops:
  0.0 3.0 %collective-permute-start.12 = (bf16[256,1024]{1,0:T(8,128)(2,1)}, bf16[256,1024]{1,0:T(8,128)(2,1)S(1)}, u32[]{:S(2)}, u32[]{:S(2)}) collective-permute-start(bf16[256,1024]{1,0:T(8,128)(2,1)} %refs_4_.1), channel_id=1, source_target_pairs={{0,2},{1,3},{2,0},{3,1},{4,6},{5,7},{6,4},{7,5},{8,10},{9,11},{10,... | collective-permute-start | bytes 1572872 | tf_op jit(solution)/shard_map/ppermute | solution.py:348
  3.0 1.5 %slice_bitcast_fusion = (bf16[1024,256]{1,0:T(8,128)(2,1)S(1)}, bf16[1024,256]{1,0:T(8,128)(2,1)S(1)}, bf16[1024,256]{1,0:T(8,128)(2,1)S(1)}) fusion(bf16[1024,3,256]{2,0,1:T(8,128)(2,1)} %param.13), kind=kLoop, calls=%fused_computation | loop fusion | bytes 3145728 | tf_op jit(solution)/shard_map/squeeze | solution.py:351
  4.6 0.1 pad.4.clone
  4.6 0.1 maximum_maximum_fusion.aux_ref
  4.7 0.4 shard_map.109
  5.1 0.0 copy-start.14
  5.1 1.6 %collective-permute-start.3 = (bf16[272,128]{1,0:T(8,128)(2,1)S(1)}, bf16[272,128]{1,0:T(8,128)(2,1)S(1)}, u32[]{:S(2)}, u32[]{:S(2)}) collective-permute-start(bf16[272,128]{1,0:T(8,128)(2,1)S(1)} %get-tuple-element.15.refs_0_.q_ref), channel_id=1, source_target_pairs={{0,8},{4,12},{8,0},{12,4},{16,24},{20,28},{24,16},{28,20},{1,9},{5... | collective-permute-start | bytes 208904 | tf_op jit(solution)/shard_map/ppermute | solution.py:345
  6.8 2.6 %collective-permute-start.4 = (bf16[272,128]{1,0:T(8,128)(2,1)S(1)}, bf16[272,128]{1,0:T(8,128)(2,1)}, u32[]{:S(2)}, u32[]{:S(2)}) collective-permute-start(bf16[272,128]{1,0:T(8,128)(2,1)S(1)} %get-tuple-element.15.refs_0_.q_ref), channel_id=1, source_target_pairs={{0,16},{4,20},{8,24},{12,28},{16,0},{20,4},{24,8},{28,12},{1,17},{... | collective-permute-start | bytes 208904 | tf_op jit(solution)/shard_map/ppermute | solution.py:345
  9.4 0.0 copy-start.12
  9.4 1.8 %fusion.1 = (bf16[512,1,256]{2,1,0:T(2,128)(2,1)}, bf16[512,1,256]{2,1,0:T(2,128)(2,1)}) fusion(bf16[512,2,256]{2,1,0:T(2,128)(2,1)S(1)} %bitcast.26), kind=kLoop, calls=%fused_computation.13 | loop fusion | bytes 1048576 | tf_op jit(solution)/shard_map/slice | solution.py:333
  11.1 1.9 %copy.19 = bf16[512,1,256]{0,2,1:T(8,128)(2,1)} copy(bf16[512,1,256]{2,1,0:T(2,128)(2,1)} %get-tuple-element.29) | data formatting | bytes 524288
  13.0 1.5 %collective-permute-start.1 = (bf16[512,256]{0,1:T(8,128)(2,1)}, bf16[512,256]{0,1:T(8,128)(2,1)}, u32[]{:S(2)}, u32[]{:S(2)}) collective-permute-start(bf16[512,256]{0,1:T(8,128)(2,1)} %bitcast.11), channel_id=1, source_target_pairs={{0,4},{4,0},{8,12},{12,8},{16,20},{20,16},{24,28},{28,24},{1,5},{5... | collective-permute-start | bytes 786440 | tf_op jit(solution)/shard_map/ppermute | solution.py:334
  14.5 0.1 select_reduce_fusion
  14.6 0.6 collective-permute-done.12.refs_5_
  15.2 0.0 collective-permute-start.14
  15.8 1.9 %copy.20 = bf16[512,1,256]{0,2,1:T(8,128)(2,1)} copy(bf16[512,1,256]{2,1,0:T(2,128)(2,1)} %get-tuple-element.28) | data formatting | bytes 524288
  17.7 1.8 %collective-permute-start.2 = (bf16[256,512]{1,0:T(8,128)(2,1)}, bf16[256,512]{1,0:T(8,128)(2,1)}, u32[]{:S(2)}, u32[]{:S(2)}) collective-permute-start(bf16[256,512]{1,0:T(8,128)(2,1)} %bitcast.13.vt_ref), channel_id=1, source_target_pairs={{0,4},{4,0},{8,12},{12,8},{16,20},{20,16},{24,28},{28,24},{1,5},{5... | collective-permute-start | bytes 786440 | tf_op jit(solution)/shard_map/ppermute | solution.py:335
  19.5 0.7 %fusion.code_ref = s32[4,128]{1,0:T(4,128)} fusion(s32[4,128]{1,0:T(4,128)S(1)} %copy-done.12, s32[]{:T(128)} %bitcast.23, s32[4]{0:T(128)S(1)} %broadcast_multiply_fusion), kind=kLoop, calls=%fused_computation.8 | loop fusion | flops 1536 | bytes 4116 | tf_op jit(solution)/shard_map/jit(_where)/select_n | solution.py:330
  20.2 1.1 %copy.23 = bf16[512,1,256]{2,0,1:T(8,128)(2,1)S(1)} copy(bf16[512,1,256]{2,1,0:T(2,128)(2,1)} %get-tuple-element.29) | data formatting | bytes 524288 | tf_op jit(solution)/shard_map/squeeze | solution.py:332
  21.3 3.7 %collective-permute-start.5 = (bf16[272,128]{1,0:T(8,128)(2,1)S(1)}, bf16[272,128]{1,0:T(8,128)(2,1)S(1)}, u32[]{:S(2)}, u32[]{:S(2)}) collective-permute-start(bf16[272,128]{1,0:T(8,128)(2,1)S(1)} %get-tuple-element.15.refs_0_.q_ref), channel_id=1, source_target_pairs={{0,24},{4,28},{8,16},{12,20},{16,8},{20,12},{24,0},{28,4},{1,25},{... | collective-permute-start | bytes 208904 | tf_op jit(solution)/shard_map/ppermute | solution.py:345
  24.9 0.6 %pad_add_fusion.ids_ref = s32[2]{0:T(128)} fusion(s32[1]{0:T(128)} %bitcast.7, s32[1]{0:T(128)} %bitcast.6), kind=kLoop, calls=%fused_computation.10 | loop fusion | flops 2 | bytes 16 | tf_op jit(solution)/shard_map/stack | solution.py:361
  25.6 2.0 %collective-permute-done.5.refs_3_ = bf16[272,128]{1,0:T(8,128)(2,1)S(1)} collective-permute-done((bf16[272,128]{1,0:T(8,128)(2,1)S(1)}, bf16[272,128]{1,0:T(8,128)(2,1)S(1)}, u32[]{:S(2)}, u32[]{:S(2)}) %collective-permute-start.5) | collective-permute-done | bytes 69664 | tf_op jit(solution)/shard_map/ppermute | solution.py:345
  27.6 0.5 collective-permute-start
  28.1 0.7 %copy-done.7 = f32[2,4]{1,0:T(2,128)S(1)} copy-done((f32[2,4]{1,0:T(2,128)S(1)}, f32[2,4]{1,0:T(2,128)}, u32[]{:S(2)}) %copy-start.7) | copy-done | bytes 56
  28.8 5.2 %shard_map.111 = (bf16[4,256,128]{2,1,0:T(8,128)(2,1)S(1)}, f32[4,4,128]{2,1,0:T(4,128)S(1)}) custom-call(s32[4,128]{1,0:T(4,128)} %fusion.code_ref, f32[2,4]{1,0:T(2,128)S(1)} %copy-done.7, bf16[512,256]{1,0:T(8,128)(2,1)S(1)} %bitcast.24, bf16[256,512]{1,0:T(8,128)(2,1)} %bitcast.13.vt_ref, bf16[272,128]{1,0:T(8,128)(2,1)S(1)} %get-tuple-element.15.refs_0_.q_ref, ...), custom_call_target="tpu_custom_call" | custom-call | flops 268435456 | bytes 804896 | tf_op jit(solution)/shard_map/pallas_call | solution.py:135
  34.1 0.7 %copy-done.2 = bf16[4,256,128]{2,1,0:T(8,128)(2,1)} copy-done((bf16[4,256,128]{2,1,0:T(8,128)(2,1)}, bf16[4,256,128]{2,1,0:T(8,128)(2,1)S(1)}, u32[]{:S(2)}) %copy-start.2) | copy-done | bytes 262168
  34.8 0.0 collective-permute-done.1
  34.8 1.1 %copy.17.k_ref = bf16[512,256]{1,0:T(8,128)(2,1)S(1)} copy(bf16[512,256]{0,1:T(8,128)(2,1)} %collective-permute-done.1) | data formatting | bytes 524288 | tf_op jit(solution)/shard_map/ppermute | solution.py:334
  35.9 0.0 collective-permute-done.code_ref
  35.9 0.0 collective-permute-done.2.vt_ref
  35.9 0.9 %copy-done.3 = bf16[4,256,128]{2,1,0:T(8,128)(2,1)S(1)} copy-done((bf16[4,256,128]{2,1,0:T(8,128)(2,1)S(1)}, bf16[4,256,128]{2,1,0:T(8,128)(2,1)}, u32[]{:S(2)}) %copy-start.3) | copy-done | bytes 262168
  36.8 0.9 %copy-done.5 = bf16[272,128]{1,0:T(8,128)(2,1)S(1)} copy-done((bf16[272,128]{1,0:T(8,128)(2,1)S(1)}, bf16[272,128]{1,0:T(8,128)(2,1)}, u32[]{:S(2)}) %copy-start.5) | copy-done | bytes 69656
  37.7 0.7 %copy-done.8 = f32[2,4]{1,0:T(2,128)S(1)} copy-done((f32[2,4]{1,0:T(2,128)S(1)}, f32[2,4]{1,0:T(2,128)}, u32[]{:S(2)}) %copy-start.8) | copy-done | bytes 56
  38.4 0.7 %copy-done.9 = s32[2]{0:T(128)S(1)} copy-done((s32[2]{0:T(128)S(1)}, s32[2]{0:T(128)}, u32[]{:S(2)}) %copy-start.9) | copy-done | bytes 32
  39.1 5.3 %shard_map.112 = (bf16[272,128]{1,0:T(8,128)(2,1)S(1)}, bf16[272,128]{1,0:T(8,128)(2,1)S(1)}, bf16[272,128]{1,0:T(8,128)(2,1)S(1)}, bf16[272,128]{1,0:T(8,128)(2,1)S(1)}) custom-call(s32[2]{0:T(128)S(1)} %copy-done.9, s32[4,128]{1,0:T(4,128)} %collective-permute-done.code_ref, f32[2,4]{1,0:T(2,128)S(1)} %copy-done.8, bf16[512,256]{1,0:T(8,128)(2,1)S(1)} %copy.17.k_ref, ...), custom_call_target="tpu_custom_call" | custom-call | flops 268435456 | bytes 1075240 | tf_op jit(solution)/shard_map/pallas_call | solution.py:135
  44.4 1.2 %collective-permute-start.6 = (bf16[272,128]{1,0:T(8,128)(2,1)S(1)}, bf16[272,128]{1,0:T(8,128)(2,1)S(1)}, u32[]{:S(2)}, u32[]{:S(2)}) collective-permute-start(bf16[272,128]{1,0:T(8,128)(2,1)S(1)} %get-tuple-element.22), channel_id=1, source_target_pairs={{0,8},{4,12},{8,0},{12,4},{16,24},{20,28},{24,16},{28,20},{1,9},{5... | collective-permute-start | bytes 208904 | tf_op jit(solution)/shard_map/ppermute | solution.py:368
  45.5 2.9 %collective-permute-start.7 = (bf16[272,128]{1,0:T(8,128)(2,1)S(1)}, bf16[272,128]{1,0:T(8,128)(2,1)S(1)}, u32[]{:S(2)}, u32[]{:S(2)}) collective-permute-start(bf16[272,128]{1,0:T(8,128)(2,1)S(1)} %get-tuple-element.23), channel_id=1, source_target_pairs={{0,16},{4,20},{8,24},{12,28},{16,0},{20,4},{24,8},{28,12},{1,17},{... | collective-permute-start | bytes 208904 | tf_op jit(solution)/shard_map/ppermute | solution.py:368
  48.4 0.4 collective-permute-start.8
  48.8 0.4 shard_map.110
  49.2 0.1 collective-permute-done.6.refs_1_
  49.3 3.0 %collective-permute-done.7.refs_2_ = bf16[272,128]{1,0:T(8,128)(2,1)S(1)} collective-permute-done((bf16[272,128]{1,0:T(8,128)(2,1)S(1)}, bf16[272,128]{1,0:T(8,128)(2,1)S(1)}, u32[]{:S(2)}, u32[]{:S(2)}) %collective-permute-start.7) | collective-permute-done | bytes 69664 | tf_op jit(solution)/shard_map/ppermute | solution.py:368
  52.3 2.3 %collective-permute-done.8.refs_3_ = bf16[272,128]{1,0:T(8,128)(2,1)S(1)} collective-permute-done((bf16[272,128]{1,0:T(8,128)(2,1)S(1)}, bf16[272,128]{1,0:T(8,128)(2,1)S(1)}, u32[]{:S(2)}, u32[]{:S(2)}) %collective-permute-start.8) | collective-permute-done | bytes 69664 | tf_op jit(solution)/shard_map/ppermute | solution.py:368
  54.6 0.2 shard_map.113.refs_0_
  54.8 1.6 %collective-permute-start.9 = (bf16[128,256]{1,0:T(8,128)(2,1)S(1)}, bf16[128,256]{1,0:T(8,128)(2,1)S(1)}, u32[]{:S(2)}, u32[]{:S(2)}) collective-permute-start(bf16[128,256]{1,0:T(8,128)(2,1)S(1)} %shard_map.113.refs_0_), channel_id=1, source_target_pairs={{0,2},{1,3},{2,0},{3,1},{4,6},{5,7},{6,4},{7,5},{8,10},{9,11},{10,... | collective-permute-start | bytes 196616 | tf_op jit(solution)/shard_map/ppermute | solution.py:370
  56.4 0.6 %collective-permute-start.11 = (bf16[128,256]{1,0:T(8,128)(2,1)S(1)}, bf16[128,256]{1,0:T(8,128)(2,1)S(1)}, u32[]{:S(2)}, u32[]{:S(2)}) collective-permute-start(bf16[128,256]{1,0:T(8,128)(2,1)S(1)} %shard_map.113.refs_0_), channel_id=1, source_target_pairs={{0,3},{1,2},{2,1},{3,0},{4,7},{5,6},{6,5},{7,4},{8,11},{9,10},{10,... | collective-permute-start | bytes 196616 | tf_op jit(solution)/shard_map/ppermute | solution.py:370
  57.0 2.1 %collective-permute-done.9.refs_1_ = bf16[128,256]{1,0:T(8,128)(2,1)S(1)} collective-permute-done((bf16[128,256]{1,0:T(8,128)(2,1)S(1)}, bf16[128,256]{1,0:T(8,128)(2,1)S(1)}, u32[]{:S(2)}, u32[]{:S(2)}) %collective-permute-start.9) | collective-permute-done | bytes 65568 | tf_op jit(solution)/shard_map/ppermute | solution.py:370
  59.1 1.0 %collective-permute-done.11.refs_3_ = bf16[128,256]{1,0:T(8,128)(2,1)S(1)} collective-permute-done((bf16[128,256]{1,0:T(8,128)(2,1)S(1)}, bf16[128,256]{1,0:T(8,128)(2,1)S(1)}, u32[]{:S(2)}, u32[]{:S(2)}) %collective-permute-start.11) | collective-permute-done | bytes 65568 | tf_op jit(solution)/shard_map/ppermute | solution.py:370
  60.1 2.2 %shard_map.114 = bf16[128,1024]{1,0:T(8,128)(2,1)} custom-call(bf16[128,1024]{1,0:T(8,128)(2,1)S(1)} %copy-done, bf16[128,256]{1,0:T(8,128)(2,1)S(1)} %shard_map.113.refs_0_, bf16[128,256]{1,0:T(8,128)(2,1)S(1)} %collective-permute-done.9.refs_1_, bf16[128,256]{1,0:T(8,128)(2,1)S(1)} %collective-permute-done.10.refs_2_, ...), custom_call_target="tpu_custom_call" | custom-call | flops 268435456 | bytes 2621440 | tf_op jit(solution)/shard_map/pallas_call | solution.py:135
  (33 shorter events, 0.1 us)
Async XLA Ops:
  0.0 9.4 %copy-start.1 = (bf16[256,1024]{1,0:T(8,128)(2,1)S(1)}, bf16[256,1024]{1,0:T(8,128)(2,1)}, u32[]{:S(2)}) copy-start(bf16[256,1024]{1,0:T(8,128)(2,1)} %refs_4_.1) | copy-start | bytes 1572868
  0.0 4.5 %copy-start.11 = (s32[128,3]{0,1:T(4,128)S(1)}, s32[128,3]{0,1:T(4,128)}, u32[]{:S(2)}) copy-start(s32[128,3]{0,1:T(4,128)} %param.20) | copy-start | bytes 4612
  0.0 4.5 %copy-start.13 = (s32[128]{0:T(128)S(1)}, s32[128]{0:T(128)}, u32[]{:S(2)}) copy-start(s32[128]{0:T(128)} %param.21) | copy-start | bytes 1540
  0.0 4.7 %copy-start = (bf16[128,1024]{1,0:T(8,128)(2,1)S(1)}, bf16[128,1024]{1,0:T(8,128)(2,1)}, u32[]{:S(2)}) copy-start(bf16[128,1024]{1,0:T(8,128)(2,1)} %tok_ref.3) | copy-start | bytes 786436
  0.0 4.7 %copy-start.6 = (f32[1024]{0:T(1024)S(1)}, f32[1024]{0:T(1024)}, u32[]{:S(2)}) copy-start(f32[1024]{0:T(1024)} %param.12) | copy-start | bytes 12292
  0.0 9.4 %copy-start.10 = (bf16[4,128,2,256]{3,2,1,0:T(2,128)(2,1)S(1)}, bf16[4,128,2,256]{3,2,1,0:T(2,128)(2,1)}, u32[]{:S(2)}) copy-start(bf16[4,128,2,256]{3,2,1,0:T(2,128)(2,1)} %param.16) | copy-start | bytes 1572868
  0.0 15.2 %collective-permute-start.12 = (bf16[256,1024]{1,0:T(8,128)(2,1)}, bf16[256,1024]{1,0:T(8,128)(2,1)S(1)}, u32[]{:S(2)}, u32[]{:S(2)}) collective-permute-start(bf16[256,1024]{1,0:T(8,128)(2,1)} %refs_4_.1), channel_id=1, source_target_pairs={{0,2},{1,3},{2,0},{3,1},{4,6},{5,7},{6,4},{7,5},{8,10},{9,11},{10,... | collective-permute-start | bytes 1572872 | tf_op jit(solution)/shard_map/ppermute | solution.py:348
  5.1 9.4 %copy-start.14 = (s32[1,4]{1,0:T(1,128)S(1)}, s32[1,4]{1,0:T(1,128)}, u32[]{:S(2)}) copy-start(s32[1,4]{1,0:T(1,128)} %param.18) | copy-start | bytes 52
  5.1 12.6 %collective-permute-start.3 = (bf16[272,128]{1,0:T(8,128)(2,1)S(1)}, bf16[272,128]{1,0:T(8,128)(2,1)S(1)}, u32[]{:S(2)}, u32[]{:S(2)}) collective-permute-start(bf16[272,128]{1,0:T(8,128)(2,1)S(1)} %get-tuple-element.15.refs_0_.q_ref), channel_id=1, source_target_pairs={{0,8},{4,12},{8,0},{12,4},{16,24},{20,28},{24,16},{28,20},{1,9},{5... | collective-permute-start | bytes 208904 | tf_op jit(solution)/shard_map/ppermute | solution.py:345
  6.8 14.5 %collective-permute-start.4 = (bf16[272,128]{1,0:T(8,128)(2,1)S(1)}, bf16[272,128]{1,0:T(8,128)(2,1)}, u32[]{:S(2)}, u32[]{:S(2)}) collective-permute-start(bf16[272,128]{1,0:T(8,128)(2,1)S(1)} %get-tuple-element.15.refs_0_.q_ref), channel_id=1, source_target_pairs={{0,16},{4,20},{8,24},{12,28},{16,0},{20,4},{24,8},{28,12},{1,17},{... | collective-permute-start | bytes 208904 | tf_op jit(solution)/shard_map/ppermute | solution.py:345
  9.4 50.8 %collective-permute-start.13 = (bf16[256,1024]{1,0:T(8,128)(2,1)S(1)}, bf16[256,1024]{1,0:T(8,128)(2,1)S(1)}, u32[]{:S(2)}, u32[]{:S(2)}) collective-permute-start(bf16[256,1024]{1,0:T(8,128)(2,1)S(1)} %copy-done.1), channel_id=1, source_target_pairs={{0,1},{1,0},{2,3},{3,2},{4,5},{5,4},{6,7},{7,6},{8,9},{9,8},{10,11... | collective-permute-start | bytes 1572872 | tf_op jit(solution)/shard_map/ppermute | solution.py:349
  9.4 10.1 %copy-start.12 = (s32[4,128]{1,0:T(4,128)S(1)}, s32[4,128]{1,0:T(4,128)}, u32[]{:S(2)}) copy-start(s32[4,128]{1,0:T(4,128)} %param.17) | copy-start | bytes 6148
  13.0 21.8 %collective-permute-start.1 = (bf16[512,256]{0,1:T(8,128)(2,1)}, bf16[512,256]{0,1:T(8,128)(2,1)}, u32[]{:S(2)}, u32[]{:S(2)}) collective-permute-start(bf16[512,256]{0,1:T(8,128)(2,1)} %bitcast.11), channel_id=1, source_target_pairs={{0,4},{4,0},{8,12},{12,8},{16,20},{20,16},{24,28},{28,24},{1,5},{5... | collective-permute-start | bytes 786440 | tf_op jit(solution)/shard_map/ppermute | solution.py:334
  15.2 44.9 %collective-permute-start.14 = (bf16[256,1024]{1,0:T(8,128)(2,1)S(1)}, bf16[256,1024]{1,0:T(8,128)(2,1)}, u32[]{:S(2)}, u32[]{:S(2)}) collective-permute-start(bf16[256,1024]{1,0:T(8,128)(2,1)S(1)} %collective-permute-done.12.refs_5_), channel_id=1, source_target_pairs={{0,1},{1,0},{2,3},{3,2},{4,5},{5,4},{6,7},{7,6},{8,9},{9,8},{10,11... | collective-permute-start | bytes 1572872 | tf_op jit(solution)/shard_map/ppermute | solution.py:349
  17.7 18.1 %collective-permute-start.2 = (bf16[256,512]{1,0:T(8,128)(2,1)}, bf16[256,512]{1,0:T(8,128)(2,1)}, u32[]{:S(2)}, u32[]{:S(2)}) collective-permute-start(bf16[256,512]{1,0:T(8,128)(2,1)} %bitcast.13.vt_ref), channel_id=1, source_target_pairs={{0,4},{4,0},{8,12},{12,8},{16,20},{20,16},{24,28},{28,24},{1,5},{5... | collective-permute-start | bytes 786440 | tf_op jit(solution)/shard_map/ppermute | solution.py:335
  21.3 6.3 %collective-permute-start.5 = (bf16[272,128]{1,0:T(8,128)(2,1)S(1)}, bf16[272,128]{1,0:T(8,128)(2,1)S(1)}, u32[]{:S(2)}, u32[]{:S(2)}) collective-permute-start(bf16[272,128]{1,0:T(8,128)(2,1)S(1)} %get-tuple-element.15.refs_0_.q_ref), channel_id=1, source_target_pairs={{0,24},{4,28},{8,16},{12,20},{16,8},{20,12},{24,0},{28,4},{1,25},{... | collective-permute-start | bytes 208904 | tf_op jit(solution)/shard_map/ppermute | solution.py:345
  27.6 6.4 %copy-start.4 = (bf16[272,128]{1,0:T(8,128)(2,1)}, bf16[272,128]{1,0:T(8,128)(2,1)S(1)}, u32[]{:S(2)}) copy-start(bf16[272,128]{1,0:T(8,128)(2,1)S(1)} %collective-permute-done.5.refs_3_) | copy-start | bytes 208900
  27.6 8.3 %collective-permute-start = (s32[4,128]{1,0:T(4,128)}, s32[4,128]{1,0:T(4,128)}, u32[]{:S(2)}, u32[]{:S(2)}) collective-permute-start(s32[4,128]{1,0:T(4,128)} %fusion.code_ref), channel_id=1, source_target_pairs={{0,4},{4,0},{8,12},{12,8},{16,20},{20,16},{24,28},{28,24},{1,5},{5... | collective-permute-start | bytes 6152 | tf_op jit(solution)/shard_map/ppermute | solution.py:336
  28.1 0.7 %copy-start.7 = (f32[2,4]{1,0:T(2,128)S(1)}, f32[2,4]{1,0:T(2,128)}, u32[]{:S(2)}) copy-start(f32[2,4]{1,0:T(2,128)} %bias_ref.5) | copy-start | bytes 100
  34.1 0.7 %copy-start.2 = (bf16[4,256,128]{2,1,0:T(8,128)(2,1)}, bf16[4,256,128]{2,1,0:T(8,128)(2,1)S(1)}, u32[]{:S(2)}) copy-start(bf16[4,256,128]{2,1,0:T(8,128)(2,1)S(1)} %get-tuple-element.19.o_ref) | copy-start | bytes 786436
  35.9 1.0 %copy-start.3 = (bf16[4,256,128]{2,1,0:T(8,128)(2,1)S(1)}, bf16[4,256,128]{2,1,0:T(8,128)(2,1)}, u32[]{:S(2)}) copy-start(bf16[4,256,128]{2,1,0:T(8,128)(2,1)} %copy-done.2) | copy-start | bytes 786436
  36.8 0.9 %copy-start.5 = (bf16[272,128]{1,0:T(8,128)(2,1)S(1)}, bf16[272,128]{1,0:T(8,128)(2,1)}, u32[]{:S(2)}) copy-start(bf16[272,128]{1,0:T(8,128)(2,1)} %copy-done.4) | copy-start | bytes 208900
  37.7 0.7 %copy-start.8 = (f32[2,4]{1,0:T(2,128)S(1)}, f32[2,4]{1,0:T(2,128)}, u32[]{:S(2)}) copy-start(f32[2,4]{1,0:T(2,128)} %bias_ref.5) | copy-start | bytes 100
  38.4 0.7 %copy-start.9 = (s32[2]{0:T(128)S(1)}, s32[2]{0:T(128)}, u32[]{:S(2)}) copy-start(s32[2]{0:T(128)} %pad_add_fusion.ids_ref) | copy-start | bytes 28
  44.4 4.9 %collective-permute-start.6 = (bf16[272,128]{1,0:T(8,128)(2,1)S(1)}, bf16[272,128]{1,0:T(8,128)(2,1)S(1)}, u32[]{:S(2)}, u32[]{:S(2)}) collective-permute-start(bf16[272,128]{1,0:T(8,128)(2,1)S(1)} %get-tuple-element.22), channel_id=1, source_target_pairs={{0,8},{4,12},{8,0},{12,4},{16,24},{20,28},{24,16},{28,20},{1,9},{5... | collective-permute-start | bytes 208904 | tf_op jit(solution)/shard_map/ppermute | solution.py:368
  45.5 6.7 %collective-permute-start.7 = (bf16[272,128]{1,0:T(8,128)(2,1)S(1)}, bf16[272,128]{1,0:T(8,128)(2,1)S(1)}, u32[]{:S(2)}, u32[]{:S(2)}) collective-permute-start(bf16[272,128]{1,0:T(8,128)(2,1)S(1)} %get-tuple-element.23), channel_id=1, source_target_pairs={{0,16},{4,20},{8,24},{12,28},{16,0},{20,4},{24,8},{28,12},{1,17},{... | collective-permute-start | bytes 208904 | tf_op jit(solution)/shard_map/ppermute | solution.py:368
  48.4 6.1 %collective-permute-start.8 = (bf16[272,128]{1,0:T(8,128)(2,1)S(1)}, bf16[272,128]{1,0:T(8,128)(2,1)S(1)}, u32[]{:S(2)}, u32[]{:S(2)}) collective-permute-start(bf16[272,128]{1,0:T(8,128)(2,1)S(1)} %get-tuple-element.24), channel_id=1, source_target_pairs={{0,24},{4,28},{8,16},{12,20},{16,8},{20,12},{24,0},{28,4},{1,25},{... | collective-permute-start | bytes 208904 | tf_op jit(solution)/shard_map/ppermute | solution.py:368
  54.8 4.3 %collective-permute-start.9 = (bf16[128,256]{1,0:T(8,128)(2,1)S(1)}, bf16[128,256]{1,0:T(8,128)(2,1)S(1)}, u32[]{:S(2)}, u32[]{:S(2)}) collective-permute-start(bf16[128,256]{1,0:T(8,128)(2,1)S(1)} %shard_map.113.refs_0_), channel_id=1, source_target_pairs={{0,2},{1,3},{2,0},{3,1},{4,6},{5,7},{6,4},{7,5},{8,10},{9,11},{10,... | collective-permute-start | bytes 196616 | tf_op jit(solution)/shard_map/ppermute | solution.py:370
  56.4 2.8 %collective-permute-start.10 = (bf16[128,256]{1,0:T(8,128)(2,1)S(1)}, bf16[128,256]{1,0:T(8,128)(2,1)S(1)}, u32[]{:S(2)}, u32[]{:S(2)}) collective-permute-start(bf16[128,256]{1,0:T(8,128)(2,1)S(1)} %shard_map.113.refs_0_), channel_id=1, source_target_pairs={{0,1},{1,0},{2,3},{3,2},{4,5},{5,4},{6,7},{7,6},{8,9},{9,8},{10,11... | collective-permute-start | bytes 196616 | tf_op jit(solution)/shard_map/ppermute | solution.py:370
  56.4 3.7 %collective-permute-start.11 = (bf16[128,256]{1,0:T(8,128)(2,1)S(1)}, bf16[128,256]{1,0:T(8,128)(2,1)S(1)}, u32[]{:S(2)}, u32[]{:S(2)}) collective-permute-start(bf16[128,256]{1,0:T(8,128)(2,1)S(1)} %shard_map.113.refs_0_), channel_id=1, source_target_pairs={{0,3},{1,2},{2,1},{3,0},{4,7},{5,6},{6,5},{7,4},{8,11},{9,10},{10,... | collective-permute-start | bytes 196616 | tf_op jit(solution)/shard_map/ppermute | solution.py:370

commit v2 on v0

--- a/solution.py
+++ b/solution.py
@@ -1,6 +1,8 @@
 import jax
 import jax.numpy as jnp
 from jax import lax
+from jax.experimental import pallas as pl
+from jax.experimental.pallas import tpu as pltpu
 from jax.sharding import PartitionSpec as P
 
 HD = 64
@@ -37,7 +39,7 @@
     return (qbuf, vbuf, flat)
 
 
-def body(
+def routed_body(
     tokens,
     norm_gain,
     w_qkv,
@@ -121,6 +123,297 @@
     return (xf + total_sum).astype(jnp.bfloat16)
 
 
+BF16, F32, I32 = jnp.bfloat16, jnp.float32, jnp.int32
+AUX = 16
+FAR = -1e30
+VMEM = pl.BlockSpec(memory_space=pltpu.VMEM)
+HBM = pl.BlockSpec(memory_space=pltpu.HBM)
+SMEM = pl.BlockSpec(memory_space=pltpu.SMEM)
+
+
+def call(kernel, outs, *args, flops=1, away=(), scratch=(), grant=16):
+    single = not isinstance(outs, (tuple, list))
+    args = [pltpu.with_memory_space_constraint(a, pltpu.HBM) if i in away else a for i, a in enumerate(args)]
+    return pl.pallas_call(
+        kernel,
+        out_shape=outs,
+        scratch_shapes=scratch,
+        in_specs=[HBM if i in away else SMEM if a.size == 1 else VMEM for i, a in enumerate(args)],
+        out_specs=VMEM if single else [VMEM] * len(outs),
+        compiler_params=pltpu.CompilerParams(vmem_limit_bytes=grant << 20),
+        cost_estimate=pl.CostEstimate(flops=1, bytes_accessed=1, transcendentals=0),
+    )(*args)
+
+
+def shape(*dims, dtype=BF16):
+    return jax.ShapeDtypeStruct(dims, dtype)
+
+
+def fetch(sems, *pairs):
+    copies = [pltpu.make_async_copy(src, dst, sems.at[i]) for i, (src, dst) in enumerate(pairs)]
+    for copy in copies:
+        copy.start()
+    return copies
+
+
+def query_kernel(
+    tok_hbm, gain_hbm, w_hbm, variate_hbm, path_hbm, bias_hbm, slot_hbm, table_hbm, len_ref,
+    msg_ref, normed_ref, rows_ref, code_ref, tok_ref,
+    gain_ref, w_ref, variate_ref, path_ref, bias_ref, slot_ref, table_ref, sems,
+):
+    copies = fetch(
+        sems, (tok_hbm, tok_ref), (w_hbm.at[0], w_ref), (gain_hbm, gain_ref), (variate_hbm, variate_ref), (path_hbm, path_ref),
+        (bias_hbm, bias_ref), (slot_hbm, slot_ref), (table_hbm, table_ref),
+    )
+    for copy in copies[2:]:
+        copy.wait()
+    pages, page = slot_ref.shape
+    length = len_ref[0]
+    offset = lax.broadcasted_iota(I32, (1, page), 1)
+    for p in range(pages):
+        place = sum(jnp.where(table_ref[0, i] == p, i, 0) for i in range(pages))
+        code_ref[p : p + 1, :] = jnp.where(place * page + offset < length, slot_ref[p : p + 1, :], 8)
+    rows, cols = tok_ref.shape[0], w_ref.shape[1]
+    for head in range(cols // HD):
+        same = jnp.full((1, rows), bias_ref[1, head], F32)
+        other = jnp.full((1, rows), bias_ref[0, head], F32)
+        rows_ref[8 * head : 8 * head + 8, :] = jnp.concatenate([same, other, same - other, jnp.zeros((5, rows), F32)], axis=0)
+    aux = [variate_ref[...].astype(F32), path_ref[...].astype(F32), jnp.zeros((AUX - 4, rows), F32)]
+    msg_ref[cols:, :] = jnp.concatenate(aux, axis=0).astype(BF16)
+    copies[0].wait()
+    x = tok_ref[...].astype(F32)
+    r = lax.rsqrt(jnp.mean(x * x, axis=1, keepdims=True) + 1e-05)
+    normed = (x * r * gain_ref[...]).astype(BF16)
+    normed_ref[...] = normed
+    copies[1].wait()
+    q = jnp.dot(normed, w_ref[...], preferred_element_type=F32).astype(BF16)
+    msg_ref[:cols, :] = (q.astype(F32) * HD ** (-0.5)).T.astype(BF16)
+
+
+def split3(x):
+    a = x.astype(BF16).astype(F32)
+    b = (x - a).astype(BF16).astype(F32)
+    return a, b, (x - a - b).astype(BF16).astype(F32)
+
+
+def split_pool(pool_ref):
+    slots, _, cols = pool_ref.shape
+    i = lax.broadcasted_iota(I32, (256, 256), 0)
+    j = lax.broadcasted_iota(I32, (256, 256), 1)
+    pick = jnp.where(j == 2 * (i % 128) + i // 128, 1.0, 0.0).astype(BF16)
+    keys, values = [], []
+    for at in range(0, slots, 128):
+        both = pool_ref[at : at + 128].reshape(256, cols)
+        apart = jnp.dot(pick, both, preferred_element_type=F32)
+        keys.append(apart[:128].astype(BF16))
+        values.append(apart[128:].T.astype(BF16))
+    return jnp.concatenate(keys, axis=0), jnp.concatenate(values, axis=1)
+
+
+def slot_terms(code_ref):
+    pages, page = code_ref.shape
+    sub = lax.broadcasted_iota(I32, (128, page), 0)
+    blocks = []
+    for p in range(pages):
+        code = jnp.broadcast_to(code_ref[p : p + 1, :], (128, page))
+        hit = ((code == sub % 8) & (sub < 24)) | ((sub >= 24) & (sub < 27))
+        term = jnp.where(hit, 1.0, 0.0)
+        term = jnp.where((sub == 27) & (code == 8), FAR, term)
+        blocks.append(term.T.astype(BF16))
+    return jnp.concatenate(blocks, axis=0)
+
+
+def row_terms(bias, variate):
+    rows = variate.shape[1]
+    sub = lax.broadcasted_iota(I32, (8, rows), 0)
+    hit = variate == sub
+    other, step = split3(bias[1:2, :]), split3(bias[2:3, :])
+    picked = [jnp.where(hit, jnp.broadcast_to(piece, (8, rows)), 0.0) for piece in step]
+    tail = jnp.where(sub == 3, 1.0, 0.0)
+    for at, piece in enumerate(other):
+        tail = jnp.where(sub == at, piece, tail)
+    top = jnp.concatenate(picked + [tail], axis=0).astype(BF16)
+    return jnp.concatenate([top, jnp.zeros((96, rows), BF16)], axis=0)
+
+
+def attend(q, keys, values_t, terms, bias, variate, head):
+    pair = head // 2
+    q_head = q[head * HD : (head + 1) * HD, :]
+    zero = jnp.zeros_like(q_head)
+    both = [q_head, zero] if head % 2 == 0 else [zero, q_head]
+    q_cat = jnp.concatenate(both + [row_terms(bias, variate)], axis=0)
+    k_cat = jnp.concatenate([keys[:, pair * 128 : (pair + 1) * 128], terms], axis=1)
+    scores = jnp.dot(k_cat, q_cat, preferred_element_type=F32)
+    peak = jnp.max(scores, axis=0, keepdims=True)
+    weights = jnp.exp(scores - peak)
+    total = jnp.sum(weights, axis=0, keepdims=True)
+    mixed = jnp.dot(values_t[head * HD : (head + 1) * HD, :], weights.astype(BF16), preferred_element_type=F32)
+    return (mixed / total).astype(BF16), peak + jnp.log(total)
+
+
+def wide(rows_ref, head, blocks):
+    return jnp.concatenate([rows_ref[8 * head : 8 * head + 8, :]] * blocks, axis=1)
+
+
+def gather_rows(msgs, cols):
+    q = jnp.concatenate([msg[:cols, :] for msg in msgs], axis=1)
+    aux = jnp.concatenate([msg[cols:, :].astype(F32).astype(I32) for msg in msgs], axis=1)
+    return q, aux
+
+
+def own_kernel(normed_ref, w_ref, k_ref, v_ref):
+    for i, own_ref in ((1, k_ref), (2, v_ref)):
+        own = jnp.dot(normed_ref[...], w_ref[i], preferred_element_type=F32).astype(BF16)
+        own_ref[...] = own.astype(F32).T.astype(BF16)
+
+
+def first_kernel(rows_ref, pool_ref, code_ref, *refs):
+    msgs, (o_ref, lse_ref) = refs[:-2], refs[-2:]
+    keys, values_t = split_pool(pool_ref)
+    terms = slot_terms(code_ref)
+    cols = keys.shape[1]
+    q, aux = gather_rows(msgs, cols)
+    for head in range(cols // HD):
+        o, lse = attend(q, keys, values_t, terms, wide(rows_ref, head, len(msgs)), aux[0:1, :], head)
+        o_ref[head * HD : (head + 1) * HD, :] = o
+        lse_ref[head : head + 1, :] = lse
+
+
+def second_kernel(rows_ref, pool_ref, code_ref, o_ref, lse_ref, *refs):
+    count = len(refs) // 2
+    msgs, outs = refs[:count], refs[count:]
+    keys, values_t = split_pool(pool_ref)
+    cols = keys.shape[1]
+    heads = cols // HD
+    rows = msgs[0].shape[1]
+    terms = slot_terms(code_ref)
+    q, aux = gather_rows(msgs, cols)
+    me = lax.axis_index("seq")
+    named = lambda node: jnp.max((aux[1:4, :] == node).astype(I32), axis=0, keepdims=True) > 0
+    mine, theirs = named(me), named(me ^ 1)
+    pieces = []
+    for head in range(heads):
+        o2, lse2 = attend(q, keys, values_t, terms, wide(rows_ref, head, count), aux[0:1, :], head)
+        lse2 = jnp.where(theirs, lse2, FAR)
+        lse1 = jnp.where(mine, lse_ref[head : head + 1, :], FAR)
+        top = jnp.maximum(lse1, lse2)
+        w1, w2 = jnp.exp(lse1 - top), jnp.exp(lse2 - top)
+        o1 = o_ref[head * HD : (head + 1) * HD, :].astype(F32)
+        merged = ((w1 * o1 + w2 * o2.astype(F32)) / (w1 + w2)).astype(BF16)
+        for b, out in enumerate(outs):
+            out[head * HD : (head + 1) * HD, :] = merged[:, b * rows : (b + 1) * rows]
+        pieces += split3(top + jnp.log(w1 + w2))
+    pieces.append(jnp.zeros((AUX - 3 * heads, count * rows), F32))
+    tail = jnp.concatenate(pieces, axis=0).astype(BF16)
+    for b, out in enumerate(outs):
+        out[cols:, :] = tail[:, b * rows : (b + 1) * rows]
+
+
+def combine_kernel(rows_ref, q_ref, k_ref, v_ref, *refs):
+    parts, attn_ref = refs[:-1], refs[-1]
+    cols = k_ref.shape[0]
+    auxes = [part[cols:, :].astype(F32) for part in parts]
+    done = []
+    for head in range(cols // HD):
+        at = slice(head * HD, (head + 1) * HD)
+        q, k = q_ref[at, :].astype(F32), k_ref[at, :].astype(F32)
+        own = jnp.sum(q * k, axis=0, keepdims=True) + rows_ref[8 * head : 8 * head + 1, :]
+        lses = [sum(aux[3 * head + i : 3 * head + i + 1, :] for i in range(3)) for aux in auxes]
+        top = own
+        for lse in lses:
+            top = jnp.maximum(top, lse)
+        weight = jnp.exp(own - top)
+        whole = weight
+        acc = weight * v_ref[at, :].astype(F32)
+        for lse, part in zip(lses, parts):
+            weight = jnp.exp(lse - top)
+            whole = whole + weight
+            acc = acc + weight * part[at, :].astype(F32)
+        done.append(acc / whole)
+    attn_ref[...] = jnp.concatenate(done, axis=0).T.astype(BF16)
+
+
+def project_kernel(tok_ref, *refs):
+    out_ref = refs[-1]
+    half = (len(refs) - 1) // 2
+    acc = None
+    for attn, w in zip(refs[:half], refs[half : 2 * half]):
+        term = jnp.dot(attn[...], w[...], preferred_element_type=F32)
+        acc = term if acc is None else acc + term
+    out_ref[...] = (tok_ref[...].astype(F32) + acc).astype(BF16)
+
+
+def xor(axis, k):
+    return [(i, i ^ k) for i in range(lax.axis_size(axis))]
+
+
+def dense_body(
+    tokens,
+    norm_gain,
+    w_qkv,
+    w_out,
+    head_bias,
+    kv_pool,
+    key_variate,
+    page_table,
+    node_len,
+    path_nodes,
+    query_variate,
+):
+    rows, width = tokens.shape
+    cols = w_qkv.shape[2]
+    heads = cols // HD
+    pages, page = key_variate.shape
+    slots = pages * page
+    groups = [2 * k for k in range(max(1, lax.axis_size("seq") // 2))]
+
+    pool = kv_pool.reshape(slots, 2, cols)
+    pool2 = lax.ppermute(pool, "seq", xor("seq", 1))
+
+    w3 = w_qkv.transpose(1, 0, 2)
+    smem = lambda *dims: pltpu.SMEM(dims, I32)
+    msg, normed, bias, code, tok = call(
+        query_kernel,
+        [
+            shape(cols + AUX, rows),
+            shape(rows, width),
+            shape(8 * heads, rows, dtype=F32),
+            shape(pages, page, dtype=I32),
+            shape(rows, width),
+        ],
+        tokens, norm_gain[None], w3, query_variate[None], path_nodes.T, head_bias, key_variate, page_table, node_len,
+        flops=2 * rows * width * cols,
+        away=range(8),
+        scratch=[
+            pltpu.VMEM((1, width), F32), pltpu.VMEM((width, cols), BF16), pltpu.VMEM((1, rows), I32), pltpu.VMEM((3, rows), I32),
+            pltpu.VMEM((2, heads), F32), pltpu.VMEM((pages, page), I32), smem(1, pages), pltpu.SemaphoreType.DMA((8,)),
+        ],
+    )
+    code2 = lax.ppermute(code, "seq", xor("seq", 1))
+    msgs = [msg] + [lax.ppermute(msg, "seq", xor("seq", k)) for k in groups[1:]]
+
+    w_own, *msgs = lax.optimization_barrier((w_out, *msgs))
+    w_far = lax.ppermute(w_own, "tp", xor("tp", 2))
+
+    work = 4 * len(groups) * rows * slots * cols
+    wide_rows = len(groups) * rows
+    o1, lse1 = call(
+        first_kernel,
+        [shape(cols, wide_rows), shape(heads, wide_rows, dtype=F32)],
+        bias, pool, code, *msgs,
+        flops=work,
+    )
+    merged = call(
+        second_kernel, [shape(cols + AUX, rows)] * len(groups), bias, pool2, code2, o1, lse1, *msgs, flops=work)
+    first, w_own, w_far, normed = lax.optimization_barrier((merged[0], w_own, w_far, normed))
+    key, value = call(own_kernel, [shape(cols, rows)] * 2, normed, w3, flops=4 * rows * width * cols)
+    outs = [w_own, w_far] + [lax.ppermute(w, "tp", xor("tp", 1)) for w in (w_own, w_far)]
+    back = [first] + [lax.ppermute(m, "seq", xor("seq", k)) for m, k in zip(merged[1:], groups[1:])]
+    attn = call(combine_kernel, shape(rows, cols), bias, msg, key, value, *back)
+    attns = [attn] + [lax.ppermute(attn, "tp", xor("tp", k)) for k in (2, 1, 3)]
+    return call(project_kernel, shape(rows, width), tok, *attns, *outs, flops=2 * rows * width * width)
+
+
 def solution(mesh):
     in_specs = (
         P("seq", None),
@@ -136,4 +429,7 @@
         P("seq"),
     )
     out_specs = P("seq", None)
+    owners, parts = mesh.shape["seq"], mesh.shape["tp"]
+    dense = owners <= 8 and owners & (owners - 1) == 0 and parts == 4
+    body = dense_body if dense else routed_body
     return jax.shard_map(body, mesh=mesh, in_specs=in_specs, out_specs=out_specs, check_vma=False)

time: 331 us -> 43.9 us (0.13)
  waiting for transfers between devices: 88.2 us -> 16.9 us
  local copies, waits for them, and re-layouts: 69.7 us -> 0.01 us
  matrix products: 52.5 us -> 0 us
  starting transfers between devices: 55.4 us -> 17.5 us
  blocking collectives: 30.2 us -> 0 us
  other arithmetic: 17.8 us -> 0 us
  between operations: 13.9 us -> 0.8 us
  Pallas kernels: 0 us -> 8.48 us
    all_to_all x12 -> x0, waiting for transfers between devices: 55.5 us -> none  [the longest x3 26 us: body(): lax.all_to_all(mixed, 'seq', split_axis=0, concat_axis=0, tiled=True)]
    all_to_all x12 -> x0, starting transfers between devices: 55.4 us -> none  [the longest x3 14.7 us: body(): lax.all_to_all(vbuf, 'seq', split_axis=0, concat_axis=0, tiled=True)]
    dot_general x26 -> x0, matrix products: 52.5 us -> none  [the longest x12 33.3 us: head_attend(): jnp.dot(qh, kh.T, preferred_element_type=jnp.float32) * HD ** (-0.5)]
    psum x1 -> x0, waiting for transfers between devices: 32.7 us -> none  [body(): total_sum = lax.psum(partial_sum, 'tp')]
    all_to_all x3 -> x0, blocking collectives: 30.2 us -> none  [the longest x2 17.9 us: body(): lax.all_to_all(total, 'seq', split_axis=0, concat_axis=0, tiled=True)]
    ppermute x0 -> x14, starting transfers between devices: none -> 17.5 us  [the longest x3 5.76 us: dense_body(): msgs = [msg] + [lax.ppermute(msg, 'seq', xor('seq', k)) for k in groups[1:]]]
    dynamic_update_slice x36 -> x0, local copies, waits for them, and re-layouts: 17.1 us -> none  [body(): lax.map(per_head, (heads_q, node_keys, node_values, head_bias[1], head_bi...]
    ppermute x0 -> x14, waiting for transfers between devices: none -> 16.9 us  [the longest x3 4.15 us: dense_body(): lax.ppermute(m, 'seq', xor('seq', k))]
  transfers between devices with their start and end apart: 13 -> 14, of which waited for: 10 -> 8; matrix products, arithmetic and copies ran while one was open for 40% -> 0% of each run, Pallas kernels for 0% -> 13%
where the time goes in v2:
time: 43.9 us; the launch traced here: 43.8 us
  starting transfers between devices  17.5 us (40%)
  waiting for transfers between devices  16.9 us (38%)
  Pallas kernels  8.48 us (19%)
  between operations  0.8 us (2%)
    pallas_call x6, Pallas kernels, call(): pl.pallas_call(kernel, out_shape=outs, scratch_shapes=scratch, in_specs=[...  8.48 us
    ppermute x3, starting transfers between devices, dense_body(): msgs = [msg] + [lax.ppermute(msg, 'seq', xor('seq', k)) for k in groups[1:]]  5.76 us
    ppermute x3, starting transfers between devices, dense_body(): lax.ppermute(m, 'seq', xor('seq', k))  4.39 us
    ppermute x3, waiting for transfers between devices, dense_body(): lax.ppermute(m, 'seq', xor('seq', k))  4.15 us
    ppermute x3, waiting for transfers between devices, dense_body(): attns = [attn] + [lax.ppermute(attn, 'tp', xor('tp', k)) for k in (2, 1, 3)]  3.78 us
    ppermute x3, waiting for transfers between devices, dense_body(): msgs = [msg] + [lax.ppermute(msg, 'seq', xor('seq', k)) for k in groups[1:]]  3.6 us
    ppermute x1, waiting for transfers between devices, dense_body(): w_far = lax.ppermute(w_own, 'tp', xor('tp', 2))  3 us
    ppermute x1, waiting for transfers between devices, dense_body(): code2 = lax.ppermute(code, 'seq', xor('seq', 1))  2.4 us
  transfers between devices with their start and end apart: 14, of which 8 were waited for; matrix products, arithmetic and copies ran while one was open for 0% of the time, Pallas kernels for 13%

profile of v2, /device:TPU:0, one launch (start us, length us, event | category | flops | bytes accessed | tf_op | source)
XLA Modules:
  0.0 43.8 jit_solution(12919902388690541063)
XLA Ops:
  0.0 0.0 copy-start.1
  0.0 0.0 copy-start.2
  0.7 0.0 copy-start
  0.8 1.8 %shard_map.109 = (bf16[272,128]{1,0:T(8,128)(2,1)S(1)}, bf16[128,1024]{1,0:T(8,128)(2,1)S(1)}, f32[32,128]{1,0:T(8,128)S(1)}, s32[4,128]{1,0:T(4,128)S(1)}, bf16[128,1024]{1,0:T(8,128)(2,1)S(1)}) custom-call(bf16[128,1024]{1,0:T(8,128)(2,1)} %tok_hbm.1, f32[1,1024]{1,0:T(1,128)} %bitcast.9, bf16[3,1024,256]{2,1,0:T(8,128)(2,1)} %bitcast.5, ...), custom_call_target="tpu_custom_call" | custom-call | flops 1 | bytes 1 | tf_op jit(solution)/shard_map/pallas_call | solution.py:137
  2.5 5.1 %collective-permute-start.4 = (bf16[272,128]{1,0:T(8,128)(2,1)S(1)}, bf16[272,128]{1,0:T(8,128)(2,1)S(1)}, u32[]{:S(2)}, u32[]{:S(2)}) collective-permute-start(bf16[272,128]{1,0:T(8,128)(2,1)S(1)} %get-tuple-element.31.refs_0_.q_ref), channel_id=1, source_target_pairs={{0,24},{4,28},{8,16},{12,20},{16,8},{20,12},{24,0},{28,4},{1,25},{... | collective-permute-start | bytes 208904 | tf_op jit(solution)/shard_map/ppermute | solution.py:393
  7.6 0.0 collective-permute-start.3
  7.6 0.6 %collective-permute-start.2 = (bf16[272,128]{1,0:T(8,128)(2,1)S(1)}, bf16[272,128]{1,0:T(8,128)(2,1)S(1)}, u32[]{:S(2)}, u32[]{:S(2)}) collective-permute-start(bf16[272,128]{1,0:T(8,128)(2,1)S(1)} %get-tuple-element.31.refs_0_.q_ref), channel_id=1, source_target_pairs={{0,8},{4,12},{8,0},{12,4},{16,24},{20,28},{24,16},{28,20},{1,9},{5... | collective-permute-start | bytes 208904 | tf_op jit(solution)/shard_map/ppermute | solution.py:393
  8.3 0.0 copy-done.1
  8.3 1.7 %collective-permute-start = (bf16[512,2,256]{2,1,0:T(2,128)(2,1)S(1)}, bf16[512,2,256]{2,1,0:T(2,128)(2,1)S(1)}, u32[]{:S(2)}, u32[]{:S(2)}) collective-permute-start(bf16[512,2,256]{2,1,0:T(2,128)(2,1)S(1)} %bitcast.7), channel_id=1, source_target_pairs={{0,4},{4,0},{8,12},{12,8},{16,20},{20,16},{24,28},{28,24},{1,5},{5... | collective-permute-start | bytes 1572872 | tf_op jit(solution)/shard_map/ppermute | solution.py:371
  9.9 0.4 collective-permute-done.4.refs_3_
  10.3 3.2 %collective-permute-done.3.refs_2_ = bf16[272,128]{1,0:T(8,128)(2,1)S(1)} collective-permute-done((bf16[272,128]{1,0:T(8,128)(2,1)S(1)}, bf16[272,128]{1,0:T(8,128)(2,1)S(1)}, u32[]{:S(2)}, u32[]{:S(2)}) %collective-permute-start.3) | collective-permute-done | bytes 69664 | tf_op jit(solution)/shard_map/ppermute | solution.py:393
  13.6 0.0 collective-permute-done.2.refs_1_
  13.6 0.0 copy-done.2
  13.6 1.5 %collective-permute-start.5 = (bf16[256,1024]{1,0:T(8,128)(2,1)S(1)}, bf16[256,1024]{1,0:T(8,128)(2,1)S(1)}, u32[]{:S(2)}, u32[]{:S(2)}) collective-permute-start(bf16[256,1024]{1,0:T(8,128)(2,1)S(1)} %copy-done.2), channel_id=1, source_target_pairs={{0,2},{1,3},{2,0},{3,1},{4,6},{5,7},{6,4},{7,5},{8,10},{9,11},{10,... | collective-permute-start | bytes 1572872 | tf_op jit(solution)/shard_map/ppermute | solution.py:396
  15.0 1.5 %collective-permute-start.1 = (s32[4,128]{1,0:T(4,128)S(1)}, s32[4,128]{1,0:T(4,128)S(1)}, u32[]{:S(2)}, u32[]{:S(2)}) collective-permute-start(s32[4,128]{1,0:T(4,128)S(1)} %get-tuple-element.30.code_ref), channel_id=1, source_target_pairs={{0,4},{4,0},{8,12},{12,8},{16,20},{20,16},{24,28},{28,24},{1,5},{5... | collective-permute-start | bytes 6152 | tf_op jit(solution)/shard_map/ppermute | solution.py:392
  16.6 2.5 %shard_map.110 = (bf16[256,512]{1,0:T(8,128)(2,1)S(1)}, f32[4,512]{1,0:T(4,128)S(1)}) custom-call(f32[32,128]{1,0:T(8,128)S(1)} %get-tuple-element.28.rows_ref, bf16[512,2,256]{2,1,0:T(2,128)(2,1)S(1)} %bitcast.8, s32[4,128]{1,0:T(4,128)S(1)} %get-tuple-element.30.code_ref, bf16[272,128]{1,0:T(8,128)(2,1)S(1)} %get-tuple-element.31.refs_0_.q_ref, ...), custom_call_target="tpu_custom_call" | custom-call | flops 1 | bytes 1 | tf_op jit(solution)/shard_map/pallas_call | solution.py:137
  19.0 2.4 %collective-permute-done.1.code_ref = s32[4,128]{1,0:T(4,128)S(1)} collective-permute-done((s32[4,128]{1,0:T(4,128)S(1)}, s32[4,128]{1,0:T(4,128)S(1)}, u32[]{:S(2)}, u32[]{:S(2)}) %collective-permute-start.1) | collective-permute-done | bytes 2080 | tf_op jit(solution)/shard_map/ppermute | solution.py:392
  21.4 0.0 collective-permute-done.pool_ref
  21.4 2.5 %shard_map.111 = (bf16[272,128]{1,0:T(8,128)(2,1)S(1)}, bf16[272,128]{1,0:T(8,128)(2,1)S(1)}, bf16[272,128]{1,0:T(8,128)(2,1)S(1)}, bf16[272,128]{1,0:T(8,128)(2,1)S(1)}) custom-call(f32[32,128]{1,0:T(8,128)S(1)} %get-tuple-element.28.rows_ref, bf16[512,2,256]{2,1,0:T(2,128)(2,1)S(1)} %collective-permute-done.pool_ref, ...), custom_call_target="tpu_custom_call" | custom-call | flops 1 | bytes 1 | tf_op jit(solution)/shard_map/pallas_call | solution.py:137
  23.9 3.0 %collective-permute-done.5.refs_5_ = bf16[256,1024]{1,0:T(8,128)(2,1)S(1)} collective-permute-done((bf16[256,1024]{1,0:T(8,128)(2,1)S(1)}, bf16[256,1024]{1,0:T(8,128)(2,1)S(1)}, u32[]{:S(2)}, u32[]{:S(2)}) %collective-permute-start.5) | collective-permute-done | bytes 524320 | tf_op jit(solution)/shard_map/ppermute | solution.py:396
  26.9 0.0 collective-permute-start.12
  26.9 0.5 %collective-permute-start.13 = (bf16[256,1024]{1,0:T(8,128)(2,1)S(1)}, bf16[256,1024]{1,0:T(8,128)(2,1)S(1)}, u32[]{:S(2)}, u32[]{:S(2)}) collective-permute-start(bf16[256,1024]{1,0:T(8,128)(2,1)S(1)} %collective-permute-done.5.refs_5_), channel_id=1, source_target_pairs={{0,1},{1,0},{2,3},{3,2},{4,5},{5,4},{6,7},{7,6},{8,9},{9,8},{10,11... | collective-permute-start | bytes 1572872 | tf_op jit(solution)/shard_map/ppermute | solution.py:410
  27.5 0.5 %collective-permute-start.6 = (bf16[272,128]{1,0:T(8,128)(2,1)S(1)}, bf16[272,128]{1,0:T(8,128)(2,1)S(1)}, u32[]{:S(2)}, u32[]{:S(2)}) collective-permute-start(bf16[272,128]{1,0:T(8,128)(2,1)S(1)} %get-tuple-element.44), channel_id=1, source_target_pairs={{0,8},{4,12},{8,0},{12,4},{16,24},{20,28},{24,16},{28,20},{1,9},{5... | collective-permute-start | bytes 208904 | tf_op jit(solution)/shard_map/ppermute | solution.py:411
  27.9 1.7 %collective-permute-start.7 = (bf16[272,128]{1,0:T(8,128)(2,1)S(1)}, bf16[272,128]{1,0:T(8,128)(2,1)S(1)}, u32[]{:S(2)}, u32[]{:S(2)}) collective-permute-start(bf16[272,128]{1,0:T(8,128)(2,1)S(1)} %get-tuple-element.45), channel_id=1, source_target_pairs={{0,16},{4,20},{8,24},{12,28},{16,0},{20,4},{24,8},{28,12},{1,17},{... | collective-permute-start | bytes 208904 | tf_op jit(solution)/shard_map/ppermute | solution.py:411
  29.7 2.2 %collective-permute-start.8 = (bf16[272,128]{1,0:T(8,128)(2,1)S(1)}, bf16[272,128]{1,0:T(8,128)(2,1)S(1)}, u32[]{:S(2)}, u32[]{:S(2)}) collective-permute-start(bf16[272,128]{1,0:T(8,128)(2,1)S(1)} %get-tuple-element.46), channel_id=1, source_target_pairs={{0,24},{4,28},{8,16},{12,20},{16,8},{20,12},{24,0},{28,4},{1,25},{... | collective-permute-start | bytes 208904 | tf_op jit(solution)/shard_map/ppermute | solution.py:411
  31.8 0.0 copy-done
  31.8 0.4 shard_map.112
  32.2 0.3 collective-permute-done.6.refs_1_
  32.5 3.9 %collective-permute-done.7.refs_2_ = bf16[272,128]{1,0:T(8,128)(2,1)S(1)} collective-permute-done((bf16[272,128]{1,0:T(8,128)(2,1)S(1)}, bf16[272,128]{1,0:T(8,128)(2,1)S(1)}, u32[]{:S(2)}, u32[]{:S(2)}) %collective-permute-start.7) | collective-permute-done | bytes 69664 | tf_op jit(solution)/shard_map/ppermute | solution.py:411
  36.4 0.0 collective-permute-done.8.refs_3_
  36.4 0.2 shard_map.113.refs_0_
  36.6 0.1 collective-permute-start.11
  36.7 1.6 %collective-permute-start.10 = (bf16[128,256]{1,0:T(8,128)(2,1)S(1)}, bf16[128,256]{1,0:T(8,128)(2,1)S(1)}, u32[]{:S(2)}, u32[]{:S(2)}) collective-permute-start(bf16[128,256]{1,0:T(8,128)(2,1)S(1)} %shard_map.113.refs_0_), channel_id=1, source_target_pairs={{0,1},{1,0},{2,3},{3,2},{4,5},{5,4},{6,7},{7,6},{8,9},{9,8},{10,11... | collective-permute-start | bytes 196616 | tf_op jit(solution)/shard_map/ppermute | solution.py:413
  38.3 0.5 %collective-permute-start.9 = (bf16[128,256]{1,0:T(8,128)(2,1)S(1)}, bf16[128,256]{1,0:T(8,128)(2,1)S(1)}, u32[]{:S(2)}, u32[]{:S(2)}) collective-permute-start(bf16[128,256]{1,0:T(8,128)(2,1)S(1)} %shard_map.113.refs_0_), channel_id=1, source_target_pairs={{0,2},{1,3},{2,0},{3,1},{4,6},{5,7},{6,4},{7,5},{8,10},{9,11},{10,... | collective-permute-start | bytes 196616 | tf_op jit(solution)/shard_map/ppermute | solution.py:413
  38.8 2.2 %collective-permute-done.11.refs_3_ = bf16[128,256]{1,0:T(8,128)(2,1)S(1)} collective-permute-done((bf16[128,256]{1,0:T(8,128)(2,1)S(1)}, bf16[128,256]{1,0:T(8,128)(2,1)S(1)}, u32[]{:S(2)}, u32[]{:S(2)}) %collective-permute-start.11) | collective-permute-done | bytes 65568 | tf_op jit(solution)/shard_map/ppermute | solution.py:413
  41.0 0.0 collective-permute-done.10.refs_2_
  41.0 1.6 %collective-permute-done.9.refs_1_ = bf16[128,256]{1,0:T(8,128)(2,1)S(1)} collective-permute-done((bf16[128,256]{1,0:T(8,128)(2,1)S(1)}, bf16[128,256]{1,0:T(8,128)(2,1)S(1)}, u32[]{:S(2)}, u32[]{:S(2)}) %collective-permute-start.9) | collective-permute-done | bytes 65568 | tf_op jit(solution)/shard_map/ppermute | solution.py:413
  42.6 0.0 collective-permute-done.12.refs_6_
  42.6 0.0 collective-permute-done.13.refs_7_
  42.6 1.2 %shard_map.114 = bf16[128,1024]{1,0:T(8,128)(2,1)} custom-call(bf16[128,1024]{1,0:T(8,128)(2,1)S(1)} %get-tuple-element.27.tok_ref, bf16[128,256]{1,0:T(8,128)(2,1)S(1)} %shard_map.113.refs_0_, bf16[128,256]{1,0:T(8,128)(2,1)S(1)} %collective-permute-done.9.refs_1_, bf16[128,256]{1,0:T(8,128)(2,1)S(1)} %collective-permute-done.10.refs_2_, ...), custom_call_target="tpu_custom_call" | custom-call | flops 1 | bytes 1 | tf_op jit(solution)/shard_map/pallas_call | solution.py:137
Async XLA Ops:
  0.0 8.3 %copy-start.1 = (bf16[4,128,2,256]{3,2,1,0:T(2,128)(2,1)S(1)}, bf16[4,128,2,256]{3,2,1,0:T(2,128)(2,1)}, u32[]{:S(2)}) copy-start(bf16[4,128,2,256]{3,2,1,0:T(2,128)(2,1)} %param.16) | copy-start | bytes 1572868
  0.0 13.6 %copy-start.2 = (bf16[256,1024]{1,0:T(8,128)(2,1)S(1)}, bf16[256,1024]{1,0:T(8,128)(2,1)}, u32[]{:S(2)}) copy-start(bf16[256,1024]{1,0:T(8,128)(2,1)} %refs_4_) | copy-start | bytes 1572868
  0.7 31.1 %copy-start = (bf16[1024,3,256]{2,0,1:T(8,128)(2,1)S(1)}, bf16[1024,3,256]{2,0,1:T(8,128)(2,1)}, u32[]{:S(2)}) copy-start(bf16[1024,3,256]{2,0,1:T(8,128)(2,1)} %param.13) | copy-start | bytes 4718596
  2.5 7.8 %collective-permute-start.4 = (bf16[272,128]{1,0:T(8,128)(2,1)S(1)}, bf16[272,128]{1,0:T(8,128)(2,1)S(1)}, u32[]{:S(2)}, u32[]{:S(2)}) collective-permute-start(bf16[272,128]{1,0:T(8,128)(2,1)S(1)} %get-tuple-element.31.refs_0_.q_ref), channel_id=1, source_target_pairs={{0,24},{4,28},{8,16},{12,20},{16,8},{20,12},{24,0},{28,4},{1,25},{... | collective-permute-start | bytes 208904 | tf_op jit(solution)/shard_map/ppermute | solution.py:393
  7.6 5.9 %collective-permute-start.3 = (bf16[272,128]{1,0:T(8,128)(2,1)S(1)}, bf16[272,128]{1,0:T(8,128)(2,1)S(1)}, u32[]{:S(2)}, u32[]{:S(2)}) collective-permute-start(bf16[272,128]{1,0:T(8,128)(2,1)S(1)} %get-tuple-element.31.refs_0_.q_ref), channel_id=1, source_target_pairs={{0,16},{4,20},{8,24},{12,28},{16,0},{20,4},{24,8},{28,12},{1,17},{... | collective-permute-start | bytes 208904 | tf_op jit(solution)/shard_map/ppermute | solution.py:393
  7.6 5.9 %collective-permute-start.2 = (bf16[272,128]{1,0:T(8,128)(2,1)S(1)}, bf16[272,128]{1,0:T(8,128)(2,1)S(1)}, u32[]{:S(2)}, u32[]{:S(2)}) collective-permute-start(bf16[272,128]{1,0:T(8,128)(2,1)S(1)} %get-tuple-element.31.refs_0_.q_ref), channel_id=1, source_target_pairs={{0,8},{4,12},{8,0},{12,4},{16,24},{20,28},{24,16},{28,20},{1,9},{5... | collective-permute-start | bytes 208904 | tf_op jit(solution)/shard_map/ppermute | solution.py:393
  8.3 13.2 %collective-permute-start = (bf16[512,2,256]{2,1,0:T(2,128)(2,1)S(1)}, bf16[512,2,256]{2,1,0:T(2,128)(2,1)S(1)}, u32[]{:S(2)}, u32[]{:S(2)}) collective-permute-start(bf16[512,2,256]{2,1,0:T(2,128)(2,1)S(1)} %bitcast.7), channel_id=1, source_target_pairs={{0,4},{4,0},{8,12},{12,8},{16,20},{20,16},{24,28},{28,24},{1,5},{5... | collective-permute-start | bytes 1572872 | tf_op jit(solution)/shard_map/ppermute | solution.py:371
  13.6 13.4 %collective-permute-start.5 = (bf16[256,1024]{1,0:T(8,128)(2,1)S(1)}, bf16[256,1024]{1,0:T(8,128)(2,1)S(1)}, u32[]{:S(2)}, u32[]{:S(2)}) collective-permute-start(bf16[256,1024]{1,0:T(8,128)(2,1)S(1)} %copy-done.2), channel_id=1, source_target_pairs={{0,2},{1,3},{2,0},{3,1},{4,6},{5,7},{6,4},{7,5},{8,10},{9,11},{10,... | collective-permute-start | bytes 1572872 | tf_op jit(solution)/shard_map/ppermute | solution.py:396
  15.0 6.4 %collective-permute-start.1 = (s32[4,128]{1,0:T(4,128)S(1)}, s32[4,128]{1,0:T(4,128)S(1)}, u32[]{:S(2)}, u32[]{:S(2)}) collective-permute-start(s32[4,128]{1,0:T(4,128)S(1)} %get-tuple-element.30.code_ref), channel_id=1, source_target_pairs={{0,4},{4,0},{8,12},{12,8},{16,20},{20,16},{24,28},{28,24},{1,5},{5... | collective-permute-start | bytes 6152 | tf_op jit(solution)/shard_map/ppermute | solution.py:392
  26.9 15.6 %collective-permute-start.12 = (bf16[256,1024]{1,0:T(8,128)(2,1)S(1)}, bf16[256,1024]{1,0:T(8,128)(2,1)S(1)}, u32[]{:S(2)}, u32[]{:S(2)}) collective-permute-start(bf16[256,1024]{1,0:T(8,128)(2,1)S(1)} %copy-done.2), channel_id=1, source_target_pairs={{0,1},{1,0},{2,3},{3,2},{4,5},{5,4},{6,7},{7,6},{8,9},{9,8},{10,11... | collective-permute-start | bytes 1572872 | tf_op jit(solution)/shard_map/ppermute | solution.py:410
  26.9 15.6 %collective-permute-start.13 = (bf16[256,1024]{1,0:T(8,128)(2,1)S(1)}, bf16[256,1024]{1,0:T(8,128)(2,1)S(1)}, u32[]{:S(2)}, u32[]{:S(2)}) collective-permute-start(bf16[256,1024]{1,0:T(8,128)(2,1)S(1)} %collective-permute-done.5.refs_5_), channel_id=1, source_target_pairs={{0,1},{1,0},{2,3},{3,2},{4,5},{5,4},{6,7},{7,6},{8,9},{9,8},{10,11... | collective-permute-start | bytes 1572872 | tf_op jit(solution)/shard_map/ppermute | solution.py:410
  27.5 5.1 %collective-permute-start.6 = (bf16[272,128]{1,0:T(8,128)(2,1)S(1)}, bf16[272,128]{1,0:T(8,128)(2,1)S(1)}, u32[]{:S(2)}, u32[]{:S(2)}) collective-permute-start(bf16[272,128]{1,0:T(8,128)(2,1)S(1)} %get-tuple-element.44), channel_id=1, source_target_pairs={{0,8},{4,12},{8,0},{12,4},{16,24},{20,28},{24,16},{28,20},{1,9},{5... | collective-permute-start | bytes 208904 | tf_op jit(solution)/shard_map/ppermute | solution.py:411
  27.9 8.4 %collective-permute-start.7 = (bf16[272,128]{1,0:T(8,128)(2,1)S(1)}, bf16[272,128]{1,0:T(8,128)(2,1)S(1)}, u32[]{:S(2)}, u32[]{:S(2)}) collective-permute-start(bf16[272,128]{1,0:T(8,128)(2,1)S(1)} %get-tuple-element.45), channel_id=1, source_target_pairs={{0,16},{4,20},{8,24},{12,28},{16,0},{20,4},{24,8},{28,12},{1,17},{... | collective-permute-start | bytes 208904 | tf_op jit(solution)/shard_map/ppermute | solution.py:411
  29.7 6.7 %collective-permute-start.8 = (bf16[272,128]{1,0:T(8,128)(2,1)S(1)}, bf16[272,128]{1,0:T(8,128)(2,1)S(1)}, u32[]{:S(2)}, u32[]{:S(2)}) collective-permute-start(bf16[272,128]{1,0:T(8,128)(2,1)S(1)} %get-tuple-element.46), channel_id=1, source_target_pairs={{0,24},{4,28},{8,16},{12,20},{16,8},{20,12},{24,0},{28,4},{1,25},{... | collective-permute-start | bytes 208904 | tf_op jit(solution)/shard_map/ppermute | solution.py:411
  36.6 4.4 %collective-permute-start.11 = (bf16[128,256]{1,0:T(8,128)(2,1)S(1)}, bf16[128,256]{1,0:T(8,128)(2,1)S(1)}, u32[]{:S(2)}, u32[]{:S(2)}) collective-permute-start(bf16[128,256]{1,0:T(8,128)(2,1)S(1)} %shard_map.113.refs_0_), channel_id=1, source_target_pairs={{0,3},{1,2},{2,1},{3,0},{4,7},{5,6},{6,5},{7,4},{8,11},{9,10},{10,... | collective-permute-start | bytes 196616 | tf_op jit(solution)/shard_map/ppermute | solution.py:413
  36.7 4.3 %collective-permute-start.10 = (bf16[128,256]{1,0:T(8,128)(2,1)S(1)}, bf16[128,256]{1,0:T(8,128)(2,1)S(1)}, u32[]{:S(2)}, u32[]{:S(2)}) collective-permute-start(bf16[128,256]{1,0:T(8,128)(2,1)S(1)} %shard_map.113.refs_0_), channel_id=1, source_target_pairs={{0,1},{1,0},{2,3},{3,2},{4,5},{5,4},{6,7},{7,6},{8,9},{9,8},{10,11... | collective-permute-start | bytes 196616 | tf_op jit(solution)/shard_map/ppermute | solution.py:413
  38.3 4.3 %collective-permute-start.9 = (bf16[128,256]{1,0:T(8,128)(2,1)S(1)}, bf16[128,256]{1,0:T(8,128)(2,1)S(1)}, u32[]{:S(2)}, u32[]{:S(2)}) collective-permute-start(bf16[128,256]{1,0:T(8,128)(2,1)S(1)} %shard_map.113.refs_0_), channel_id=1, source_target_pairs={{0,2},{1,3},{2,0},{3,1},{4,6},{5,7},{6,4},{7,5},{8,10},{9,11},{10,... | collective-permute-start | bytes 196616 | tf_op jit(solution)/shard_map/ppermute | solution.py:413

commit v3 on v2

--- a/solution.py
+++ b/solution.py
@@ -196,14 +196,13 @@
     return a, b, (x - a - b).astype(BF16).astype(F32)
 
 
-def split_pool(pool_ref):
-    slots, _, cols = pool_ref.shape
+def split_pool(*pool_refs):
+    cols = pool_refs[0].shape[2]
     i = lax.broadcasted_iota(I32, (256, 256), 0)
     j = lax.broadcasted_iota(I32, (256, 256), 1)
     pick = jnp.where(j == 2 * (i % 128) + i // 128, 1.0, 0.0).astype(BF16)
     keys, values = [], []
-    for at in range(0, slots, 128):
-        both = pool_ref[at : at + 128].reshape(256, cols)
+    for both in [ref[at : at + 128].reshape(256, cols) for ref in pool_refs for at in range(0, ref.shape[0], 128)]:
         apart = jnp.dot(pick, both, preferred_element_type=F32)
         keys.append(apart[:128].astype(BF16))
         values.append(apart[128:].T.astype(BF16))
@@ -392,8 +391,7 @@
     code2 = lax.ppermute(code, "seq", xor("seq", 1))
     msgs = [msg] + [lax.ppermute(msg, "seq", xor("seq", k)) for k in groups[1:]]
 
-    w_own, *msgs = lax.optimization_barrier((w_out, *msgs))
-    w_far = lax.ppermute(w_own, "tp", xor("tp", 2))
+    w_far = lax.ppermute(w_out, "tp", xor("tp", 2))
 
     work = 4 * len(groups) * rows * slots * cols
     wide_rows = len(groups) * rows
@@ -403,12 +401,15 @@
         bias, pool, code, *msgs,
         flops=work,
     )
+    pool2, w_far = lax.optimization_barrier((pool2, w_far))
     merged = call(
-        second_kernel, [shape(cols + AUX, rows)] * len(groups), bias, pool2, code2, o1, lse1, *msgs, flops=work)
-    first, w_own, w_far, normed = lax.optimization_barrier((merged[0], w_own, w_far, normed))
+        second_kernel, [shape(cols + AUX, rows)] * len(groups), bias, pool2, code2, o1, lse1, *msgs, flops=work
+    )
+    first, normed = lax.optimization_barrier((merged[0], normed))
     key, value = call(own_kernel, [shape(cols, rows)] * 2, normed, w3, flops=4 * rows * width * cols)
+    back = [first] + [lax.ppermute(m, "seq", xor("seq", k)) for m, k in zip(merged[1:], groups[1:])]
+    w_own, w_far, *back = lax.optimization_barrier((w_out, w_far, *back))
     outs = [w_own, w_far] + [lax.ppermute(w, "tp", xor("tp", 1)) for w in (w_own, w_far)]
-    back = [first] + [lax.ppermute(m, "seq", xor("seq", k)) for m, k in zip(merged[1:], groups[1:])]
     attn = call(combine_kernel, shape(rows, cols), bias, msg, key, value, *back)
     attns = [attn] + [lax.ppermute(attn, "tp", xor("tp", k)) for k in (2, 1, 3)]
     return call(project_kernel, shape(rows, width), tok, *attns, *outs, flops=2 * rows * width * width)

time: 43.9 us -> 38.7 us (0.88)
  waiting for transfers between devices: 16.9 us -> 12.7 us
  starting transfers between devices: 17.5 us -> 16.6 us
    ppermute x1, waiting for transfers between devices: 3 us -> 0.01 us  [dense_body(): w_far = lax.ppermute(w_out, 'tp', xor('tp', 2))]
    ppermute x1, waiting for transfers between devices: 2.4 us -> 0.01 us  [dense_body(): code2 = lax.ppermute(code, 'seq', xor('seq', 1))]
    ppermute x1, starting transfers between devices: 1.66 us -> 2.97 us  [dense_body(): pool2 = lax.ppermute(pool, 'seq', xor('seq', 1))]
    ppermute x3, starting transfers between devices: 5.76 us -> 4.45 us  [dense_body(): msgs = [msg] + [lax.ppermute(msg, 'seq', xor('seq', k)) for k in groups[1:]]]
    ppermute x1, starting transfers between devices: 1.52 us -> 0.51 us  [dense_body(): code2 = lax.ppermute(code, 'seq', xor('seq', 1))]
    ppermute x3, waiting for transfers between devices: 3.6 us -> 4.27 us  [dense_body(): msgs = [msg] + [lax.ppermute(msg, 'seq', xor('seq', k)) for k in groups[1:]]]
    ppermute x3, waiting for transfers between devices: 4.15 us -> 4.79 us  [dense_body(): lax.ppermute(m, 'seq', xor('seq', k))]
  transfers between devices with their start and end apart: 14 -> 14, of which waited for: 8 -> 7; matrix products, arithmetic and copies ran while one was open for 0% -> 0% of each run, Pallas kernels for 13% -> 13%
where the time goes in v3:
time: 38.7 us; the launch traced here: 38.6 us
  starting transfers between devices  16.6 us (43%)
  waiting for transfers between devices  12.7 us (33%)
  Pallas kernels  8.52 us (22%)
  between operations  0.74 us (2%)
    pallas_call x6, Pallas kernels, call(): pl.pallas_call(kernel, out_shape=outs, scratch_shapes=scratch, in_specs=[...  8.52 us
    ppermute x3, waiting for transfers between devices, dense_body(): lax.ppermute(m, 'seq', xor('seq', k))  4.79 us
    ppermute x3, starting transfers between devices, dense_body(): msgs = [msg] + [lax.ppermute(msg, 'seq', xor('seq', k)) for k in groups[1:]]  4.45 us
    ppermute x3, starting transfers between devices, dense_body(): lax.ppermute(m, 'seq', xor('seq', k))  4.45 us
    ppermute x3, waiting for transfers between devices, dense_body(): msgs = [msg] + [lax.ppermute(msg, 'seq', xor('seq', k)) for k in groups[1:]]  4.27 us
    ppermute x3, waiting for transfers between devices, dense_body(): attns = [attn] + [lax.ppermute(attn, 'tp', xor('tp', k)) for k in (2, 1, 3)]  3.65 us
    ppermute x1, starting transfers between devices, dense_body(): pool2 = lax.ppermute(pool, 'seq', xor('seq', 1))  2.97 us
    ppermute x3, starting transfers between devices, dense_body(): attns = [attn] + [lax.ppermute(attn, 'tp', xor('tp', k)) for k in (2, 1, 3)]  2.21 us
  transfers between devices with their start and end apart: 14, of which 7 were waited for; matrix products, arithmetic and copies ran while one was open for 0% of the time, Pallas kernels for 13%

profile of v3, /device:TPU:0, one launch (start us, length us, event | category | flops | bytes accessed | tf_op | source)
XLA Modules:
  0.0 38.6 jit_solution(12675204469261222204)
XLA Ops:
  0.0 0.0 copy-start.1
  0.0 3.0 %collective-permute-start = (bf16[512,2,256]{2,1,0:T(2,128)(2,1)}, bf16[512,2,256]{2,1,0:T(2,128)(2,1)S(1)}, u32[]{:S(2)}, u32[]{:S(2)}) collective-permute-start(bf16[512,2,256]{2,1,0:T(2,128)(2,1)} %bitcast.7), channel_id=1, source_target_pairs={{0,4},{4,0},{8,12},{12,8},{16,20},{20,16},{24,28},{28,24},{1,5},{5... | collective-permute-start | bytes 1572872 | tf_op jit(solution)/shard_map/ppermute | solution.py:370
  3.0 1.5 %collective-permute-start.1 = (bf16[256,1024]{1,0:T(8,128)(2,1)}, bf16[256,1024]{1,0:T(8,128)(2,1)S(1)}, u32[]{:S(2)}, u32[]{:S(2)}) collective-permute-start(bf16[256,1024]{1,0:T(8,128)(2,1)} %refs_4_), channel_id=1, source_target_pairs={{0,2},{1,3},{2,0},{3,1},{4,6},{5,7},{6,4},{7,5},{8,10},{9,11},{10,... | collective-permute-start | bytes 1572872 | tf_op jit(solution)/shard_map/ppermute | solution.py:394
  5.1 0.0 copy-start.2
  5.1 0.0 copy-start
  5.1 1.8 %shard_map.109 = (bf16[272,128]{1,0:T(8,128)(2,1)S(1)}, bf16[128,1024]{1,0:T(8,128)(2,1)S(1)}, f32[32,128]{1,0:T(8,128)S(1)}, s32[4,128]{1,0:T(4,128)S(1)}, bf16[128,1024]{1,0:T(8,128)(2,1)S(1)}) custom-call(bf16[128,1024]{1,0:T(8,128)(2,1)} %tok_hbm.1, f32[1,1024]{1,0:T(1,128)} %bitcast.9, bf16[3,1024,256]{2,1,0:T(8,128)(2,1)} %bitcast.5, ...), custom_call_target="tpu_custom_call" | custom-call | flops 1 | bytes 1 | tf_op jit(solution)/shard_map/pallas_call | solution.py:137
  6.9 3.7 %collective-permute-start.5 = (bf16[272,128]{1,0:T(8,128)(2,1)S(1)}, bf16[272,128]{1,0:T(8,128)(2,1)S(1)}, u32[]{:S(2)}, u32[]{:S(2)}) collective-permute-start(bf16[272,128]{1,0:T(8,128)(2,1)S(1)} %get-tuple-element.30.refs_0_.q_ref), channel_id=1, source_target_pairs={{0,24},{4,28},{8,16},{12,20},{16,8},{20,12},{24,0},{28,4},{1,25},{... | collective-permute-start | bytes 208904 | tf_op jit(solution)/shard_map/ppermute | solution.py:392
  10.6 0.0 collective-permute-start.4
  10.6 0.8 %collective-permute-start.3 = (bf16[272,128]{1,0:T(8,128)(2,1)S(1)}, bf16[272,128]{1,0:T(8,128)(2,1)S(1)}, u32[]{:S(2)}, u32[]{:S(2)}) collective-permute-start(bf16[272,128]{1,0:T(8,128)(2,1)S(1)} %get-tuple-element.30.refs_0_.q_ref), channel_id=1, source_target_pairs={{0,8},{4,12},{8,0},{12,4},{16,24},{20,28},{24,16},{28,20},{1,9},{5... | collective-permute-start | bytes 208904 | tf_op jit(solution)/shard_map/ppermute | solution.py:392
  11.4 2.3 %collective-permute-done.5.refs_3_ = bf16[272,128]{1,0:T(8,128)(2,1)S(1)} collective-permute-done((bf16[272,128]{1,0:T(8,128)(2,1)S(1)}, bf16[272,128]{1,0:T(8,128)(2,1)S(1)}, u32[]{:S(2)}, u32[]{:S(2)}) %collective-permute-start.5) | collective-permute-done | bytes 69664 | tf_op jit(solution)/shard_map/ppermute | solution.py:392
  13.7 0.5 %collective-permute-start.2 = (s32[4,128]{1,0:T(4,128)S(1)}, s32[4,128]{1,0:T(4,128)S(1)}, u32[]{:S(2)}, u32[]{:S(2)}) collective-permute-start(s32[4,128]{1,0:T(4,128)S(1)} %get-tuple-element.32.code_ref), channel_id=1, source_target_pairs={{0,4},{4,0},{8,12},{12,8},{16,20},{20,16},{24,28},{28,24},{1,5},{5... | collective-permute-start | bytes 6152 | tf_op jit(solution)/shard_map/ppermute | solution.py:391
  14.2 1.9 %collective-permute-done.4.refs_2_ = bf16[272,128]{1,0:T(8,128)(2,1)S(1)} collective-permute-done((bf16[272,128]{1,0:T(8,128)(2,1)S(1)}, bf16[272,128]{1,0:T(8,128)(2,1)S(1)}, u32[]{:S(2)}, u32[]{:S(2)}) %collective-permute-start.4) | collective-permute-done | bytes 69664 | tf_op jit(solution)/shard_map/ppermute | solution.py:392
  16.1 0.1 collective-permute-done.3.refs_1_
  16.2 0.0 copy-done.1
  16.2 2.5 %shard_map.110 = (bf16[256,512]{1,0:T(8,128)(2,1)S(1)}, f32[4,512]{1,0:T(4,128)S(1)}) custom-call(f32[32,128]{1,0:T(8,128)S(1)} %get-tuple-element.29.rows_ref, bf16[512,2,256]{2,1,0:T(2,128)(2,1)S(1)} %bitcast.8, s32[4,128]{1,0:T(4,128)S(1)} %get-tuple-element.32.code_ref, bf16[272,128]{1,0:T(8,128)(2,1)S(1)} %get-tuple-element.30.refs_0_.q_ref, ...), custom_call_target="tpu_custom_call" | custom-call | flops 1 | bytes 1 | tf_op jit(solution)/shard_map/pallas_call | solution.py:137
  18.6 0.0 collective-permute-done.pool_ref
  18.6 0.0 collective-permute-done.1.refs_5_
  18.7 0.0 collective-permute-done.2.code_ref
  18.7 2.5 %shard_map.111 = (bf16[272,128]{1,0:T(8,128)(2,1)S(1)}, bf16[272,128]{1,0:T(8,128)(2,1)S(1)}, bf16[272,128]{1,0:T(8,128)(2,1)S(1)}, bf16[272,128]{1,0:T(8,128)(2,1)S(1)}) custom-call(f32[32,128]{1,0:T(8,128)S(1)} %get-tuple-element.29.rows_ref, bf16[512,2,256]{2,1,0:T(2,128)(2,1)S(1)} %collective-permute-done.pool_ref, ...), custom_call_target="tpu_custom_call" | custom-call | flops 1 | bytes 1 | tf_op jit(solution)/shard_map/pallas_call | solution.py:137
  21.2 0.9 %collective-permute-start.6 = (bf16[272,128]{1,0:T(8,128)(2,1)S(1)}, bf16[272,128]{1,0:T(8,128)(2,1)S(1)}, u32[]{:S(2)}, u32[]{:S(2)}) collective-permute-start(bf16[272,128]{1,0:T(8,128)(2,1)S(1)} %get-tuple-element.42), channel_id=1, source_target_pairs={{0,8},{4,12},{8,0},{12,4},{16,24},{20,28},{24,16},{28,20},{1,9},{5... | collective-permute-start | bytes 208904 | tf_op jit(solution)/shard_map/ppermute | solution.py:410
  22.1 2.2 %collective-permute-start.7 = (bf16[272,128]{1,0:T(8,128)(2,1)S(1)}, bf16[272,128]{1,0:T(8,128)(2,1)S(1)}, u32[]{:S(2)}, u32[]{:S(2)}) collective-permute-start(bf16[272,128]{1,0:T(8,128)(2,1)S(1)} %get-tuple-element.43), channel_id=1, source_target_pairs={{0,16},{4,20},{8,24},{12,28},{16,0},{20,4},{24,8},{28,12},{1,17},{... | collective-permute-start | bytes 208904 | tf_op jit(solution)/shard_map/ppermute | solution.py:410
  24.3 1.3 %collective-permute-start.8 = (bf16[272,128]{1,0:T(8,128)(2,1)S(1)}, bf16[272,128]{1,0:T(8,128)(2,1)S(1)}, u32[]{:S(2)}, u32[]{:S(2)}) collective-permute-start(bf16[272,128]{1,0:T(8,128)(2,1)S(1)} %get-tuple-element.44), channel_id=1, source_target_pairs={{0,24},{4,28},{8,16},{12,20},{16,8},{20,12},{24,0},{28,4},{1,25},{... | collective-permute-start | bytes 208904 | tf_op jit(solution)/shard_map/ppermute | solution.py:410
  25.6 0.0 collective-permute-done.6.refs_1_
  25.6 3.0 %collective-permute-done.7.refs_2_ = bf16[272,128]{1,0:T(8,128)(2,1)S(1)} collective-permute-done((bf16[272,128]{1,0:T(8,128)(2,1)S(1)}, bf16[272,128]{1,0:T(8,128)(2,1)S(1)}, u32[]{:S(2)}, u32[]{:S(2)}) %collective-permute-start.7) | collective-permute-done | bytes 69664 | tf_op jit(solution)/shard_map/ppermute | solution.py:410
  28.6 1.8 %collective-permute-done.8.refs_3_ = bf16[272,128]{1,0:T(8,128)(2,1)S(1)} collective-permute-done((bf16[272,128]{1,0:T(8,128)(2,1)S(1)}, bf16[272,128]{1,0:T(8,128)(2,1)S(1)}, u32[]{:S(2)}, u32[]{:S(2)}) %collective-permute-start.8) | collective-permute-done | bytes 69664 | tf_op jit(solution)/shard_map/ppermute | solution.py:410
  30.4 0.0 copy-done.2
  30.4 0.0 collective-permute-start.12
  30.4 0.5 %collective-permute-start.13 = (bf16[256,1024]{1,0:T(8,128)(2,1)S(1)}, bf16[256,1024]{1,0:T(8,128)(2,1)S(1)}, u32[]{:S(2)}, u32[]{:S(2)}) collective-permute-start(bf16[256,1024]{1,0:T(8,128)(2,1)S(1)} %collective-permute-done.1.refs_5_), channel_id=1, source_target_pairs={{0,1},{1,0},{2,3},{3,2},{4,5},{5,4},{6,7},{7,6},{8,9},{9,8},{10,11... | collective-permute-start | bytes 1572872 | tf_op jit(solution)/shard_map/ppermute | solution.py:412
  30.9 0.0 copy-done
  30.9 0.4 shard_map.112
  31.3 0.2 shard_map.113.refs_0_
  31.5 0.2 collective-permute-start.11
  31.8 0.5 %collective-permute-start.10 = (bf16[128,256]{1,0:T(8,128)(2,1)S(1)}, bf16[128,256]{1,0:T(8,128)(2,1)S(1)}, u32[]{:S(2)}, u32[]{:S(2)}) collective-permute-start(bf16[128,256]{1,0:T(8,128)(2,1)S(1)} %shard_map.113.refs_0_), channel_id=1, source_target_pairs={{0,1},{1,0},{2,3},{3,2},{4,5},{5,4},{6,7},{7,6},{8,9},{9,8},{10,11... | collective-permute-start | bytes 196616 | tf_op jit(solution)/shard_map/ppermute | solution.py:414
  32.3 1.5 %collective-permute-start.9 = (bf16[128,256]{1,0:T(8,128)(2,1)S(1)}, bf16[128,256]{1,0:T(8,128)(2,1)S(1)}, u32[]{:S(2)}, u32[]{:S(2)}) collective-permute-start(bf16[128,256]{1,0:T(8,128)(2,1)S(1)} %shard_map.113.refs_0_), channel_id=1, source_target_pairs={{0,2},{1,3},{2,0},{3,1},{4,6},{5,7},{6,4},{7,5},{8,10},{9,11},{10,... | collective-permute-start | bytes 196616 | tf_op jit(solution)/shard_map/ppermute | solution.py:414
  33.8 2.1 %collective-permute-done.11.refs_3_ = bf16[128,256]{1,0:T(8,128)(2,1)S(1)} collective-permute-done((bf16[128,256]{1,0:T(8,128)(2,1)S(1)}, bf16[128,256]{1,0:T(8,128)(2,1)S(1)}, u32[]{:S(2)}, u32[]{:S(2)}) %collective-permute-start.11) | collective-permute-done | bytes 65568 | tf_op jit(solution)/shard_map/ppermute | solution.py:414
  35.8 0.0 collective-permute-done.10.refs_2_
  35.8 1.6 %collective-permute-done.9.refs_1_ = bf16[128,256]{1,0:T(8,128)(2,1)S(1)} collective-permute-done((bf16[128,256]{1,0:T(8,128)(2,1)S(1)}, bf16[128,256]{1,0:T(8,128)(2,1)S(1)}, u32[]{:S(2)}, u32[]{:S(2)}) %collective-permute-start.9) | collective-permute-done | bytes 65568 | tf_op jit(solution)/shard_map/ppermute | solution.py:414
  37.4 0.0 collective-permute-done.12.refs_6_
  37.4 0.0 collective-permute-done.13.refs_7_
  37.4 1.2 %shard_map.114 = bf16[128,1024]{1,0:T(8,128)(2,1)} custom-call(bf16[128,1024]{1,0:T(8,128)(2,1)S(1)} %get-tuple-element.28.tok_ref, bf16[128,256]{1,0:T(8,128)(2,1)S(1)} %shard_map.113.refs_0_, bf16[128,256]{1,0:T(8,128)(2,1)S(1)} %collective-permute-done.9.refs_1_, bf16[128,256]{1,0:T(8,128)(2,1)S(1)} %collective-permute-done.10.refs_2_, ...), custom_call_target="tpu_custom_call" | custom-call | flops 1 | bytes 1 | tf_op jit(solution)/shard_map/pallas_call | solution.py:137
Async XLA Ops:
  0.0 16.2 %copy-start.1 = (bf16[4,128,2,256]{3,2,1,0:T(2,128)(2,1)S(1)}, bf16[4,128,2,256]{3,2,1,0:T(2,128)(2,1)}, u32[]{:S(2)}) copy-start(bf16[4,128,2,256]{3,2,1,0:T(2,128)(2,1)} %param.16) | copy-start | bytes 1572868
  0.0 18.6 %collective-permute-start = (bf16[512,2,256]{2,1,0:T(2,128)(2,1)}, bf16[512,2,256]{2,1,0:T(2,128)(2,1)S(1)}, u32[]{:S(2)}, u32[]{:S(2)}) collective-permute-start(bf16[512,2,256]{2,1,0:T(2,128)(2,1)} %bitcast.7), channel_id=1, source_target_pairs={{0,4},{4,0},{8,12},{12,8},{16,20},{20,16},{24,28},{28,24},{1,5},{5... | collective-permute-start | bytes 1572872 | tf_op jit(solution)/shard_map/ppermute | solution.py:370
  3.0 15.7 %collective-permute-start.1 = (bf16[256,1024]{1,0:T(8,128)(2,1)}, bf16[256,1024]{1,0:T(8,128)(2,1)S(1)}, u32[]{:S(2)}, u32[]{:S(2)}) collective-permute-start(bf16[256,1024]{1,0:T(8,128)(2,1)} %refs_4_), channel_id=1, source_target_pairs={{0,2},{1,3},{2,0},{3,1},{4,6},{5,7},{6,4},{7,5},{8,10},{9,11},{10,... | collective-permute-start | bytes 1572872 | tf_op jit(solution)/shard_map/ppermute | solution.py:394
  5.1 25.3 %copy-start.2 = (bf16[256,1024]{1,0:T(8,128)(2,1)S(1)}, bf16[256,1024]{1,0:T(8,128)(2,1)}, u32[]{:S(2)}) copy-start(bf16[256,1024]{1,0:T(8,128)(2,1)} %refs_4_) | copy-start | bytes 1572868
  5.1 25.8 %copy-start = (bf16[1024,3,256]{2,0,1:T(8,128)(2,1)S(1)}, bf16[1024,3,256]{2,0,1:T(8,128)(2,1)}, u32[]{:S(2)}) copy-start(bf16[1024,3,256]{2,0,1:T(8,128)(2,1)} %param.13) | copy-start | bytes 4718596
  6.9 6.8 %collective-permute-start.5 = (bf16[272,128]{1,0:T(8,128)(2,1)S(1)}, bf16[272,128]{1,0:T(8,128)(2,1)S(1)}, u32[]{:S(2)}, u32[]{:S(2)}) collective-permute-start(bf16[272,128]{1,0:T(8,128)(2,1)S(1)} %get-tuple-element.30.refs_0_.q_ref), channel_id=1, source_target_pairs={{0,24},{4,28},{8,16},{12,20},{16,8},{20,12},{24,0},{28,4},{1,25},{... | collective-permute-start | bytes 208904 | tf_op jit(solution)/shard_map/ppermute | solution.py:392
  10.6 5.5 %collective-permute-start.4 = (bf16[272,128]{1,0:T(8,128)(2,1)S(1)}, bf16[272,128]{1,0:T(8,128)(2,1)S(1)}, u32[]{:S(2)}, u32[]{:S(2)}) collective-permute-start(bf16[272,128]{1,0:T(8,128)(2,1)S(1)} %get-tuple-element.30.refs_0_.q_ref), channel_id=1, source_target_pairs={{0,16},{4,20},{8,24},{12,28},{16,0},{20,4},{24,8},{28,12},{1,17},{... | collective-permute-start | bytes 208904 | tf_op jit(solution)/shard_map/ppermute | solution.py:392
  10.6 5.6 %collective-permute-start.3 = (bf16[272,128]{1,0:T(8,128)(2,1)S(1)}, bf16[272,128]{1,0:T(8,128)(2,1)S(1)}, u32[]{:S(2)}, u32[]{:S(2)}) collective-permute-start(bf16[272,128]{1,0:T(8,128)(2,1)S(1)} %get-tuple-element.30.refs_0_.q_ref), channel_id=1, source_target_pairs={{0,8},{4,12},{8,0},{12,4},{16,24},{20,28},{24,16},{28,20},{1,9},{5... | collective-permute-start | bytes 208904 | tf_op jit(solution)/shard_map/ppermute | solution.py:392
  13.7 5.0 %collective-permute-start.2 = (s32[4,128]{1,0:T(4,128)S(1)}, s32[4,128]{1,0:T(4,128)S(1)}, u32[]{:S(2)}, u32[]{:S(2)}) collective-permute-start(s32[4,128]{1,0:T(4,128)S(1)} %get-tuple-element.32.code_ref), channel_id=1, source_target_pairs={{0,4},{4,0},{8,12},{12,8},{16,20},{20,16},{24,28},{28,24},{1,5},{5... | collective-permute-start | bytes 6152 | tf_op jit(solution)/shard_map/ppermute | solution.py:391
  21.2 4.5 %collective-permute-start.6 = (bf16[272,128]{1,0:T(8,128)(2,1)S(1)}, bf16[272,128]{1,0:T(8,128)(2,1)S(1)}, u32[]{:S(2)}, u32[]{:S(2)}) collective-permute-start(bf16[272,128]{1,0:T(8,128)(2,1)S(1)} %get-tuple-element.42), channel_id=1, source_target_pairs={{0,8},{4,12},{8,0},{12,4},{16,24},{20,28},{24,16},{28,20},{1,9},{5... | collective-permute-start | bytes 208904 | tf_op jit(solution)/shard_map/ppermute | solution.py:410
  22.1 6.5 %collective-permute-start.7 = (bf16[272,128]{1,0:T(8,128)(2,1)S(1)}, bf16[272,128]{1,0:T(8,128)(2,1)S(1)}, u32[]{:S(2)}, u32[]{:S(2)}) collective-permute-start(bf16[272,128]{1,0:T(8,128)(2,1)S(1)} %get-tuple-element.43), channel_id=1, source_target_pairs={{0,16},{4,20},{8,24},{12,28},{16,0},{20,4},{24,8},{28,12},{1,17},{... | collective-permute-start | bytes 208904 | tf_op jit(solution)/shard_map/ppermute | solution.py:410
  24.3 6.1 %collective-permute-start.8 = (bf16[272,128]{1,0:T(8,128)(2,1)S(1)}, bf16[272,128]{1,0:T(8,128)(2,1)S(1)}, u32[]{:S(2)}, u32[]{:S(2)}) collective-permute-start(bf16[272,128]{1,0:T(8,128)(2,1)S(1)} %get-tuple-element.44), channel_id=1, source_target_pairs={{0,24},{4,28},{8,16},{12,20},{16,8},{20,12},{24,0},{28,4},{1,25},{... | collective-permute-start | bytes 208904 | tf_op jit(solution)/shard_map/ppermute | solution.py:410
  30.4 7.0 %collective-permute-start.12 = (bf16[256,1024]{1,0:T(8,128)(2,1)S(1)}, bf16[256,1024]{1,0:T(8,128)(2,1)S(1)}, u32[]{:S(2)}, u32[]{:S(2)}) collective-permute-start(bf16[256,1024]{1,0:T(8,128)(2,1)S(1)} %copy-done.2), channel_id=1, source_target_pairs={{0,1},{1,0},{2,3},{3,2},{4,5},{5,4},{6,7},{7,6},{8,9},{9,8},{10,11... | collective-permute-start | bytes 1572872 | tf_op jit(solution)/shard_map/ppermute | solution.py:412
  30.4 7.0 %collective-permute-start.13 = (bf16[256,1024]{1,0:T(8,128)(2,1)S(1)}, bf16[256,1024]{1,0:T(8,128)(2,1)S(1)}, u32[]{:S(2)}, u32[]{:S(2)}) collective-permute-start(bf16[256,1024]{1,0:T(8,128)(2,1)S(1)} %collective-permute-done.1.refs_5_), channel_id=1, source_target_pairs={{0,1},{1,0},{2,3},{3,2},{4,5},{5,4},{6,7},{7,6},{8,9},{9,8},{10,11... | collective-permute-start | bytes 1572872 | tf_op jit(solution)/shard_map/ppermute | solution.py:412
  31.5 4.3 %collective-permute-start.11 = (bf16[128,256]{1,0:T(8,128)(2,1)S(1)}, bf16[128,256]{1,0:T(8,128)(2,1)S(1)}, u32[]{:S(2)}, u32[]{:S(2)}) collective-permute-start(bf16[128,256]{1,0:T(8,128)(2,1)S(1)} %shard_map.113.refs_0_), channel_id=1, source_target_pairs={{0,3},{1,2},{2,1},{3,0},{4,7},{5,6},{6,5},{7,4},{8,11},{9,10},{10,... | collective-permute-start | bytes 196616 | tf_op jit(solution)/shard_map/ppermute | solution.py:414
  31.8 4.1 %collective-permute-start.10 = (bf16[128,256]{1,0:T(8,128)(2,1)S(1)}, bf16[128,256]{1,0:T(8,128)(2,1)S(1)}, u32[]{:S(2)}, u32[]{:S(2)}) collective-permute-start(bf16[128,256]{1,0:T(8,128)(2,1)S(1)} %shard_map.113.refs_0_), channel_id=1, source_target_pairs={{0,1},{1,0},{2,3},{3,2},{4,5},{5,4},{6,7},{7,6},{8,9},{9,8},{10,11... | collective-permute-start | bytes 196616 | tf_op jit(solution)/shard_map/ppermute | solution.py:414
  32.3 5.1 %collective-permute-start.9 = (bf16[128,256]{1,0:T(8,128)(2,1)S(1)}, bf16[128,256]{1,0:T(8,128)(2,1)S(1)}, u32[]{:S(2)}, u32[]{:S(2)}) collective-permute-start(bf16[128,256]{1,0:T(8,128)(2,1)S(1)} %shard_map.113.refs_0_), channel_id=1, source_target_pairs={{0,2},{1,3},{2,0},{3,1},{4,6},{5,7},{6,4},{7,5},{8,10},{9,11},{10,... | collective-permute-start | bytes 196616 | tf_op jit(solution)/shard_map/ppermute | solution.py:414

commit v4 on v3

--- a/solution.py
+++ b/solution.py
@@ -1,3 +1,5 @@
+import functools
+
 import jax
 import jax.numpy as jnp
 from jax import lax
@@ -156,16 +158,8 @@
     return copies
 
 
-def query_kernel(
-    tok_hbm, gain_hbm, w_hbm, variate_hbm, path_hbm, bias_hbm, slot_hbm, table_hbm, len_ref,
-    msg_ref, normed_ref, rows_ref, code_ref, tok_ref,
-    gain_ref, w_ref, variate_ref, path_ref, bias_ref, slot_ref, table_ref, sems,
-):
-    copies = fetch(
-        sems, (tok_hbm, tok_ref), (w_hbm.at[0], w_ref), (gain_hbm, gain_ref), (variate_hbm, variate_ref), (path_hbm, path_ref),
-        (bias_hbm, bias_ref), (slot_hbm, slot_ref), (table_hbm, table_ref),
-    )
-    for copy in copies[2:]:
+def code_kernel(len_ref, slot_hbm, table_hbm, code_ref, slot_ref, table_ref, sems):
+    for copy in fetch(sems, (slot_hbm, slot_ref), (table_hbm, table_ref)):
         copy.wait()
     pages, page = slot_ref.shape
     length = len_ref[0]
@@ -173,6 +167,19 @@
     for p in range(pages):
         place = sum(jnp.where(table_ref[0, i] == p, i, 0) for i in range(pages))
         code_ref[p : p + 1, :] = jnp.where(place * page + offset < length, slot_ref[p : p + 1, :], 8)
+
+
+def query_kernel(
+    tok_hbm, gain_hbm, w_hbm, variate_hbm, path_hbm, bias_hbm, pool_hbm,
+    msg_ref, normed_ref, rows_ref, tok_ref, pool_ref,
+    gain_ref, w_ref, variate_ref, path_ref, bias_ref, sems,
+):
+    copies = fetch(
+        sems, (tok_hbm, tok_ref), (w_hbm.at[0], w_ref), (gain_hbm, gain_ref), (variate_hbm, variate_ref), (path_hbm, path_ref),
+        (bias_hbm, bias_ref), (pool_hbm, pool_ref),
+    )
+    for copy in copies[2:6]:
+        copy.wait()
     rows, cols = tok_ref.shape[0], w_ref.shape[1]
     for head in range(cols // HD):
         same = jnp.full((1, rows), bias_ref[1, head], F32)
@@ -188,6 +195,7 @@
     copies[1].wait()
     q = jnp.dot(normed, w_ref[...], preferred_element_type=F32).astype(BF16)
     msg_ref[:cols, :] = (q.astype(F32) * HD ** (-0.5)).T.astype(BF16)
+    copies[6].wait()
 
 
 def split3(x):
@@ -260,16 +268,17 @@
     return q, aux
 
 
-def own_kernel(normed_ref, w_ref, k_ref, v_ref):
+def own_kernel(normed_ref, w_ref, pool_ref, code_ref, k_ref, v_ref, keys_ref, values_ref, terms_ref):
     for i, own_ref in ((1, k_ref), (2, v_ref)):
         own = jnp.dot(normed_ref[...], w_ref[i], preferred_element_type=F32).astype(BF16)
         own_ref[...] = own.astype(F32).T.astype(BF16)
-
-
-def first_kernel(rows_ref, pool_ref, code_ref, *refs):
+    keys_ref[...], values_ref[...] = split_pool(pool_ref)
+    terms_ref[...] = slot_terms(code_ref)
+
+
+def first_kernel(rows_ref, keys_ref, values_ref, terms_ref, *refs):
     msgs, (o_ref, lse_ref) = refs[:-2], refs[-2:]
-    keys, values_t = split_pool(pool_ref)
-    terms = slot_terms(code_ref)
+    keys, values_t, terms = keys_ref[...], values_ref[...], terms_ref[...]
     cols = keys.shape[1]
     q, aux = gather_rows(msgs, cols)
     for head in range(cols // HD):
@@ -332,14 +341,13 @@
     attn_ref[...] = jnp.concatenate(done, axis=0).T.astype(BF16)
 
 
-def project_kernel(tok_ref, *refs):
-    out_ref = refs[-1]
-    half = (len(refs) - 1) // 2
-    acc = None
-    for attn, w in zip(refs[:half], refs[half : 2 * half]):
-        term = jnp.dot(attn[...], w[...], preferred_element_type=F32)
-        acc = term if acc is None else acc + term
-    out_ref[...] = (tok_ref[...].astype(F32) + acc).astype(BF16)
+def project_kernel(base_ref, *refs):
+    *pairs, out_ref = refs
+    half = len(pairs) // 2
+    total = base_ref[...].astype(F32)
+    for attn, w in zip(pairs[:half], pairs[half:]):
+        total = total + jnp.dot(attn[...], w[...], preferred_element_type=F32)
+    out_ref[...] = total.astype(out_ref.dtype)
 
 
 def xor(axis, k):
@@ -364,55 +372,54 @@
     heads = cols // HD
     pages, page = key_variate.shape
     slots = pages * page
-    groups = [2 * k for k in range(max(1, lax.axis_size("seq") // 2))]
+    groups = [0] + [2 * k for k in reversed(range(1, lax.axis_size("seq") // 2))]
 
     pool = kv_pool.reshape(slots, 2, cols)
     pool2 = lax.ppermute(pool, "seq", xor("seq", 1))
+    w_far = lax.ppermute(w_out, "tp", xor("tp", 2))
 
     w3 = w_qkv.transpose(1, 0, 2)
-    smem = lambda *dims: pltpu.SMEM(dims, I32)
-    msg, normed, bias, code, tok = call(
+    msg, normed, bias, tok, pool = call(
         query_kernel,
         [
-            shape(cols + AUX, rows),
-            shape(rows, width),
-            shape(8 * heads, rows, dtype=F32),
-            shape(pages, page, dtype=I32),
-            shape(rows, width),
+            shape(cols + AUX, rows), shape(rows, width), shape(8 * heads, rows, dtype=F32), shape(rows, width), shape(slots, 2, cols),
         ],
-        tokens, norm_gain[None], w3, query_variate[None], path_nodes.T, head_bias, key_variate, page_table, node_len,
-        flops=2 * rows * width * cols,
-        away=range(8),
+        tokens, norm_gain[None], w3, query_variate[None], path_nodes.T, head_bias, pool,
+        away=range(7),
         scratch=[
             pltpu.VMEM((1, width), F32), pltpu.VMEM((width, cols), BF16), pltpu.VMEM((1, rows), I32), pltpu.VMEM((3, rows), I32),
-            pltpu.VMEM((2, heads), F32), pltpu.VMEM((pages, page), I32), smem(1, pages), pltpu.SemaphoreType.DMA((8,)),
+            pltpu.VMEM((2, heads), F32), pltpu.SemaphoreType.DMA((7,)),
         ],
     )
+    msgs = [msg] + [lax.ppermute(msg, "seq", xor("seq", k)) for k in groups[1:]]
+    count = len(msgs)
+
+    node_len, normed = lax.optimization_barrier((node_len, normed))
+    code = call(
+        code_kernel, shape(pages, page, dtype=I32), node_len, key_variate, page_table,
+        away=(1, 2),
+        scratch=[pltpu.VMEM((pages, page), I32), pltpu.SMEM((1, pages), I32), pltpu.SemaphoreType.DMA((2,))],
+    )
     code2 = lax.ppermute(code, "seq", xor("seq", 1))
-    msgs = [msg] + [lax.ppermute(msg, "seq", xor("seq", k)) for k in groups[1:]]
-
-    w_far = lax.ppermute(w_out, "tp", xor("tp", 2))
-
-    work = 4 * len(groups) * rows * slots * cols
-    wide_rows = len(groups) * rows
+    key, value, keys, values_t, terms = call(
+        own_kernel,
+        [shape(cols, rows), shape(cols, rows), shape(slots, cols), shape(cols, slots), shape(slots, 128)],
+        normed, w3, pool, code,
+    )
+
+    wide_rows = count * rows
     o1, lse1 = call(
-        first_kernel,
-        [shape(cols, wide_rows), shape(heads, wide_rows, dtype=F32)],
-        bias, pool, code, *msgs,
-        flops=work,
+        first_kernel, [shape(cols, wide_rows), shape(heads, wide_rows, dtype=F32)], bias, keys, values_t, terms, *msgs
     )
     pool2, w_far = lax.optimization_barrier((pool2, w_far))
-    merged = call(
-        second_kernel, [shape(cols + AUX, rows)] * len(groups), bias, pool2, code2, o1, lse1, *msgs, flops=work
-    )
-    first, normed = lax.optimization_barrier((merged[0], normed))
-    key, value = call(own_kernel, [shape(cols, rows)] * 2, normed, w3, flops=4 * rows * width * cols)
-    back = [first] + [lax.ppermute(m, "seq", xor("seq", k)) for m, k in zip(merged[1:], groups[1:])]
+    merged = call(second_kernel, [shape(cols + AUX, rows)] * count, bias, pool2, code2, o1, lse1, *msgs)
+    back = [merged[0]] + [lax.ppermute(m, "seq", xor("seq", k)) for m, k in zip(merged[1:], groups[1:])]
     w_own, w_far, *back = lax.optimization_barrier((w_out, w_far, *back))
-    outs = [w_own, w_far] + [lax.ppermute(w, "tp", xor("tp", 1)) for w in (w_own, w_far)]
+    w_near, w_last = (lax.ppermute(w, "tp", xor("tp", 1)) for w in (w_own, w_far))
     attn = call(combine_kernel, shape(rows, cols), bias, msg, key, value, *back)
-    attns = [attn] + [lax.ppermute(attn, "tp", xor("tp", k)) for k in (2, 1, 3)]
-    return call(project_kernel, shape(rows, width), tok, *attns, *outs, flops=2 * rows * width * width)
+    x_near, x_far, x_last = (lax.ppermute(attn, "tp", xor("tp", k)) for k in (1, 2, 3))
+    total = call(project_kernel, shape(rows, width, dtype=F32), tok, attn, x_near, w_own, w_near)
+    return call(project_kernel, shape(rows, width), total, x_far, x_last, w_far, w_last)
 
 
 def solution(mesh):

time: 38.7 us -> 36.5 us (0.943)
  waiting for transfers between devices: 12.7 us -> 9.93 us
  Pallas kernels: 8.52 us -> 9.32 us
    ppermute x3, waiting for transfers between devices: 4.27 us -> 2.11 us  [dense_body(): msgs = [msg] + [lax.ppermute(msg, 'seq', xor('seq', k)) for k in groups[1:]]]
    pallas_call x6 -> x8, Pallas kernels: 8.52 us -> 9.32 us  [call(): pl.pallas_call(kernel, out_shape=outs, scratch_shapes=scratch, in_specs=[...]
  transfers between devices with their start and end apart: 14 -> 14, of which waited for: 7 -> 8; matrix products, arithmetic and copies ran while one was open for 0% -> 0% of each run, Pallas kernels for 13% -> 16%
where the time goes in v4:
time: 36.5 us; the launch traced here: 36.3 us
  starting transfers between devices  16.3 us (45%)
  waiting for transfers between devices  9.93 us (27%)
  Pallas kernels  9.32 us (26%)
  between operations  0.75 us (2%)
    pallas_call x8, Pallas kernels, call(): pl.pallas_call(kernel, out_shape=outs, scratch_shapes=scratch, in_specs=[...  9.32 us
    ppermute x3, waiting for transfers between devices, dense_body(): lax.ppermute(m, 'seq', xor('seq', k))  4.53 us
    ppermute x3, starting transfers between devices, dense_body(): lax.ppermute(m, 'seq', xor('seq', k))  4.45 us
    ppermute x3, starting transfers between devices, dense_body(): msgs = [msg] + [lax.ppermute(msg, 'seq', xor('seq', k)) for k in groups[1:]]  4.45 us
    ppermute x3, waiting for transfers between devices, dense_body(): lax.ppermute(attn, 'tp', xor('tp', k))  3.27 us
    ppermute x1, starting transfers between devices, dense_body(): pool2 = lax.ppermute(pool, 'seq', xor('seq', 1))  2.97 us
    ppermute x3, waiting for transfers between devices, dense_body(): msgs = [msg] + [lax.ppermute(msg, 'seq', xor('seq', k)) for k in groups[1:]]  2.11 us
    ppermute x3, starting transfers between devices, dense_body(): lax.ppermute(attn, 'tp', xor('tp', k))  1.94 us
  transfers between devices with their start and end apart: 14, of which 8 were waited for; matrix products, arithmetic and copies ran while one was open for 0% of the time, Pallas kernels for 16%

profile of v4, /device:TPU:0, one launch (start us, length us, event | category | flops | bytes accessed | tf_op | source)
XLA Modules:
  0.0 36.3 jit_solution(14448104791273412525)
XLA Ops:
  0.0 0.0 copy-start
  0.0 3.0 %collective-permute-start = (bf16[512,2,256]{2,1,0:T(2,128)(2,1)}, bf16[512,2,256]{2,1,0:T(2,128)(2,1)S(1)}, u32[]{:S(2)}, u32[]{:S(2)}) collective-permute-start(bf16[512,2,256]{2,1,0:T(2,128)(2,1)} %bitcast.7), channel_id=1, source_target_pairs={{0,4},{4,0},{8,12},{12,8},{16,20},{20,16},{24,28},{28,24},{1,5},{5... | collective-permute-start | bytes 1572872 | tf_op jit(solution)/shard_map/ppermute | solution.py:378
  3.0 1.5 %collective-permute-start.1 = (bf16[256,1024]{1,0:T(8,128)(2,1)}, bf16[256,1024]{1,0:T(8,128)(2,1)S(1)}, u32[]{:S(2)}, u32[]{:S(2)}) collective-permute-start(bf16[256,1024]{1,0:T(8,128)(2,1)} %refs_2_), channel_id=1, source_target_pairs={{0,2},{1,3},{2,0},{3,1},{4,6},{5,7},{6,4},{7,5},{8,10},{9,11},{10,... | collective-permute-start | bytes 1572872 | tf_op jit(solution)/shard_map/ppermute | solution.py:379
  4.5 1.6 %shard_map.109 = (bf16[272,128]{1,0:T(8,128)(2,1)S(1)}, bf16[128,1024]{1,0:T(8,128)(2,1)S(1)}, f32[32,128]{1,0:T(8,128)S(1)}, bf16[128,1024]{1,0:T(8,128)(2,1)S(1)}, bf16[512,2,256]{2,1,0:T(2,128)(2,1)S(1)}) custom-call(bf16[128,1024]{1,0:T(8,128)(2,1)} %tok_hbm.1, f32[1,1024]{1,0:T(1,128)} %bitcast.9, bf16[3,1024,256]{2,1,0:T(8,128)(2,1)} %bitcast.5, ...), custom_call_target="tpu_custom_call" | custom-call | flops 1 | bytes 1 | tf_op jit(solution)/shard_map/pallas_call | solution.py:139
  6.1 3.7 %collective-permute-start.3 = (bf16[272,128]{1,0:T(8,128)(2,1)S(1)}, bf16[272,128]{1,0:T(8,128)(2,1)S(1)}, u32[]{:S(2)}, u32[]{:S(2)}) collective-permute-start(bf16[272,128]{1,0:T(8,128)(2,1)S(1)} %get-tuple-element.33.refs_0_.q_ref), channel_id=1, source_target_pairs={{0,24},{4,28},{8,16},{12,20},{16,8},{20,12},{24,0},{28,4},{1,25},{... | collective-permute-start | bytes 208904 | tf_op jit(solution)/shard_map/ppermute | solution.py:394
  9.7 0.0 collective-permute-start.4
  9.7 0.8 %collective-permute-start.5 = (bf16[272,128]{1,0:T(8,128)(2,1)S(1)}, bf16[272,128]{1,0:T(8,128)(2,1)S(1)}, u32[]{:S(2)}, u32[]{:S(2)}) collective-permute-start(bf16[272,128]{1,0:T(8,128)(2,1)S(1)} %get-tuple-element.33.refs_0_.q_ref), channel_id=1, source_target_pairs={{0,8},{4,12},{8,0},{12,4},{16,24},{20,28},{24,16},{28,20},{1,9},{5... | collective-permute-start | bytes 208904 | tf_op jit(solution)/shard_map/ppermute | solution.py:394
  11.2 0.8 %shard_map.110.code_ref = s32[4,128]{1,0:T(4,128)S(1)} custom-call(s32[1]{0:T(128)S(6)} %copy.12.len_ref, s32[4,128]{1,0:T(4,128)} %slot_hbm.1, s32[1,4]{1,0:T(1,128)} %table_hbm.1), custom_call_target="tpu_custom_call" | custom-call | flops 1 | bytes 1 | tf_op jit(solution)/shard_map/pallas_call | solution.py:139
  12.0 0.8 %collective-permute-done.3.refs_1_ = bf16[272,128]{1,0:T(8,128)(2,1)S(1)} collective-permute-done((bf16[272,128]{1,0:T(8,128)(2,1)S(1)}, bf16[272,128]{1,0:T(8,128)(2,1)S(1)}, u32[]{:S(2)}, u32[]{:S(2)}) %collective-permute-start.3) | collective-permute-done | bytes 69664 | tf_op jit(solution)/shard_map/ppermute | solution.py:394
  12.8 0.5 %collective-permute-start.2 = (s32[4,128]{1,0:T(4,128)S(1)}, s32[4,128]{1,0:T(4,128)S(1)}, u32[]{:S(2)}, u32[]{:S(2)}) collective-permute-start(s32[4,128]{1,0:T(4,128)S(1)} %shard_map.110.code_ref), channel_id=1, source_target_pairs={{0,4},{4,0},{8,12},{12,8},{16,20},{20,16},{24,28},{28,24},{1,5},{5... | collective-permute-start | bytes 6152 | tf_op jit(solution)/shard_map/ppermute | solution.py:403
  13.3 0.0 copy-done
  13.3 0.6 %shard_map.111 = (bf16[256,128]{1,0:T(8,128)(2,1)S(1)}, bf16[256,128]{1,0:T(8,128)(2,1)S(1)}, bf16[512,256]{1,0:T(8,128)(2,1)S(1)}, bf16[256,512]{1,0:T(8,128)(2,1)S(1)}, bf16[512,128]{1,0:T(8,128)(2,1)S(1)}) custom-call(bf16[128,1024]{1,0:T(8,128)(2,1)S(1)} %get-tuple-element.35.normed_ref, bf16[3,1024,256]{2,1,0:T(8,128)(2,1)S(1)} %bitcast.6, ...), custom_call_target="tpu_custom_call" | custom-call | flops 1 | bytes 1 | tf_op jit(solution)/shard_map/pallas_call | solution.py:139
  14.0 0.0 copy-start.1
  14.0 1.3 %collective-permute-done.4.refs_2_ = bf16[272,128]{1,0:T(8,128)(2,1)S(1)} collective-permute-done((bf16[272,128]{1,0:T(8,128)(2,1)S(1)}, bf16[272,128]{1,0:T(8,128)(2,1)S(1)}, u32[]{:S(2)}, u32[]{:S(2)}) %collective-permute-start.4) | collective-permute-done | bytes 69664 | tf_op jit(solution)/shard_map/ppermute | solution.py:394
  15.3 0.1 collective-permute-done.5.refs_3_
  15.3 2.2 %shard_map.112 = (bf16[256,512]{1,0:T(8,128)(2,1)S(1)}, f32[4,512]{1,0:T(4,128)S(1)}) custom-call(f32[32,128]{1,0:T(8,128)S(1)} %get-tuple-element.32.rows_ref, bf16[512,256]{1,0:T(8,128)(2,1)S(1)} %get-tuple-element.42.keys_ref, bf16[256,512]{1,0:T(8,128)(2,1)S(1)} %get-tuple-element.43.values_ref, bf16[512,128]{1,0:T(8,128)(2,1)S(1)} %get-tuple-element.44.terms_ref, ...), custom_call_target="tpu_custom_call" | custom-call | flops 1 | bytes 1 | tf_op jit(solution)/shard_map/pallas_call | solution.py:139
  17.5 0.0 collective-permute-done.pool_ref
  17.5 0.0 collective-permute-done.1.refs_2_
  17.5 0.0 collective-permute-done.2.code_ref
  17.5 2.5 %shard_map.113 = (bf16[272,128]{1,0:T(8,128)(2,1)S(1)}, bf16[272,128]{1,0:T(8,128)(2,1)S(1)}, bf16[272,128]{1,0:T(8,128)(2,1)S(1)}, bf16[272,128]{1,0:T(8,128)(2,1)S(1)}) custom-call(f32[32,128]{1,0:T(8,128)S(1)} %get-tuple-element.32.rows_ref, bf16[512,2,256]{2,1,0:T(2,128)(2,1)S(1)} %collective-permute-done.pool_ref, ...), custom_call_target="tpu_custom_call" | custom-call | flops 1 | bytes 1 | tf_op jit(solution)/shard_map/pallas_call | solution.py:139
  20.0 2.7 %collective-permute-start.6 = (bf16[272,128]{1,0:T(8,128)(2,1)S(1)}, bf16[272,128]{1,0:T(8,128)(2,1)S(1)}, u32[]{:S(2)}, u32[]{:S(2)}) collective-permute-start(bf16[272,128]{1,0:T(8,128)(2,1)S(1)} %get-tuple-element.48), channel_id=1, source_target_pairs={{0,24},{4,28},{8,16},{12,20},{16,8},{20,12},{24,0},{28,4},{1,25},{... | collective-permute-start | bytes 208904 | tf_op jit(solution)/shard_map/ppermute | solution.py:416
  22.7 0.0 collective-permute-start.7
  22.7 1.8 %collective-permute-start.8 = (bf16[272,128]{1,0:T(8,128)(2,1)S(1)}, bf16[272,128]{1,0:T(8,128)(2,1)S(1)}, u32[]{:S(2)}, u32[]{:S(2)}) collective-permute-start(bf16[272,128]{1,0:T(8,128)(2,1)S(1)} %get-tuple-element.50), channel_id=1, source_target_pairs={{0,8},{4,12},{8,0},{12,4},{16,24},{20,28},{24,16},{28,20},{1,9},{5... | collective-permute-start | bytes 208904 | tf_op jit(solution)/shard_map/ppermute | solution.py:416
  24.5 2.2 %collective-permute-done.6.refs_1_ = bf16[272,128]{1,0:T(8,128)(2,1)S(1)} collective-permute-done((bf16[272,128]{1,0:T(8,128)(2,1)S(1)}, bf16[272,128]{1,0:T(8,128)(2,1)S(1)}, u32[]{:S(2)}, u32[]{:S(2)}) %collective-permute-start.6) | collective-permute-done | bytes 69664 | tf_op jit(solution)/shard_map/ppermute | solution.py:416
  26.7 2.3 %collective-permute-done.7.refs_2_ = bf16[272,128]{1,0:T(8,128)(2,1)S(1)} collective-permute-done((bf16[272,128]{1,0:T(8,128)(2,1)S(1)}, bf16[272,128]{1,0:T(8,128)(2,1)S(1)}, u32[]{:S(2)}, u32[]{:S(2)}) %collective-permute-start.7) | collective-permute-done | bytes 69664 | tf_op jit(solution)/shard_map/ppermute | solution.py:416
  29.0 0.0 collective-permute-done.8.refs_3_
  29.0 0.0 copy-done.1
  29.0 0.0 collective-permute-start.10
  29.0 0.5 %collective-permute-start.13 = (bf16[256,1024]{1,0:T(8,128)(2,1)S(1)}, bf16[256,1024]{1,0:T(8,128)(2,1)S(1)}, u32[]{:S(2)}, u32[]{:S(2)}) collective-permute-start(bf16[256,1024]{1,0:T(8,128)(2,1)S(1)} %collective-permute-done.1.refs_2_), channel_id=1, source_target_pairs={{0,1},{1,0},{2,3},{3,2},{4,5},{5,4},{6,7},{7,6},{8,9},{9,8},{10,11... | collective-permute-start | bytes 1572872 | tf_op jit(solution)/shard_map/ppermute | solution.py:418
  29.5 0.2 shard_map.114.refs_0_
  29.8 0.1 collective-permute-start.9
  29.9 0.5 %collective-permute-start.11 = (bf16[128,256]{1,0:T(8,128)(2,1)S(1)}, bf16[128,256]{1,0:T(8,128)(2,1)S(1)}, u32[]{:S(2)}, u32[]{:S(2)}) collective-permute-start(bf16[128,256]{1,0:T(8,128)(2,1)S(1)} %shard_map.114.refs_0_), channel_id=1, source_target_pairs={{0,2},{1,3},{2,0},{3,1},{4,6},{5,7},{6,4},{7,5},{8,10},{9,11},{10,... | collective-permute-start | bytes 196616 | tf_op jit(solution)/shard_map/ppermute | solution.py:420
  30.5 1.3 %collective-permute-start.12 = (bf16[128,256]{1,0:T(8,128)(2,1)S(1)}, bf16[128,256]{1,0:T(8,128)(2,1)S(1)}, u32[]{:S(2)}, u32[]{:S(2)}) collective-permute-start(bf16[128,256]{1,0:T(8,128)(2,1)S(1)} %shard_map.114.refs_0_), channel_id=1, source_target_pairs={{0,3},{1,2},{2,1},{3,0},{4,7},{5,6},{6,5},{7,4},{8,11},{9,10},{10,... | collective-permute-start | bytes 196616 | tf_op jit(solution)/shard_map/ppermute | solution.py:420
  31.7 0.1 collective-permute-done.9.refs_1_
  31.8 0.0 collective-permute-done.10.refs_3_
  31.8 0.3 shard_map.115.base_ref
  32.1 2.7 %collective-permute-done.11.refs_0_ = bf16[128,256]{1,0:T(8,128)(2,1)S(1)} collective-permute-done((bf16[128,256]{1,0:T(8,128)(2,1)S(1)}, bf16[128,256]{1,0:T(8,128)(2,1)S(1)}, u32[]{:S(2)}, u32[]{:S(2)}) %collective-permute-start.11) | collective-permute-done | bytes 65568 | tf_op jit(solution)/shard_map/ppermute | solution.py:420
  34.8 0.5 %collective-permute-done.12.refs_1_ = bf16[128,256]{1,0:T(8,128)(2,1)S(1)} collective-permute-done((bf16[128,256]{1,0:T(8,128)(2,1)S(1)}, bf16[128,256]{1,0:T(8,128)(2,1)S(1)}, u32[]{:S(2)}, u32[]{:S(2)}) %collective-permute-start.12) | collective-permute-done | bytes 65568 | tf_op jit(solution)/shard_map/ppermute | solution.py:420
  35.3 0.0 collective-permute-done.13.refs_3_
  35.3 1.0 %shard_map.116 = bf16[128,1024]{1,0:T(8,128)(2,1)} custom-call(f32[128,1024]{1,0:T(8,128)S(1)} %shard_map.115.base_ref, bf16[128,256]{1,0:T(8,128)(2,1)S(1)} %collective-permute-done.11.refs_0_, bf16[128,256]{1,0:T(8,128)(2,1)S(1)} %collective-permute-done.12.refs_1_, bf16[256,1024]{1,0:T(8,128)(2,1)S(1)} %collective-permute-done.1.refs_2_, ...), custom_call_target="tpu_custom_call" | custom-call | flops 1 | bytes 1 | tf_op jit(solution)/shard_map/pallas_call | solution.py:139
Async XLA Ops:
  0.0 13.3 %copy-start = (bf16[1024,3,256]{2,0,1:T(8,128)(2,1)S(1)}, bf16[1024,3,256]{2,0,1:T(8,128)(2,1)}, u32[]{:S(2)}) copy-start(bf16[1024,3,256]{2,0,1:T(8,128)(2,1)} %param.13) | copy-start | bytes 4718596
  0.0 17.5 %collective-permute-start = (bf16[512,2,256]{2,1,0:T(2,128)(2,1)}, bf16[512,2,256]{2,1,0:T(2,128)(2,1)S(1)}, u32[]{:S(2)}, u32[]{:S(2)}) collective-permute-start(bf16[512,2,256]{2,1,0:T(2,128)(2,1)} %bitcast.7), channel_id=1, source_target_pairs={{0,4},{4,0},{8,12},{12,8},{16,20},{20,16},{24,28},{28,24},{1,5},{5... | collective-permute-start | bytes 1572872 | tf_op jit(solution)/shard_map/ppermute | solution.py:378
  3.0 14.6 %collective-permute-start.1 = (bf16[256,1024]{1,0:T(8,128)(2,1)}, bf16[256,1024]{1,0:T(8,128)(2,1)S(1)}, u32[]{:S(2)}, u32[]{:S(2)}) collective-permute-start(bf16[256,1024]{1,0:T(8,128)(2,1)} %refs_2_), channel_id=1, source_target_pairs={{0,2},{1,3},{2,0},{3,1},{4,6},{5,7},{6,4},{7,5},{8,10},{9,11},{10,... | collective-permute-start | bytes 1572872 | tf_op jit(solution)/shard_map/ppermute | solution.py:379
  6.1 6.8 %collective-permute-start.3 = (bf16[272,128]{1,0:T(8,128)(2,1)S(1)}, bf16[272,128]{1,0:T(8,128)(2,1)S(1)}, u32[]{:S(2)}, u32[]{:S(2)}) collective-permute-start(bf16[272,128]{1,0:T(8,128)(2,1)S(1)} %get-tuple-element.33.refs_0_.q_ref), channel_id=1, source_target_pairs={{0,24},{4,28},{8,16},{12,20},{16,8},{20,12},{24,0},{28,4},{1,25},{... | collective-permute-start | bytes 208904 | tf_op jit(solution)/shard_map/ppermute | solution.py:394
  9.7 5.5 %collective-permute-start.4 = (bf16[272,128]{1,0:T(8,128)(2,1)S(1)}, bf16[272,128]{1,0:T(8,128)(2,1)S(1)}, u32[]{:S(2)}, u32[]{:S(2)}) collective-permute-start(bf16[272,128]{1,0:T(8,128)(2,1)S(1)} %get-tuple-element.33.refs_0_.q_ref), channel_id=1, source_target_pairs={{0,16},{4,20},{8,24},{12,28},{16,0},{20,4},{24,8},{28,12},{1,17},{... | collective-permute-start | bytes 208904 | tf_op jit(solution)/shard_map/ppermute | solution.py:394
  9.7 5.6 %collective-permute-start.5 = (bf16[272,128]{1,0:T(8,128)(2,1)S(1)}, bf16[272,128]{1,0:T(8,128)(2,1)S(1)}, u32[]{:S(2)}, u32[]{:S(2)}) collective-permute-start(bf16[272,128]{1,0:T(8,128)(2,1)S(1)} %get-tuple-element.33.refs_0_.q_ref), channel_id=1, source_target_pairs={{0,8},{4,12},{8,0},{12,4},{16,24},{20,28},{24,16},{28,20},{1,9},{5... | collective-permute-start | bytes 208904 | tf_op jit(solution)/shard_map/ppermute | solution.py:394
  12.8 4.7 %collective-permute-start.2 = (s32[4,128]{1,0:T(4,128)S(1)}, s32[4,128]{1,0:T(4,128)S(1)}, u32[]{:S(2)}, u32[]{:S(2)}) collective-permute-start(s32[4,128]{1,0:T(4,128)S(1)} %shard_map.110.code_ref), channel_id=1, source_target_pairs={{0,4},{4,0},{8,12},{12,8},{16,20},{20,16},{24,28},{28,24},{1,5},{5... | collective-permute-start | bytes 6152 | tf_op jit(solution)/shard_map/ppermute | solution.py:403
  14.0 15.1 %copy-start.1 = (bf16[256,1024]{1,0:T(8,128)(2,1)S(1)}, bf16[256,1024]{1,0:T(8,128)(2,1)}, u32[]{:S(2)}) copy-start(bf16[256,1024]{1,0:T(8,128)(2,1)} %refs_2_) | copy-start | bytes 1572868
  20.0 6.6 %collective-permute-start.6 = (bf16[272,128]{1,0:T(8,128)(2,1)S(1)}, bf16[272,128]{1,0:T(8,128)(2,1)S(1)}, u32[]{:S(2)}, u32[]{:S(2)}) collective-permute-start(bf16[272,128]{1,0:T(8,128)(2,1)S(1)} %get-tuple-element.48), channel_id=1, source_target_pairs={{0,24},{4,28},{8,16},{12,20},{16,8},{20,12},{24,0},{28,4},{1,25},{... | collective-permute-start | bytes 208904 | tf_op jit(solution)/shard_map/ppermute | solution.py:416
  22.7 6.3 %collective-permute-start.7 = (bf16[272,128]{1,0:T(8,128)(2,1)S(1)}, bf16[272,128]{1,0:T(8,128)(2,1)S(1)}, u32[]{:S(2)}, u32[]{:S(2)}) collective-permute-start(bf16[272,128]{1,0:T(8,128)(2,1)S(1)} %get-tuple-element.49), channel_id=1, source_target_pairs={{0,16},{4,20},{8,24},{12,28},{16,0},{20,4},{24,8},{28,12},{1,17},{... | collective-permute-start | bytes 208904 | tf_op jit(solution)/shard_map/ppermute | solution.py:416
  22.7 6.3 %collective-permute-start.8 = (bf16[272,128]{1,0:T(8,128)(2,1)S(1)}, bf16[272,128]{1,0:T(8,128)(2,1)S(1)}, u32[]{:S(2)}, u32[]{:S(2)}) collective-permute-start(bf16[272,128]{1,0:T(8,128)(2,1)S(1)} %get-tuple-element.50), channel_id=1, source_target_pairs={{0,8},{4,12},{8,0},{12,4},{16,24},{20,28},{24,16},{28,20},{1,9},{5... | collective-permute-start | bytes 208904 | tf_op jit(solution)/shard_map/ppermute | solution.py:416
  29.0 2.8 %collective-permute-start.10 = (bf16[256,1024]{1,0:T(8,128)(2,1)S(1)}, bf16[256,1024]{1,0:T(8,128)(2,1)S(1)}, u32[]{:S(2)}, u32[]{:S(2)}) collective-permute-start(bf16[256,1024]{1,0:T(8,128)(2,1)S(1)} %copy-done.1), channel_id=1, source_target_pairs={{0,1},{1,0},{2,3},{3,2},{4,5},{5,4},{6,7},{7,6},{8,9},{9,8},{10,11... | collective-permute-start | bytes 1572872 | tf_op jit(solution)/shard_map/ppermute | solution.py:418
  29.0 6.3 %collective-permute-start.13 = (bf16[256,1024]{1,0:T(8,128)(2,1)S(1)}, bf16[256,1024]{1,0:T(8,128)(2,1)S(1)}, u32[]{:S(2)}, u32[]{:S(2)}) collective-permute-start(bf16[256,1024]{1,0:T(8,128)(2,1)S(1)} %collective-permute-done.1.refs_2_), channel_id=1, source_target_pairs={{0,1},{1,0},{2,3},{3,2},{4,5},{5,4},{6,7},{7,6},{8,9},{9,8},{10,11... | collective-permute-start | bytes 1572872 | tf_op jit(solution)/shard_map/ppermute | solution.py:418
  29.8 2.0 %collective-permute-start.9 = (bf16[128,256]{1,0:T(8,128)(2,1)S(1)}, bf16[128,256]{1,0:T(8,128)(2,1)S(1)}, u32[]{:S(2)}, u32[]{:S(2)}) collective-permute-start(bf16[128,256]{1,0:T(8,128)(2,1)S(1)} %shard_map.114.refs_0_), channel_id=1, source_target_pairs={{0,1},{1,0},{2,3},{3,2},{4,5},{5,4},{6,7},{7,6},{8,9},{9,8},{10,11... | collective-permute-start | bytes 196616 | tf_op jit(solution)/shard_map/ppermute | solution.py:420
  29.9 4.9 %collective-permute-start.11 = (bf16[128,256]{1,0:T(8,128)(2,1)S(1)}, bf16[128,256]{1,0:T(8,128)(2,1)S(1)}, u32[]{:S(2)}, u32[]{:S(2)}) collective-permute-start(bf16[128,256]{1,0:T(8,128)(2,1)S(1)} %shard_map.114.refs_0_), channel_id=1, source_target_pairs={{0,2},{1,3},{2,0},{3,1},{4,6},{5,7},{6,4},{7,5},{8,10},{9,11},{10,... | collective-permute-start | bytes 196616 | tf_op jit(solution)/shard_map/ppermute | solution.py:420
  30.5 4.9 %collective-permute-start.12 = (bf16[128,256]{1,0:T(8,128)(2,1)S(1)}, bf16[128,256]{1,0:T(8,128)(2,1)S(1)}, u32[]{:S(2)}, u32[]{:S(2)}) collective-permute-start(bf16[128,256]{1,0:T(8,128)(2,1)S(1)} %shard_map.114.refs_0_), channel_id=1, source_target_pairs={{0,3},{1,2},{2,1},{3,0},{4,7},{5,6},{6,5},{7,4},{8,11},{9,10},{10,... | collective-permute-start | bytes 196616 | tf_op jit(solution)/shard_map/ppermute | solution.py:420

commit v5 on v4

v5 whole, which is shorter than its diff:
```python
import jax
import jax.numpy as jnp
from jax import lax
from jax.experimental import pallas as pl
from jax.experimental.pallas import tpu as pltpu
from jax.sharding import PartitionSpec as P

HD = 64


def head_attend(qh, kh, vh, same, bias_same, bias_diff, valid):
    scores = jnp.dot(qh, kh.T, preferred_element_type=jnp.float32) * HD ** (-0.5)
    scores = scores + jnp.where(same, bias_same, bias_diff)
    scores = jnp.where(valid[None, :], scores, -1e30)
    peak = jnp.max(scores, axis=1)
    weights = jnp.exp(scores - peak[:, None])
    total = jnp.sum(weights, axis=1)
    mixed = (
        jnp.dot(weights.astype(jnp.bfloat16), vh, preferred_element_type=jnp.float32)
        / total[:, None]
    )
    mixed = lax.optimization_barrier(mixed.astype(jnp.bfloat16))
    return (mixed, peak, total)


def place_rows(dest, values, variates, owners, slots):
    onehot = (dest[:, None] == jnp.arange(owners, dtype=jnp.int32)[None, :]).astype(jnp.int32)
    before = jnp.cumsum(onehot, axis=0) - onehot
    slot = jnp.sum(before * onehot, axis=1)
    flat = dest * slots + slot
    width = values.shape[1]
    qbuf = (
        jnp.zeros((owners * slots, width), jnp.bfloat16)
        .at[flat]
        .set(values)
        .reshape(owners, slots, width)
    )
    vbuf = jnp.zeros((owners * slots,), jnp.int32).at[flat].set(variates).reshape(owners, slots)
    return (qbuf, vbuf, flat)


def routed_body(
    tokens,
    norm_gain,
    w_qkv,
    w_out,
    head_bias,
    kv_pool,
    key_variate,
    page_table,
    node_len,
    path_nodes,
    query_variate,
):
    tok_rows, width = tokens.shape
    heads_here = w_qkv.shape[2] // HD
    owners = lax.axis_size("seq")
    slots = min(tok_rows, 8 * tok_rows // owners)
    xf = tokens.astype(jnp.float32)
    normed = (xf * lax.rsqrt(jnp.mean(xf * xf, axis=1, keepdims=True) + 1e-05) * norm_gain).astype(
        jnp.bfloat16
    )
    qkv = jnp.dot(
        normed, w_qkv.reshape(width, 3 * heads_here * HD), preferred_element_type=jnp.float32
    ).astype(jnp.bfloat16)
    qkv = qkv.reshape(tok_rows, 3, heads_here, HD)
    query, key, value = (qkv[:, 0], qkv[:, 1], qkv[:, 2])
    order = page_table[0]
    node_slots = kv_pool.shape[0] * kv_pool.shape[1]
    pages = kv_pool[order].reshape(node_slots, 2, heads_here, HD)
    node_keys = jnp.moveaxis(pages[:, 0], 1, 0)
    node_values = jnp.moveaxis(pages[:, 1], 1, 0)
    key_var = key_variate[order].reshape(node_slots)
    valid = jnp.arange(node_slots, dtype=jnp.int32) < node_len[0]
    qflat = query.reshape(tok_rows, heads_here * HD)
    out_list, peak_list, total_list = ([], [], [])
    for level in range(3):
        qbuf, vbuf, flat = place_rows(path_nodes[:, level], qflat, query_variate, owners, slots)
        owner_qbuf = lax.all_to_all(qbuf, "seq", split_axis=0, concat_axis=0, tiled=True)
        owner_vbuf = lax.all_to_all(vbuf, "seq", split_axis=0, concat_axis=0, tiled=True)
        sources, count, cols = owner_qbuf.shape
        rows = sources * count
        heads_q = jnp.moveaxis(owner_qbuf.reshape(rows, heads_here, HD), 1, 0)
        same = owner_vbuf.reshape(rows)[:, None] == key_var[None, :]

        def per_head(xs):
            return head_attend(xs[0], xs[1], xs[2], same, xs[3], xs[4], valid)

        mixed, peak, total = lax.map(
            per_head, (heads_q, node_keys, node_values, head_bias[1], head_bias[0])
        )
        mixed = jnp.moveaxis(mixed, 0, 1).reshape(sources, count, cols)
        peak = peak.T.reshape(sources, count, heads_here)
        total = total.T.reshape(sources, count, heads_here)
        mixed_back = lax.all_to_all(mixed, "seq", split_axis=0, concat_axis=0, tiled=True)
        peak_back = lax.all_to_all(peak, "seq", split_axis=0, concat_axis=0, tiled=True)
        total_back = lax.all_to_all(total, "seq", split_axis=0, concat_axis=0, tiled=True)
        mixed = mixed_back
        peak = peak_back
        total = total_back
        out_list.append(mixed.reshape(owners * slots, -1)[flat].reshape(tok_rows, heads_here, HD))
        peak_list.append(peak.reshape(owners * slots, heads_here)[flat])
        total_list.append(total.reshape(owners * slots, heads_here)[flat])
    outs = jnp.stack(out_list, axis=1)
    peaks = jnp.stack(peak_list, axis=1)
    totals = jnp.stack(total_list, axis=1)
    own_peak = (
        jnp.sum(query.astype(jnp.float32) * key.astype(jnp.float32), axis=2) * HD ** (-0.5)
        + head_bias[1][None, :]
    )
    all_o = jnp.concatenate([value.astype(jnp.float32)[:, None], outs.astype(jnp.float32)], axis=1)
    all_m = jnp.concatenate([own_peak[:, None], peaks], axis=1)
    all_l = jnp.concatenate([jnp.ones((tok_rows, 1, heads_here), jnp.float32), totals], axis=1)
    top = jnp.max(all_m, axis=1, keepdims=True)
    scale = all_l * jnp.exp(all_m - top)
    attn = (jnp.sum(scale[..., None] * all_o, axis=1) / jnp.sum(scale, axis=1)[..., None]).astype(
        jnp.bfloat16
    )
    partial_sum = jnp.dot(
        attn.reshape(tok_rows, heads_here * HD), w_out, preferred_element_type=jnp.float32
    )
    total_sum = lax.psum(partial_sum, "tp")
    return (xf + total_sum).astype(jnp.bfloat16)


BF16, F32, I32 = jnp.bfloat16, jnp.float32, jnp.int32
AUX = 16
FAR = -1e30
PAGE = 128
MATES = (1, 2)
PEERS = ((6, 5), (4, 4), (2, 1))
VMEM = pl.BlockSpec(memory_space=pltpu.VMEM)
HBM = pl.BlockSpec(memory_space=pltpu.HBM)
SMEM = pl.BlockSpec(memory_space=pltpu.SMEM)


def call(kernel, outs, *args, flops=1, away=(), scratch=(), leaves=False):
    single = not isinstance(outs, (tuple, list))
    args = [pltpu.with_memory_space_constraint(a, pltpu.HBM) if i in away else a for i, a in enumerate(args)]
    return pl.pallas_call(
        kernel,
        out_shape=outs,
        scratch_shapes=scratch,
        in_specs=[HBM if i in away else SMEM if a.size == 1 else VMEM for i, a in enumerate(args)],
        out_specs=HBM if leaves else VMEM if single else [VMEM] * len(outs),
        compiler_params=pltpu.CompilerParams(vmem_limit_bytes=16 << 20),
        cost_estimate=pl.CostEstimate(flops=flops, bytes_accessed=1, transcendentals=0),
    )(*args)


def shape(*dims, dtype=BF16):
    return jax.ShapeDtypeStruct(dims, dtype)


def fetch(sems, *pairs):
    copies = [pltpu.make_async_copy(src, dst, sems.at[i]) for i, (src, dst) in enumerate(pairs)]
    for copy in copies:
        copy.start()
    return copies


def query_kernel(
    len_ref, tok_hbm, gain_hbm, w_hbm, variate_hbm, path_hbm, bias_hbm, slot_hbm, table_hbm, pool_hbm,
    msg_ref, normed_ref, rows_ref, tok_ref, pool_ref,
    gain_ref, w_ref, variate_ref, path_ref, bias_ref, slot_ref, table_ref, sems,
):
    pages, page = slot_ref.shape
    slots = pages * page
    copies = fetch(
        sems, (tok_hbm, tok_ref), (w_hbm.at[0], w_ref), (gain_hbm, gain_ref), (variate_hbm, variate_ref), (path_hbm, path_ref),
        (bias_hbm, bias_ref), (slot_hbm, slot_ref), (table_hbm, table_ref), (pool_hbm, pool_ref.at[pl.ds(0, slots)]),
    )
    for copy in copies[2:8]:
        copy.wait()
    rows, cols = tok_ref.shape[0], w_ref.shape[1]
    length = len_ref[0]
    offset = lax.broadcasted_iota(I32, (1, page), 1)
    for p in range(pages):
        place = sum(jnp.where(table_ref[0, i] == p, i, 0) for i in range(pages))
        code = jnp.where(place * page + offset < length, slot_ref[p : p + 1, :], 8).astype(F32)
        wide_code = jnp.concatenate([code, jnp.zeros((1, cols - page), F32)], axis=1) if cols > page else code
        pool_ref[slots + p] = jnp.concatenate([wide_code, wide_code], axis=0).astype(BF16)
    for head in range(cols // HD):
        same = jnp.full((1, rows), bias_ref[1, head], F32)
        other = jnp.full((1, rows), bias_ref[0, head], F32)
        rows_ref[8 * head : 8 * head + 8, :] = jnp.concatenate([same, other, same - other, jnp.zeros((5, rows), F32)], axis=0)
    aux = [variate_ref[...].astype(F32), path_ref[...].astype(F32), jnp.zeros((AUX - 4, rows), F32)]
    msg_ref[cols:, :] = jnp.concatenate(aux, axis=0).astype(BF16)
    copies[0].wait()
    x = tok_ref[...].astype(F32)
    r = lax.rsqrt(jnp.mean(x * x, axis=1, keepdims=True) + 1e-05)
    normed = (x * r * gain_ref[...]).astype(BF16)
    normed_ref[...] = normed
    copies[1].wait()
    q = jnp.dot(normed, w_ref[...], preferred_element_type=F32).astype(BF16)
    msg_ref[:cols, :] = (q.astype(F32) * HD ** (-0.5)).T.astype(BF16)
    copies[8].wait()


def split3(x):
    a = x.astype(BF16).astype(F32)
    b = (x - a).astype(BF16).astype(F32)
    return a, b, (x - a - b).astype(BF16).astype(F32)


def split_pool(pool_ref):
    rows, _, cols = pool_ref.shape
    pages = rows // (PAGE + 1)
    i = lax.broadcasted_iota(I32, (2 * PAGE, 2 * PAGE), 0)
    j = lax.broadcasted_iota(I32, (2 * PAGE, 2 * PAGE), 1)
    pick = jnp.where(j == 2 * (i % PAGE) + i // PAGE, 1.0, 0.0).astype(BF16)
    keys, values = [], []
    for p in range(pages):
        both = pool_ref[p * PAGE : (p + 1) * PAGE].reshape(2 * PAGE, cols)
        apart = jnp.dot(pick, both, preferred_element_type=F32)
        keys.append(apart[:PAGE].astype(BF16))
        values.append(apart[PAGE:].T.astype(BF16))
    codes = [pool_ref[pages * PAGE + p].astype(F32)[0:1, :PAGE].astype(I32) for p in range(pages)]
    return jnp.concatenate(keys, axis=0), jnp.concatenate(values, axis=1), slot_terms(codes)


def slot_terms(codes):
    sub = lax.broadcasted_iota(I32, (128, PAGE), 0)
    blocks = []
    for row in codes:
        code = jnp.broadcast_to(row, (128, PAGE))
        hit = ((code == sub % 8) & (sub < 24)) | ((sub >= 24) & (sub < 27))
        term = jnp.where(hit, 1.0, 0.0)
        term = jnp.where((sub == 27) & (code == 8), FAR, term)
        blocks.append(term.T.astype(BF16))
    return jnp.concatenate(blocks, axis=0)


def row_terms(bias, variate):
    rows = variate.shape[1]
    sub = lax.broadcasted_iota(I32, (8, rows), 0)
    hit = variate == sub
    other, step = split3(bias[1:2, :]), split3(bias[2:3, :])
    picked = [jnp.where(hit, jnp.broadcast_to(piece, (8, rows)), 0.0) for piece in step]
    tail = jnp.where(sub == 3, 1.0, 0.0)
    for at, piece in enumerate(other):
        tail = jnp.where(sub == at, piece, tail)
    top = jnp.concatenate(picked + [tail], axis=0).astype(BF16)
    return jnp.concatenate([top, jnp.zeros((96, rows), BF16)], axis=0)


def query_terms(q, rows_ref, variate):
    blocks = variate.shape[1] // rows_ref.shape[1]
    cats = []
    for head in range(q.shape[0] // HD):
        q_head = q[head * HD : (head + 1) * HD, :]
        zero = jnp.zeros_like(q_head)
        both = [q_head, zero] if head % 2 == 0 else [zero, q_head]
        cats.append(jnp.concatenate(both + [row_terms(wide(rows_ref, head, blocks), variate)], axis=0))
    return cats


def attend(cats, node):
    keys, values_t, terms = node
    scores = []
    for head, cat in enumerate(cats):
        pair = head // 2
        k_cat = jnp.concatenate([keys[:, pair * 128 : (pair + 1) * 128], terms], axis=1)
        scores.append(jnp.dot(k_cat, cat, preferred_element_type=F32))
    done = []
    for head, score in enumerate(scores):
        peak = jnp.max(score, axis=0, keepdims=True)
        weights = jnp.exp(score - peak)
        total = jnp.sum(weights, axis=0, keepdims=True)
        mixed = jnp.dot(values_t[head * HD : (head + 1) * HD, :], weights.astype(BF16), preferred_element_type=F32)
        done.append(((mixed / total).astype(BF16), peak + jnp.log(total)))
    return done


def wide(rows_ref, head, blocks):
    return jnp.concatenate([rows_ref[8 * head : 8 * head + 8, :]] * blocks, axis=1)


def gather_rows(msgs, cols):
    q = jnp.concatenate([msg[:cols, :] for msg in msgs], axis=1)
    aux = jnp.concatenate([msg[cols:, :].astype(F32).astype(I32) for msg in msgs], axis=1)
    return q, aux


def own_kernel(normed_ref, w_ref, pool_ref, out_hbm, k_ref, v_ref, keys_ref, values_ref, terms_ref, out_ref, sem):
    copy = pltpu.make_async_copy(out_hbm, out_ref, sem)
    copy.start()
    for i, own_ref in ((1, k_ref), (2, v_ref)):
        own = jnp.dot(normed_ref[...], w_ref[i], preferred_element_type=F32).astype(BF16)
        own_ref[...] = own.astype(F32).T.astype(BF16)
    keys_ref[...], values_ref[...], terms_ref[...] = split_pool(pool_ref)
    copy.wait()


def pair_terms(rows_ref, mine, theirs, msgs, outs):
    count = len(msgs)
    cols = mine[0].shape[1]
    rows = msgs[0].shape[1]
    q, aux = gather_rows(msgs, cols)
    cats = query_terms(q, rows_ref, aux[0:1, :])
    me = lax.axis_index("seq")
    mate = me ^ jnp.where(lax.axis_index("tp") % 2 == 0, MATES[0], MATES[1])
    named = lambda node: jnp.max((aux[1:4, :] == node).astype(I32), axis=0, keepdims=True) > 0
    named_1, named_2 = named(me), named(mate)
    pieces = []
    for head, ((o1, lse1), (o2, lse2)) in enumerate(zip(attend(cats, mine), attend(cats, theirs))):
        lse1 = jnp.where(named_1, lse1, FAR)
        lse2 = jnp.where(named_2, lse2, FAR)
        top = jnp.maximum(lse1, lse2)
        w1, w2 = jnp.exp(lse1 - top), jnp.exp(lse2 - top)
        merged = ((w1 * o1.astype(F32) + w2 * o2.astype(F32)) / (w1 + w2)).astype(BF16)
        for b, out in enumerate(outs):
            out[head * HD : (head + 1) * HD, :] = merged[:, b * rows : (b + 1) * rows]
        pieces += split3(top + jnp.log(w1 + w2))
    pieces.append(jnp.zeros((AUX - len(pieces), count * rows), F32))
    tail = jnp.concatenate(pieces, axis=0).astype(BF16)
    for b, out in enumerate(outs):
        out[cols:, :] = tail[:, b * rows : (b + 1) * rows]


def far_kernel(rows_ref, keys_ref, values_ref, terms_ref, pool_ref, *refs):
    count = (len(refs) - 3) // 2
    mate = split_pool(pool_ref)
    pair_terms(rows_ref, (keys_ref[...], values_ref[...], terms_ref[...]), mate, refs[:count], refs[count : 2 * count])
    for ref, value in zip(refs[2 * count :], mate):
        ref[...] = value


def near_kernel(rows_ref, *refs):
    nodes, refs = [ref[...] for ref in refs[:6]], refs[6:]
    count = len(refs) // 2
    pair_terms(rows_ref, nodes[:3], nodes[3:], refs[:count], refs[count:])


def add_parts(acc, parts, cols):
    auxes = [part[cols:, :].astype(F32) for part in parts]
    for head, (top, whole, total) in enumerate(acc):
        at = slice(head * HD, (head + 1) * HD)
        lses = [sum(aux[3 * head + i : 3 * head + i + 1, :] for i in range(3)) for aux in auxes]
        peak = top
        for lse in lses:
            peak = jnp.maximum(peak, lse)
        weight = jnp.exp(top - peak)
        whole, total = weight * whole, weight * total
        for lse, part in zip(lses, parts):
            weight = jnp.exp(lse - peak)
            whole = whole + weight
            total = total + weight * part[at, :].astype(F32)
        yield peak, whole, total


def combine_far_kernel(rows_ref, q_ref, k_ref, v_ref, *refs):
    *parts, acc_ref, side_ref = refs
    cols = k_ref.shape[0]
    acc = []
    for head in range(cols // HD):
        at = slice(head * HD, (head + 1) * HD)
        q, k = q_ref[at, :].astype(F32), k_ref[at, :].astype(F32)
        own = jnp.sum(q * k, axis=0, keepdims=True) + rows_ref[8 * head : 8 * head + 1, :]
        acc.append((own, jnp.ones_like(own), v_ref[at, :].astype(F32)))
    for head, (top, whole, total) in enumerate(add_parts(acc, parts, cols)):
        acc_ref[head * HD : (head + 1) * HD, :] = total
        side_ref[2 * head : 2 * head + 2, :] = jnp.concatenate([top, whole], axis=0)


def combine_near_kernel(acc_ref, side_ref, *refs):
    *parts, attn_ref = refs
    cols = acc_ref.shape[0]
    acc = [
        (side_ref[2 * head : 2 * head + 1, :], side_ref[2 * head + 1 : 2 * head + 2, :], acc_ref[head * HD : (head + 1) * HD, :])
        for head in range(cols // HD)
    ]
    done = [total / whole for _, whole, total in add_parts(acc, parts, cols)]
    attn_ref[...] = jnp.concatenate(done, axis=0).T.astype(BF16)


def project_kernel(base_ref, *refs):
    *pairs, out_ref = refs
    half = len(pairs) // 2
    total = base_ref[...].astype(F32)
    for attn, w in zip(pairs[:half], pairs[half:]):
        total = total + jnp.dot(attn[...], w[...], preferred_element_type=F32)
    out_ref[...] = total.astype(out_ref.dtype)


def last_kernel(base_ref, *refs):
    *pairs, out_hbm, out_ref, sems = refs
    half = len(pairs) // 2
    step = 256
    copies = []
    for i, at in enumerate(range(0, base_ref.shape[1], step)):
        span = slice(at, at + step)
        total = base_ref[:, span]
        for attn, w in zip(pairs[:half], pairs[half:]):
            total = total + jnp.dot(attn[...], w[:, span], preferred_element_type=F32)
        out_ref[:, span] = total.astype(out_ref.dtype)
        copies.append(pltpu.make_async_copy(out_ref.at[:, span], out_hbm.at[:, span], sems.at[i]))
        copies[-1].start()
    for copy in copies:
        copy.wait()


def swap(x, masks):
    owners, parts = lax.axis_size("seq"), lax.axis_size("tp")
    pairs = [(i * parts + t, (i ^ masks[t % 2]) * parts + t) for i in range(owners) for t in range(parts)]
    return lax.ppermute(x, ("seq", "tp"), pairs)


def across(x, mask):
    return lax.ppermute(x, "tp", [(t, t ^ mask) for t in range(lax.axis_size("tp"))])


def dense_body(
    tokens,
    norm_gain,
    w_qkv,
    w_out,
    head_bias,
    kv_pool,
    key_variate,
    page_table,
    node_len,
    path_nodes,
    query_variate,
):
    rows, width = tokens.shape
    cols = w_qkv.shape[2]
    heads = cols // HD
    pages, page = key_variate.shape
    slots = pages * page

    w3 = w_qkv.transpose(1, 0, 2)
    msg, normed, bias, tok, pool = call(
        query_kernel,
        [
            shape(cols + AUX, rows), shape(rows, width), shape(8 * heads, rows, dtype=F32), shape(rows, width),
            shape(slots + pages, 2, cols),
        ],
        node_len, tokens, norm_gain[None], w3, query_variate[None], path_nodes.T, head_bias, key_variate, page_table,
        kv_pool.reshape(slots, 2, cols),
        away=range(1, 10),
        scratch=[
            pltpu.VMEM((1, width), F32), pltpu.VMEM((width, cols), BF16), pltpu.VMEM((1, rows), I32), pltpu.VMEM((3, rows), I32),
            pltpu.VMEM((2, heads), F32), pltpu.VMEM((pages, page), I32), pltpu.SMEM((1, pages), I32),
            pltpu.SemaphoreType.DMA((9,)),
        ],
    )
    msgs = [msg] + [swap(msg, peer) for peer in PEERS]
    pool2 = swap(pool, MATES)

    key, value, keys, values_t, terms, w_own = call(
        own_kernel,
        [
            shape(cols, rows), shape(cols, rows), shape(slots, cols), shape(cols, slots), shape(slots, 128), shape(cols, width),
        ],
        normed, w3, pool, w_out,
        flops=115300000,
        away=(3,),
        scratch=[pltpu.SemaphoreType.DMA],
    )
    w_far = across(w_own, 2)
    far = len(PEERS) - 1
    node = [shape(slots, cols), shape(cols, slots), shape(slots, 128)]
    message = shape(cols + AUX, rows)
    *far_out, keys2, values2, terms2 = call(
        far_kernel, [message] * far + node, bias, keys, values_t, terms, pool2, *msgs[1 : 1 + far], flops=2306000000
    )
    own_out, near_out = call(
        near_kernel, [message] * 2, bias, keys, values_t, terms, keys2, values2, terms2, msgs[0], msgs[-1], flops=2306000000
    )
    far_back = [swap(m, peer) for m, peer in zip(far_out, PEERS)]
    near_back = swap(near_out, PEERS[-1])
    acc, side = call(
        combine_far_kernel, [shape(cols, rows, dtype=F32), shape(2 * heads, rows, dtype=F32)],
        bias, msg, key, value, *far_back,
        flops=4612000000,
    )
    w_own, w_far, acc, near_back = lax.optimization_barrier((w_own, w_far, acc, near_back))
    w_near, w_last = across(w_own, 1), across(w_far, 1)
    attn = call(combine_near_kernel, shape(rows, cols), acc, side, own_out, near_back, flops=115300000)
    x_near, x_far, x_last = (across(attn, k) for k in (1, 2, 3))
    total = call(project_kernel, shape(rows, width, dtype=F32), tok, attn, x_near, w_own, w_near)
    return call(
        last_kernel, shape(rows, width), total, x_far, x_last, w_far, w_last,
        scratch=[pltpu.VMEM((rows, width), BF16), pltpu.SemaphoreType.DMA((width // 256,))],
        leaves=True,
    )


def solution(mesh):
    in_specs = (
        P("seq", None),
        P(),
        P(None, None, "tp"),
        P("tp", None),
        P(None, "tp"),
        P("seq", None, None, "tp"),
        P("seq", None),
        P("seq", None),
        P("seq"),
        P("seq", None),
        P("seq"),
    )
    out_specs = P("seq", None)
    owners, parts = mesh.shape["seq"], mesh.shape["tp"]
    dense = owners == 8 and parts == 4
    body = dense_body if dense else routed_body
    return jax.shard_map(body, mesh=mesh, in_specs=in_specs, out_specs=out_specs, check_vma=False)
```

time: 36.5 us -> 35.1 us (0.962)
  Pallas kernels: 9.32 us -> 8.02 us
    pallas_call x8, Pallas kernels: 9.32 us -> 8.02 us  [call(): pl.pallas_call(kernel, out_shape=outs, scratch_shapes=scratch, in_specs=[...]
    ppermute x14 -> x13, starting transfers between devices: 16.3 us -> 16 us  [the longest x7 11.9 us: swap(): return lax.ppermute(x, ('seq', 'tp'), pairs)]
    ppermute x14 -> x13, waiting for transfers between devices: 9.93 us -> 10 us  [the longest x7 6.43 us: swap(): return lax.ppermute(x, ('seq', 'tp'), pairs)]
  transfers between devices with their start and end apart: 14 -> 13, of which waited for: 8 -> 6; matrix products, arithmetic and copies ran while one was open for 0% -> 0% of each run, Pallas kernels for 16% -> 15%
where the time goes in v5:
time: 35.1 us; the launch traced here: 34.9 us
  starting transfers between devices  16 us (46%)
  waiting for transfers between devices  10 us (28%)
  Pallas kernels  8.02 us (23%)
  between operations  0.85 us (2%)
    ppermute x7, starting transfers between devices, swap(): return lax.ppermute(x, ('seq', 'tp'), pairs)  11.9 us
    pallas_call x8, Pallas kernels, call(): pl.pallas_call(kernel, out_shape=outs, scratch_shapes=scratch, in_specs=[...  8.02 us
    ppermute x7, waiting for transfers between devices, swap(): return lax.ppermute(x, ('seq', 'tp'), pairs)  6.43 us
    ppermute x6, starting transfers between devices, across(): lax.ppermute(x, 'tp', [(t, t ^ mask) for t in range(lax.axis_size('tp'))])  4.06 us
    ppermute x6, waiting for transfers between devices, across(): lax.ppermute(x, 'tp', [(t, t ^ mask) for t in range(lax.axis_size('tp'))])  3.59 us
  transfers between devices with their start and end apart: 13, of which 6 were waited for; matrix products, arithmetic and copies ran while one was open for 0% of the time, Pallas kernels for 15%

profile of v5, /device:TPU:0, one launch (start us, length us, event | category | flops | bytes accessed | tf_op | source)
XLA Modules:
  0.0 34.9 jit_solution(8747608900758160723)
XLA Ops:
  0.0 0.0 copy-start
  0.8 1.7 %shard_map.109 = (bf16[272,128]{1,0:T(8,128)(2,1)S(1)}, bf16[128,1024]{1,0:T(8,128)(2,1)S(1)}, f32[32,128]{1,0:T(8,128)S(1)}, bf16[128,1024]{1,0:T(8,128)(2,1)S(1)}, bf16[516,2,256]{2,1,0:T(2,128)(2,1)S(1)}) custom-call(s32[1]{0:T(128)S(6)} %copy.12.len_ref, bf16[128,1024]{1,0:T(8,128)(2,1)} %tok_hbm.1, f32[1,1024]{1,0:T(1,128)} %bitcast.8, ...), custom_call_target="tpu_custom_call" | custom-call | flops 1 | bytes 1 | tf_op jit(solution)/shard_map/pallas_call | solution.py:140
  2.4 3.0 %collective-permute-start.1 = (bf16[516,2,256]{2,1,0:T(2,128)(2,1)S(1)}, bf16[516,2,256]{2,1,0:T(2,128)(2,1)S(1)}, u32[]{:S(2)}, u32[]{:S(2)}) collective-permute-start(bf16[516,2,256]{2,1,0:T(2,128)(2,1)S(1)} %get-tuple-element.31.pool_ref), channel_id=1, source_target_pairs={{0,4},{1,9},{2,6},{3,11},{4,0},{5,13},{6,2},{7,15},{8,12},{9,1},{1... | collective-permute-start | bytes 1585160 | tf_op jit(solution)/shard_map/ppermute | solution.py:406
  5.5 3.6 %collective-permute-start.2 = (bf16[272,128]{1,0:T(8,128)(2,1)S(1)}, bf16[272,128]{1,0:T(8,128)(2,1)S(1)}, u32[]{:S(2)}, u32[]{:S(2)}) collective-permute-start(bf16[272,128]{1,0:T(8,128)(2,1)S(1)} %get-tuple-element.34.q_ref.refs_6_), channel_id=1, source_target_pairs={{0,24},{1,21},{2,26},{3,23},{4,28},{5,17},{6,30},{7,19},{8,16},{9,... | collective-permute-start | bytes 208904 | tf_op jit(solution)/shard_map/ppermute | solution.py:406
  9.1 0.0 collective-permute-start.3
  9.1 0.8 %collective-permute-start.6 = (bf16[272,128]{1,0:T(8,128)(2,1)S(1)}, bf16[272,128]{1,0:T(8,128)(2,1)S(1)}, u32[]{:S(2)}, u32[]{:S(2)}) collective-permute-start(bf16[272,128]{1,0:T(8,128)(2,1)S(1)} %get-tuple-element.34.q_ref.refs_6_), channel_id=1, source_target_pairs={{0,8},{1,5},{2,10},{3,7},{4,12},{5,1},{6,14},{7,3},{8,0},{9,13},{1... | collective-permute-start | bytes 208904 | tf_op jit(solution)/shard_map/ppermute | solution.py:406
  9.9 0.0 copy-done
  9.9 1.1 %shard_map.110 = (bf16[256,128]{1,0:T(8,128)(2,1)S(1)}, bf16[256,128]{1,0:T(8,128)(2,1)S(1)}, bf16[512,256]{1,0:T(8,128)(2,1)S(1)}, bf16[256,512]{1,0:T(8,128)(2...) custom-call(bf16[128,1024]{1,0:T(8,128)(2,1)S(1)} %get-tuple-element.30.normed_ref, ...), custom_call_target="tpu_custom_call" | custom-call | flops 115300000 | bytes 1 | tf_op jit(solution)/shard_map/pallas_call | solution.py:140
  10.9 1.6 %collective-permute-start = (bf16[256,1024]{1,0:T(8,128)(2,1)S(1)}, bf16[256,1024]{1,0:T(8,128)(2,1)S(1)}, u32[]{:S(2)}, u32[]{:S(2)}) collective-permute-start(bf16[256,1024]{1,0:T(8,128)(2,1)S(1)} %get-tuple-element.51.refs_2_), channel_id=1, source_target_pairs={{0,2},{1,3},{2,0},{3,1},{4,6},{5,7},{6,4},{7,5},{8,10},{9,11},{10,... | collective-permute-start | bytes 1572872 | tf_op jit(solution)/shard_map/ppermute | solution.py:410
  12.5 0.0 collective-permute-done.2.refs_0_
  12.5 2.1 %collective-permute-done.3.refs_1_ = bf16[272,128]{1,0:T(8,128)(2,1)S(1)} collective-permute-done((bf16[272,128]{1,0:T(8,128)(2,1)S(1)}, bf16[272,128]{1,0:T(8,128)(2,1)S(1)}, u32[]{:S(2)}, u32[]{:S(2)}) %collective-permute-start.3) | collective-permute-done | bytes 69664 | tf_op jit(solution)/shard_map/ppermute | solution.py:406
  14.6 0.0 collective-permute-done.1.pool_ref
  14.6 2.0 %shard_map.111 = (bf16[272,128]{1,0:T(8,128)(2,1)S(1)}, bf16[272,128]{1,0:T(8,128)(2,1)S(1)}, bf16[512,256]{1,0:T(8,128)(2,1)S(1)}, bf16[256,512]{1,0:T(8,128)(2,1)S(1)}, bf16[512,128]{1,0:T(8,128)(2,1)S(1)}) custom-call(f32[32,128]{1,0:T(8,128)S(1)} %get-tuple-element.33.rows_ref, bf16[512,256]{1,0:T(8,128)(2,1)S(1)} %get-tuple-element.37.keys_ref.refs_0_, ...), custom_call_target="tpu_custom_call" | custom-call | flops 2305999872 | bytes 1 | tf_op jit(solution)/shard_map/pallas_call | solution.py:140
  16.6 3.7 %collective-permute-start.4 = (bf16[272,128]{1,0:T(8,128)(2,1)S(1)}, bf16[272,128]{1,0:T(8,128)(2,1)S(1)}, u32[]{:S(2)}, u32[]{:S(2)}) collective-permute-start(bf16[272,128]{1,0:T(8,128)(2,1)S(1)} %get-tuple-element.40), channel_id=1, source_target_pairs={{0,24},{1,21},{2,26},{3,23},{4,28},{5,17},{6,30},{7,19},{8,16},{9,... | collective-permute-start | bytes 208904 | tf_op jit(solution)/shard_map/ppermute | solution.py:406
  20.4 0.0 collective-permute-start.5
  20.4 0.0 collective-permute-done.6.refs_7_
  20.4 1.7 %shard_map.113 = (bf16[272,128]{1,0:T(8,128)(2,1)S(1)}, bf16[272,128]{1,0:T(8,128)(2,1)S(1)}) custom-call(f32[32,128]{1,0:T(8,128)S(1)} %get-tuple-element.33.rows_ref, bf16[512,256]{1,0:T(8,128)(2,1)S(1)} %get-tuple-element.37.keys_ref.refs_0_, bf16[256,512]{1,0:T(8,128)(2,1)S(1)} %get-tuple-element.38.values_ref.refs_1_, ...), custom_call_target="tpu_custom_call" | custom-call | flops 2305999872 | bytes 1 | tf_op jit(solution)/shard_map/pallas_call | solution.py:140
  22.1 0.8 %collective-permute-start.7 = (bf16[272,128]{1,0:T(8,128)(2,1)S(1)}, bf16[272,128]{1,0:T(8,128)(2,1)S(1)}, u32[]{:S(2)}, u32[]{:S(2)}) collective-permute-start(bf16[272,128]{1,0:T(8,128)(2,1)S(1)} %get-tuple-element.46), channel_id=1, source_target_pairs={{0,8},{1,5},{2,10},{3,7},{4,12},{5,1},{6,14},{7,3},{8,0},{9,13},{1... | collective-permute-start | bytes 208904 | tf_op jit(solution)/shard_map/ppermute | solution.py:406
  22.9 0.1 collective-permute-done.4.refs_0_
  23.0 4.2 %collective-permute-done.5.refs_1_ = bf16[272,128]{1,0:T(8,128)(2,1)S(1)} collective-permute-done((bf16[272,128]{1,0:T(8,128)(2,1)S(1)}, bf16[272,128]{1,0:T(8,128)(2,1)S(1)}, u32[]{:S(2)}, u32[]{:S(2)}) %collective-permute-start.5) | collective-permute-done | bytes 69664 | tf_op jit(solution)/shard_map/ppermute | solution.py:406
  27.2 0.1 shard_map.112
  27.3 0.0 collective-permute-done.refs_2_
  27.3 0.0 collective-permute-done.7.refs_1_
  27.3 0.2 collective-permute-start.9
  27.5 0.4 %collective-permute-start.12 = (bf16[256,1024]{1,0:T(8,128)(2,1)S(1)}, bf16[256,1024]{1,0:T(8,128)(2,1)S(1)}, u32[]{:S(2)}, u32[]{:S(2)}) collective-permute-start(bf16[256,1024]{1,0:T(8,128)(2,1)S(1)} %collective-permute-done.refs_2_), channel_id=1, source_target_pairs={{0,1},{1,0},{2,3},{3,2},{4,5},{5,4},{6,7},{7,6},{8,9},{9,8},{10,11... | collective-permute-start | bytes 1572872 | tf_op jit(solution)/shard_map/ppermute | solution.py:410
  27.9 0.1 shard_map.114.refs_0_
  28.0 0.2 collective-permute-start.8
  28.2 1.5 %collective-permute-start.10 = (bf16[128,256]{1,0:T(8,128)(2,1)S(1)}, bf16[128,256]{1,0:T(8,128)(2,1)S(1)}, u32[]{:S(2)}, u32[]{:S(2)}) collective-permute-start(bf16[128,256]{1,0:T(8,128)(2,1)S(1)} %shard_map.114.refs_0_), channel_id=1, source_target_pairs={{0,2},{1,3},{2,0},{3,1},{4,6},{5,7},{6,4},{7,5},{8,10},{9,11},{10,... | collective-permute-start | bytes 196616 | tf_op jit(solution)/shard_map/ppermute | solution.py:410
  29.7 0.2 collective-permute-start.11
  30.0 0.2 collective-permute-done.8.refs_1_
  30.1 0.0 collective-permute-done.9.refs_3_
  30.1 0.3 shard_map.115.base_ref
  30.5 2.1 %collective-permute-done.10.refs_0_ = bf16[128,256]{1,0:T(8,128)(2,1)S(1)} collective-permute-done((bf16[128,256]{1,0:T(8,128)(2,1)S(1)}, bf16[128,256]{1,0:T(8,128)(2,1)S(1)}, u32[]{:S(2)}, u32[]{:S(2)}) %collective-permute-start.10) | collective-permute-done | bytes 65568 | tf_op jit(solution)/shard_map/ppermute | solution.py:410
  32.6 1.3 %collective-permute-done.11.refs_1_ = bf16[128,256]{1,0:T(8,128)(2,1)S(1)} collective-permute-done((bf16[128,256]{1,0:T(8,128)(2,1)S(1)}, bf16[128,256]{1,0:T(8,128)(2,1)S(1)}, u32[]{:S(2)}, u32[]{:S(2)}) %collective-permute-start.11) | collective-permute-done | bytes 65568 | tf_op jit(solution)/shard_map/ppermute | solution.py:410
  33.9 0.0 collective-permute-done.12.refs_3_
  33.9 1.0 %shard_map.116 = bf16[128,1024]{1,0:T(8,128)(2,1)} custom-call(f32[128,1024]{1,0:T(8,128)S(1)} %shard_map.115.base_ref, bf16[128,256]{1,0:T(8,128)(2,1)S(1)} %collective-permute-done.10.refs_0_, bf16[128,256]{1,0:T(8,128)(2,1)S(1)} %collective-permute-done.11.refs_1_, bf16[256,1024]{1,0:T(8,128)(2,1)S(1)} %collective-permute-done.refs_2_, ...), custom_call_target="tpu_custom_call" | custom-call | flops 1 | bytes 1 | tf_op jit(solution)/shard_map/pallas_call | solution.py:140
Async XLA Ops:
  0.0 9.9 %copy-start = (bf16[1024,3,256]{2,0,1:T(8,128)(2,1)S(1)}, bf16[1024,3,256]{2,0,1:T(8,128)(2,1)}, u32[]{:S(2)}) copy-start(bf16[1024,3,256]{2,0,1:T(8,128)(2,1)} %param.13) | copy-start | bytes 4718596
  2.4 12.2 %collective-permute-start.1 = (bf16[516,2,256]{2,1,0:T(2,128)(2,1)S(1)}, bf16[516,2,256]{2,1,0:T(2,128)(2,1)S(1)}, u32[]{:S(2)}, u32[]{:S(2)}) collective-permute-start(bf16[516,2,256]{2,1,0:T(2,128)(2,1)S(1)} %get-tuple-element.31.pool_ref), channel_id=1, source_target_pairs={{0,4},{1,9},{2,6},{3,11},{4,0},{5,13},{6,2},{7,15},{8,12},{9,1},{1... | collective-permute-start | bytes 1585160 | tf_op jit(solution)/shard_map/ppermute | solution.py:406
  5.5 7.0 %collective-permute-start.2 = (bf16[272,128]{1,0:T(8,128)(2,1)S(1)}, bf16[272,128]{1,0:T(8,128)(2,1)S(1)}, u32[]{:S(2)}, u32[]{:S(2)}) collective-permute-start(bf16[272,128]{1,0:T(8,128)(2,1)S(1)} %get-tuple-element.34.q_ref.refs_6_), channel_id=1, source_target_pairs={{0,24},{1,21},{2,26},{3,23},{4,28},{5,17},{6,30},{7,19},{8,16},{9,... | collective-permute-start | bytes 208904 | tf_op jit(solution)/shard_map/ppermute | solution.py:406
  9.1 5.5 %collective-permute-start.3 = (bf16[272,128]{1,0:T(8,128)(2,1)S(1)}, bf16[272,128]{1,0:T(8,128)(2,1)S(1)}, u32[]{:S(2)}, u32[]{:S(2)}) collective-permute-start(bf16[272,128]{1,0:T(8,128)(2,1)S(1)} %get-tuple-element.34.q_ref.refs_6_), channel_id=1, source_target_pairs={{0,16},{1,17},{2,18},{3,19},{4,20},{5,21},{6,22},{7,23},{8,24},{9,... | collective-permute-start | bytes 208904 | tf_op jit(solution)/shard_map/ppermute | solution.py:406
  9.1 11.3 %collective-permute-start.6 = (bf16[272,128]{1,0:T(8,128)(2,1)S(1)}, bf16[272,128]{1,0:T(8,128)(2,1)S(1)}, u32[]{:S(2)}, u32[]{:S(2)}) collective-permute-start(bf16[272,128]{1,0:T(8,128)(2,1)S(1)} %get-tuple-element.34.q_ref.refs_6_), channel_id=1, source_target_pairs={{0,8},{1,5},{2,10},{3,7},{4,12},{5,1},{6,14},{7,3},{8,0},{9,13},{1... | collective-permute-start | bytes 208904 | tf_op jit(solution)/shard_map/ppermute | solution.py:406
  10.9 16.4 %collective-permute-start = (bf16[256,1024]{1,0:T(8,128)(2,1)S(1)}, bf16[256,1024]{1,0:T(8,128)(2,1)S(1)}, u32[]{:S(2)}, u32[]{:S(2)}) collective-permute-start(bf16[256,1024]{1,0:T(8,128)(2,1)S(1)} %get-tuple-element.51.refs_2_), channel_id=1, source_target_pairs={{0,2},{1,3},{2,0},{3,1},{4,6},{5,7},{6,4},{7,5},{8,10},{9,11},{10,... | collective-permute-start | bytes 1572872 | tf_op jit(solution)/shard_map/ppermute | solution.py:410
  16.6 6.3 %collective-permute-start.4 = (bf16[272,128]{1,0:T(8,128)(2,1)S(1)}, bf16[272,128]{1,0:T(8,128)(2,1)S(1)}, u32[]{:S(2)}, u32[]{:S(2)}) collective-permute-start(bf16[272,128]{1,0:T(8,128)(2,1)S(1)} %get-tuple-element.40), channel_id=1, source_target_pairs={{0,24},{1,21},{2,26},{3,23},{4,28},{5,17},{6,30},{7,19},{8,16},{9,... | collective-permute-start | bytes 208904 | tf_op jit(solution)/shard_map/ppermute | solution.py:406
  20.4 6.8 %collective-permute-start.5 = (bf16[272,128]{1,0:T(8,128)(2,1)S(1)}, bf16[272,128]{1,0:T(8,128)(2,1)S(1)}, u32[]{:S(2)}, u32[]{:S(2)}) collective-permute-start(bf16[272,128]{1,0:T(8,128)(2,1)S(1)} %get-tuple-element.41), channel_id=1, source_target_pairs={{0,16},{1,17},{2,18},{3,19},{4,20},{5,21},{6,22},{7,23},{8,24},{9,... | collective-permute-start | bytes 208904 | tf_op jit(solution)/shard_map/ppermute | solution.py:406
  22.1 5.2 %collective-permute-start.7 = (bf16[272,128]{1,0:T(8,128)(2,1)S(1)}, bf16[272,128]{1,0:T(8,128)(2,1)S(1)}, u32[]{:S(2)}, u32[]{:S(2)}) collective-permute-start(bf16[272,128]{1,0:T(8,128)(2,1)S(1)} %get-tuple-element.46), channel_id=1, source_target_pairs={{0,8},{1,5},{2,10},{3,7},{4,12},{5,1},{6,14},{7,3},{8,0},{9,13},{1... | collective-permute-start | bytes 208904 | tf_op jit(solution)/shard_map/ppermute | solution.py:406
  27.3 2.8 %collective-permute-start.9 = (bf16[256,1024]{1,0:T(8,128)(2,1)S(1)}, bf16[256,1024]{1,0:T(8,128)(2,1)S(1)}, u32[]{:S(2)}, u32[]{:S(2)}) collective-permute-start(bf16[256,1024]{1,0:T(8,128)(2,1)S(1)} %get-tuple-element.51.refs_2_), channel_id=1, source_target_pairs={{0,1},{1,0},{2,3},{3,2},{4,5},{5,4},{6,7},{7,6},{8,9},{9,8},{10,11... | collective-permute-start | bytes 1572872 | tf_op jit(solution)/shard_map/ppermute | solution.py:410
  27.5 6.4 %collective-permute-start.12 = (bf16[256,1024]{1,0:T(8,128)(2,1)S(1)}, bf16[256,1024]{1,0:T(8,128)(2,1)S(1)}, u32[]{:S(2)}, u32[]{:S(2)}) collective-permute-start(bf16[256,1024]{1,0:T(8,128)(2,1)S(1)} %collective-permute-done.refs_2_), channel_id=1, source_target_pairs={{0,1},{1,0},{2,3},{3,2},{4,5},{5,4},{6,7},{7,6},{8,9},{9,8},{10,11... | collective-permute-start | bytes 1572872 | tf_op jit(solution)/shard_map/ppermute | solution.py:410
  28.0 2.1 %collective-permute-start.8 = (bf16[128,256]{1,0:T(8,128)(2,1)S(1)}, bf16[128,256]{1,0:T(8,128)(2,1)S(1)}, u32[]{:S(2)}, u32[]{:S(2)}) collective-permute-start(bf16[128,256]{1,0:T(8,128)(2,1)S(1)} %shard_map.114.refs_0_), channel_id=1, source_target_pairs={{0,1},{1,0},{2,3},{3,2},{4,5},{5,4},{6,7},{7,6},{8,9},{9,8},{10,11... | collective-permute-start | bytes 196616 | tf_op jit(solution)/shard_map/ppermute | solution.py:410
  28.2 4.4 %collective-permute-start.10 = (bf16[128,256]{1,0:T(8,128)(2,1)S(1)}, bf16[128,256]{1,0:T(8,128)(2,1)S(1)}, u32[]{:S(2)}, u32[]{:S(2)}) collective-permute-start(bf16[128,256]{1,0:T(8,128)(2,1)S(1)} %shard_map.114.refs_0_), channel_id=1, source_target_pairs={{0,2},{1,3},{2,0},{3,1},{4,6},{5,7},{6,4},{7,5},{8,10},{9,11},{10,... | collective-permute-start | bytes 196616 | tf_op jit(solution)/shard_map/ppermute | solution.py:410
  29.7 4.1 %collective-permute-start.11 = (bf16[128,256]{1,0:T(8,128)(2,1)S(1)}, bf16[128,256]{1,0:T(8,128)(2,1)S(1)}, u32[]{:S(2)}, u32[]{:S(2)}) collective-permute-start(bf16[128,256]{1,0:T(8,128)(2,1)S(1)} %shard_map.114.refs_0_), channel_id=1, source_target_pairs={{0,3},{1,2},{2,1},{3,0},{4,7},{5,6},{6,5},{7,4},{8,11},{9,10},{10,... | collective-permute-start | bytes 196616 | tf_op jit(solution)/shard_map/ppermute | solution.py:410

commit v6 on v5

--- a/solution.py
+++ b/solution.py
@@ -126,9 +126,8 @@
 BF16, F32, I32 = jnp.bfloat16, jnp.float32, jnp.int32
 AUX = 16
 FAR = -1e30
-PAGE = 128
 MATES = (1, 2)
-PEERS = ((6, 5), (4, 4), (2, 1))
+PEERS = ((4, 5), (6, 4), (2, 1))
 VMEM = pl.BlockSpec(memory_space=pltpu.VMEM)
 HBM = pl.BlockSpec(memory_space=pltpu.HBM)
 SMEM = pl.BlockSpec(memory_space=pltpu.SMEM)
@@ -161,14 +160,13 @@
 
 def query_kernel(
     len_ref, tok_hbm, gain_hbm, w_hbm, variate_hbm, path_hbm, bias_hbm, slot_hbm, table_hbm, pool_hbm,
-    msg_ref, normed_ref, rows_ref, tok_ref, pool_ref,
+    msg_ref, normed_ref, rows_ref, tok_ref, pool_ref, code_ref,
     gain_ref, w_ref, variate_ref, path_ref, bias_ref, slot_ref, table_ref, sems,
 ):
     pages, page = slot_ref.shape
-    slots = pages * page
     copies = fetch(
         sems, (tok_hbm, tok_ref), (w_hbm.at[0], w_ref), (gain_hbm, gain_ref), (variate_hbm, variate_ref), (path_hbm, path_ref),
-        (bias_hbm, bias_ref), (slot_hbm, slot_ref), (table_hbm, table_ref), (pool_hbm, pool_ref.at[pl.ds(0, slots)]),
+        (bias_hbm, bias_ref), (slot_hbm, slot_ref), (table_hbm, table_ref), (pool_hbm, pool_ref),
     )
     for copy in copies[2:8]:
         copy.wait()
@@ -177,9 +175,7 @@
     offset = lax.broadcasted_iota(I32, (1, page), 1)
     for p in range(pages):
         place = sum(jnp.where(table_ref[0, i] == p, i, 0) for i in range(pages))
-        code = jnp.where(place * page + offset < length, slot_ref[p : p + 1, :], 8).astype(F32)
-        wide_code = jnp.concatenate([code, jnp.zeros((1, cols - page), F32)], axis=1) if cols > page else code
-        pool_ref[slots + p] = jnp.concatenate([wide_code, wide_code], axis=0).astype(BF16)
+        code_ref[p : p + 1, :] = jnp.where(place * page + offset < length, slot_ref[p : p + 1, :], 8)
     for head in range(cols // HD):
         same = jnp.full((1, rows), bias_ref[1, head], F32)
         other = jnp.full((1, rows), bias_ref[0, head], F32)
@@ -203,27 +199,27 @@
     return a, b, (x - a - b).astype(BF16).astype(F32)
 
 
-def split_pool(pool_ref):
-    rows, _, cols = pool_ref.shape
-    pages = rows // (PAGE + 1)
-    i = lax.broadcasted_iota(I32, (2 * PAGE, 2 * PAGE), 0)
-    j = lax.broadcasted_iota(I32, (2 * PAGE, 2 * PAGE), 1)
-    pick = jnp.where(j == 2 * (i % PAGE) + i // PAGE, 1.0, 0.0).astype(BF16)
+def split_pool(pool_ref, code_ref):
+    cols = pool_ref.shape[2]
+    pages, page = code_ref.shape
+    i = lax.broadcasted_iota(I32, (2 * page, 2 * page), 0)
+    j = lax.broadcasted_iota(I32, (2 * page, 2 * page), 1)
+    pick = jnp.where(j == 2 * (i % page) + i // page, 1.0, 0.0).astype(BF16)
     keys, values = [], []
     for p in range(pages):
-        both = pool_ref[p * PAGE : (p + 1) * PAGE].reshape(2 * PAGE, cols)
+        both = pool_ref[p * page : (p + 1) * page].reshape(2 * page, cols)
         apart = jnp.dot(pick, both, preferred_element_type=F32)
-        keys.append(apart[:PAGE].astype(BF16))
-        values.append(apart[PAGE:].T.astype(BF16))
-    codes = [pool_ref[pages * PAGE + p].astype(F32)[0:1, :PAGE].astype(I32) for p in range(pages)]
-    return jnp.concatenate(keys, axis=0), jnp.concatenate(values, axis=1), slot_terms(codes)
-
-
-def slot_terms(codes):
-    sub = lax.broadcasted_iota(I32, (128, PAGE), 0)
+        keys.append(apart[:page].astype(BF16))
+        values.append(apart[page:].T.astype(BF16))
+    return jnp.concatenate(keys, axis=0), jnp.concatenate(values, axis=1), slot_terms(code_ref)
+
+
+def slot_terms(code_ref):
+    pages, page = code_ref.shape
+    sub = lax.broadcasted_iota(I32, (128, page), 0)
     blocks = []
-    for row in codes:
-        code = jnp.broadcast_to(row, (128, PAGE))
+    for p in range(pages):
+        code = jnp.broadcast_to(code_ref[p : p + 1, :], (128, page))
         hit = ((code == sub % 8) & (sub < 24)) | ((sub >= 24) & (sub < 27))
         term = jnp.where(hit, 1.0, 0.0)
         term = jnp.where((sub == 27) & (code == 8), FAR, term)
@@ -282,14 +278,11 @@
     return q, aux
 
 
-def own_kernel(normed_ref, w_ref, pool_ref, out_hbm, k_ref, v_ref, keys_ref, values_ref, terms_ref, out_ref, sem):
-    copy = pltpu.make_async_copy(out_hbm, out_ref, sem)
-    copy.start()
+def own_kernel(normed_ref, w_ref, pool_ref, code_ref, k_ref, v_ref, keys_ref, values_ref, terms_ref):
     for i, own_ref in ((1, k_ref), (2, v_ref)):
         own = jnp.dot(normed_ref[...], w_ref[i], preferred_element_type=F32).astype(BF16)
         own_ref[...] = own.astype(F32).T.astype(BF16)
-    keys_ref[...], values_ref[...], terms_ref[...] = split_pool(pool_ref)
-    copy.wait()
+    keys_ref[...], values_ref[...], terms_ref[...] = split_pool(pool_ref, code_ref)
 
 
 def pair_terms(rows_ref, mine, theirs, msgs, outs):
@@ -318,9 +311,9 @@
         out[cols:, :] = tail[:, b * rows : (b + 1) * rows]
 
 
-def far_kernel(rows_ref, keys_ref, values_ref, terms_ref, pool_ref, *refs):
+def far_kernel(rows_ref, keys_ref, values_ref, terms_ref, pool_ref, code_ref, *refs):
     count = (len(refs) - 3) // 2
-    mate = split_pool(pool_ref)
+    mate = split_pool(pool_ref, code_ref)
     pair_terms(rows_ref, (keys_ref[...], values_ref[...], terms_ref[...]), mate, refs[:count], refs[count : 2 * count])
     for ref, value in zip(refs[2 * count :], mate):
         ref[...] = value
@@ -429,15 +422,18 @@
     pages, page = key_variate.shape
     slots = pages * page
 
+    pool = kv_pool.reshape(slots, 2, cols)
+    pool2 = swap(pool, MATES)
+
     w3 = w_qkv.transpose(1, 0, 2)
-    msg, normed, bias, tok, pool = call(
+    msg, normed, bias, tok, pool, code = call(
         query_kernel,
         [
             shape(cols + AUX, rows), shape(rows, width), shape(8 * heads, rows, dtype=F32), shape(rows, width),
-            shape(slots + pages, 2, cols),
+            shape(slots, 2, cols), shape(pages, page, dtype=I32),
         ],
         node_len, tokens, norm_gain[None], w3, query_variate[None], path_nodes.T, head_bias, key_variate, page_table,
-        kv_pool.reshape(slots, 2, cols),
+        pool,
         away=range(1, 10),
         scratch=[
             pltpu.VMEM((1, width), F32), pltpu.VMEM((width, cols), BF16), pltpu.VMEM((1, rows), I32), pltpu.VMEM((3, rows), I32),
@@ -446,24 +442,22 @@
         ],
     )
     msgs = [msg] + [swap(msg, peer) for peer in PEERS]
-    pool2 = swap(pool, MATES)
-
-    key, value, keys, values_t, terms, w_own = call(
+    code2 = swap(code, MATES)
+
+    key, value, keys, values_t, terms = call(
         own_kernel,
         [
-            shape(cols, rows), shape(cols, rows), shape(slots, cols), shape(cols, slots), shape(slots, 128), shape(cols, width),
+            shape(cols, rows), shape(cols, rows), shape(slots, cols), shape(cols, slots), shape(slots, 128),
         ],
-        normed, w3, pool, w_out,
+        normed, w3, pool, code,
         flops=115300000,
-        away=(3,),
-        scratch=[pltpu.SemaphoreType.DMA],
-    )
-    w_far = across(w_own, 2)
+    )
+    w_far = across(w_out, 2)
     far = len(PEERS) - 1
     node = [shape(slots, cols), shape(cols, slots), shape(slots, 128)]
     message = shape(cols + AUX, rows)
     *far_out, keys2, values2, terms2 = call(
-        far_kernel, [message] * far + node, bias, keys, values_t, terms, pool2, *msgs[1 : 1 + far], flops=2306000000
+        far_kernel, [message] * far + node, bias, keys, values_t, terms, pool2, code2, *msgs[1 : 1 + far], flops=2306000000
     )
     own_out, near_out = call(
         near_kernel, [message] * 2, bias, keys, values_t, terms, keys2, values2, terms2, msgs[0], msgs[-1], flops=2306000000
@@ -472,12 +466,12 @@
     near_back = swap(near_out, PEERS[-1])
     acc, side = call(
         combine_far_kernel, [shape(cols, rows, dtype=F32), shape(2 * heads, rows, dtype=F32)],
-        bias, msg, key, value, *far_back,
+        bias, msg, key, value, own_out, *far_back,
         flops=4612000000,
     )
-    w_own, w_far, acc, near_back = lax.optimization_barrier((w_own, w_far, acc, near_back))
+    w_own, w_far, acc = lax.optimization_barrier((w_out, w_far, acc))
     w_near, w_last = across(w_own, 1), across(w_far, 1)
-    attn = call(combine_near_kernel, shape(rows, cols), acc, side, own_out, near_back, flops=115300000)
+    attn = call(combine_near_kernel, shape(rows, cols), acc, side, near_back, flops=4612000000)
     x_near, x_far, x_last = (across(attn, k) for k in (1, 2, 3))
     total = call(project_kernel, shape(rows, width, dtype=F32), tok, attn, x_near, w_own, w_near)
     return call(

time: 35.1 us -> 34.3 us (0.977)
  waiting for transfers between devices: 10 us -> 9.51 us
  Pallas kernels: 8.02 us -> 7.6 us
    ppermute x6, starting transfers between devices: 4.06 us -> 4.48 us  [across(): lax.ppermute(x, 'tp', [(t, t ^ mask) for t in range(lax.axis_size('tp'))])]
    pallas_call x8, Pallas kernels: 8.02 us -> 7.6 us  [call(): pl.pallas_call(kernel, out_shape=outs, scratch_shapes=scratch, in_specs=[...]
    ppermute x7 -> x8, waiting for transfers between devices: 6.43 us -> 6.06 us  [swap(): return lax.ppermute(x, ('seq', 'tp'), pairs)]
    ppermute x7 -> x8, starting transfers between devices: 11.9 us -> 11.8 us  [swap(): return lax.ppermute(x, ('seq', 'tp'), pairs)]
  transfers between devices with their start and end apart: 13 -> 14, of which waited for: 6 -> 6; matrix products, arithmetic and copies ran while one was open for 0% -> 0% of each run, Pallas kernels for 15% -> 19%
where the time goes in v6:
time: 34.3 us; the launch traced here: 34.2 us
  starting transfers between devices  16.3 us (48%)
  waiting for transfers between devices  9.51 us (28%)
  Pallas kernels  7.6 us (22%)
  between operations  0.75 us (2%)
    ppermute x8, starting transfers between devices, swap(): return lax.ppermute(x, ('seq', 'tp'), pairs)  11.8 us
    pallas_call x8, Pallas kernels, call(): pl.pallas_call(kernel, out_shape=outs, scratch_shapes=scratch, in_specs=[...  7.6 us
    ppermute x8, waiting for transfers between devices, swap(): return lax.ppermute(x, ('seq', 'tp'), pairs)  6.06 us
    ppermute x6, starting transfers between devices, across(): lax.ppermute(x, 'tp', [(t, t ^ mask) for t in range(lax.axis_size('tp'))])  4.48 us
    ppermute x6, waiting for transfers between devices, across(): lax.ppermute(x, 'tp', [(t, t ^ mask) for t in range(lax.axis_size('tp'))])  3.45 us
  transfers between devices with their start and end apart: 14, of which 6 were waited for; matrix products, arithmetic and copies ran while one was open for 0% of the time, Pallas kernels for 19%

profile of v6, /device:TPU:0, one launch (start us, length us, event | category | flops | bytes accessed | tf_op | source)
XLA Modules:
  0.0 34.2 jit_solution(3158454565364285939)
XLA Ops:
  0.0 0.0 copy-start
  0.0 3.0 %collective-permute-start.1 = (bf16[512,2,256]{2,1,0:T(2,128)(2,1)}, bf16[512,2,256]{2,1,0:T(2,128)(2,1)S(1)}, u32[]{:S(2)}, u32[]{:S(2)}) collective-permute-start(bf16[512,2,256]{2,1,0:T(2,128)(2,1)} %bitcast.7), channel_id=1, source_target_pairs={{0,4},{1,9},{2,6},{3,11},{4,0},{5,13},{6,2},{7,15},{8,12},{9,1},{1... | collective-permute-start | bytes 1572872 | tf_op jit(solution)/shard_map/ppermute | solution.py:399
  3.6 1.7 %shard_map.109 = (bf16[272,128]{1,0:T(8,128)(2,1)S(1)}, bf16[128,1024]{1,0:T(8,128)(2,1)S(1)}, f32[32,128]{1,0:T(8,128)S(1)}, bf16[128,1024]{1,0:T(8,128)(2,1)S(...) custom-call(s32[1]{0:T(128)S(6)} %copy.12.len_ref, bf16[128,1024]{1,0:T(8,128)(2,1)} %tok_hbm.1, ...), custom_call_target="tpu_custom_call" | custom-call | flops 1 | bytes 1 | tf_op jit(solution)/shard_map/pallas_call | solution.py:139
  5.3 0.0 copy-start.1
  5.3 2.7 %collective-permute-start.3 = (bf16[272,128]{1,0:T(8,128)(2,1)S(1)}, bf16[272,128]{1,0:T(8,128)(2,1)S(1)}, u32[]{:S(2)}, u32[]{:S(2)}) collective-permute-start(bf16[272,128]{1,0:T(8,128)(2,1)S(1)} %get-tuple-element.30.refs_6_.q_ref), channel_id=1, source_target_pairs={{0,16},{1,21},{2,18},{3,23},{4,20},{5,17},{6,22},{7,19},{8,24},{9,... | collective-permute-start | bytes 208904 | tf_op jit(solution)/shard_map/ppermute | solution.py:399
  8.0 1.3 %collective-permute-start.4 = (bf16[272,128]{1,0:T(8,128)(2,1)S(1)}, bf16[272,128]{1,0:T(8,128)(2,1)S(1)}, u32[]{:S(2)}, u32[]{:S(2)}) collective-permute-start(bf16[272,128]{1,0:T(8,128)(2,1)S(1)} %get-tuple-element.30.refs_6_.q_ref), channel_id=1, source_target_pairs={{0,24},{1,17},{2,26},{3,19},{4,28},{5,21},{6,30},{7,23},{8,16},{9,... | collective-permute-start | bytes 208904 | tf_op jit(solution)/shard_map/ppermute | solution.py:399
  9.3 0.2 collective-permute-start.5
  9.5 0.5 %collective-permute-start.2 = (s32[4,128]{1,0:T(4,128)S(1)}, s32[4,128]{1,0:T(4,128)S(1)}, u32[]{:S(2)}, u32[]{:S(2)}) collective-permute-start(s32[4,128]{1,0:T(4,128)S(1)} %get-tuple-element.33.code_ref), channel_id=1, source_target_pairs={{0,4},{1,9},{2,6},{3,11},{4,0},{5,13},{6,2},{7,15},{8,12},{9,1},{1... | collective-permute-start | bytes 6152 | tf_op jit(solution)/shard_map/ppermute | solution.py:399
  10.0 0.0 copy-done
  10.0 0.6 %shard_map.110 = (bf16[256,128]{1,0:T(8,128)(2,1)S(1)}, bf16[256,128]{1,0:T(8,128)(2,1)S(1)}, bf16[512,256]{1,0:T(8,128)(2,1)S(1)}, bf16[256,512]{1,0:T(8,128)(2,1)S(1)}, bf16[512,128]{1,0:T(8,128)(2,1)S(1)}) custom-call(bf16[128,1024]{1,0:T(8,128)(2,1)S(1)} %get-tuple-element.31.normed_ref, bf16[3,1024,256]{2,1,0:T(8,128)(2,1)S(1)} %bitcast.6, ...), custom_call_target="tpu_custom_call" | custom-call | flops 115300000 | bytes 1 | tf_op jit(solution)/shard_map/pallas_call | solution.py:139
  10.7 2.4 %collective-permute-done.2.code_ref = s32[4,128]{1,0:T(4,128)S(1)} collective-permute-done((s32[4,128]{1,0:T(4,128)S(1)}, s32[4,128]{1,0:T(4,128)S(1)}, u32[]{:S(2)}, u32[]{:S(2)}) %collective-permute-start.2) | collective-permute-done | bytes 2080 | tf_op jit(solution)/shard_map/ppermute | solution.py:399
  13.1 0.0 copy-done.1
  13.1 1.5 %collective-permute-start = (bf16[256,1024]{1,0:T(8,128)(2,1)S(1)}, bf16[256,1024]{1,0:T(8,128)(2,1)S(1)}, u32[]{:S(2)}, u32[]{:S(2)}) collective-permute-start(bf16[256,1024]{1,0:T(8,128)(2,1)S(1)} %copy-done.1), channel_id=1, source_target_pairs={{0,2},{1,3},{2,0},{3,1},{4,6},{5,7},{6,4},{7,5},{8,10},{9,11},{10,... | collective-permute-start | bytes 1572872 | tf_op jit(solution)/shard_map/ppermute | solution.py:403
  14.6 0.0 collective-permute-done.3.refs_0_
  14.6 0.2 collective-permute-done.4.refs_1_
  14.8 0.0 collective-permute-done.1.pool_ref
  14.8 2.0 %shard_map.111 = (bf16[272,128]{1,0:T(8,128)(2,1)S(1)}, bf16[272,128]{1,0:T(8,128)(2,1)S(1)}, bf16[512,256]{1,0:T(8,128)(2,1)S(1)}, bf16[256,512]{1,0:T(8,128)(2,1)S(1)}, bf16[512,128]{1,0:T(8,128)(2,1)S(1)}) custom-call(f32[32,128]{1,0:T(8,128)S(1)} %get-tuple-element.29.rows_ref, bf16[512,256]{1,0:T(8,128)(2,1)S(1)} %get-tuple-element.36.keys_ref.refs_0_, ...), custom_call_target="tpu_custom_call" | custom-call | flops 2305999872 | bytes 1 | tf_op jit(solution)/shard_map/pallas_call | solution.py:139
  16.8 2.7 %collective-permute-start.6 = (bf16[272,128]{1,0:T(8,128)(2,1)S(1)}, bf16[272,128]{1,0:T(8,128)(2,1)S(1)}, u32[]{:S(2)}, u32[]{:S(2)}) collective-permute-start(bf16[272,128]{1,0:T(8,128)(2,1)S(1)} %get-tuple-element.43), channel_id=1, source_target_pairs={{0,16},{1,21},{2,18},{3,23},{4,20},{5,17},{6,22},{7,19},{8,24},{9,... | collective-permute-start | bytes 208904 | tf_op jit(solution)/shard_map/ppermute | solution.py:399
  19.5 1.4 %collective-permute-start.7 = (bf16[272,128]{1,0:T(8,128)(2,1)S(1)}, bf16[272,128]{1,0:T(8,128)(2,1)S(1)}, u32[]{:S(2)}, u32[]{:S(2)}) collective-permute-start(bf16[272,128]{1,0:T(8,128)(2,1)S(1)} %get-tuple-element.44), channel_id=1, source_target_pairs={{0,24},{1,17},{2,26},{3,19},{4,28},{5,21},{6,30},{7,23},{8,16},{9,... | collective-permute-start | bytes 208904 | tf_op jit(solution)/shard_map/ppermute | solution.py:399
  20.9 0.0 collective-permute-done.5.refs_7_
  20.9 1.7 %shard_map.112 = (bf16[272,128]{1,0:T(8,128)(2,1)S(1)}, bf16[272,128]{1,0:T(8,128)(2,1)S(1)}) custom-call(f32[32,128]{1,0:T(8,128)S(1)} %get-tuple-element.29.rows_ref, bf16[512,256]{1,0:T(8,128)(2,1)S(1)} %get-tuple-element.36.keys_ref.refs_0_, bf16[256,512]{1,0:T(8,128)(2,1)S(1)} %get-tuple-element.37.values_ref.refs_1_, ...), custom_call_target="tpu_custom_call" | custom-call | flops 2305999872 | bytes 1 | tf_op jit(solution)/shard_map/pallas_call | solution.py:139
  22.6 0.1 collective-permute-start.8
  22.7 0.0 collective-permute-done.6.refs_1_
  22.7 3.1 %collective-permute-done.7.refs_2_ = bf16[272,128]{1,0:T(8,128)(2,1)S(1)} collective-permute-done((bf16[272,128]{1,0:T(8,128)(2,1)S(1)}, bf16[272,128]{1,0:T(8,128)(2,1)S(1)}, u32[]{:S(2)}, u32[]{:S(2)}) %collective-permute-start.7) | collective-permute-done | bytes 69664 | tf_op jit(solution)/shard_map/ppermute | solution.py:399
  25.9 0.1 shard_map.113
  26.0 0.0 collective-permute-done.refs_2_
  26.0 1.0 %collective-permute-start.10 = (bf16[256,1024]{1,0:T(8,128)(2,1)S(1)}, bf16[256,1024]{1,0:T(8,128)(2,1)S(1)}, u32[]{:S(2)}, u32[]{:S(2)}) collective-permute-start(bf16[256,1024]{1,0:T(8,128)(2,1)S(1)} %copy-done.1), channel_id=1, source_target_pairs={{0,1},{1,0},{2,3},{3,2},{4,5},{5,4},{6,7},{7,6},{8,9},{9,8},{10,11... | collective-permute-start | bytes 1572872 | tf_op jit(solution)/shard_map/ppermute | solution.py:403
  27.0 0.1 collective-permute-start.13
  27.0 0.3 collective-permute-done.8.refs_0_
  27.3 0.1 shard_map.114.refs_0_
  27.5 0.2 collective-permute-start.9
  27.7 1.1 %collective-permute-start.11 = (bf16[128,256]{1,0:T(8,128)(2,1)S(1)}, bf16[128,256]{1,0:T(8,128)(2,1)S(1)}, u32[]{:S(2)}, u32[]{:S(2)}) collective-permute-start(bf16[128,256]{1,0:T(8,128)(2,1)S(1)} %shard_map.114.refs_0_), channel_id=1, source_target_pairs={{0,2},{1,3},{2,0},{3,1},{4,6},{5,7},{6,4},{7,5},{8,10},{9,11},{10,... | collective-permute-start | bytes 196616 | tf_op jit(solution)/shard_map/ppermute | solution.py:403
  28.8 0.6 %collective-permute-start.12 = (bf16[128,256]{1,0:T(8,128)(2,1)S(1)}, bf16[128,256]{1,0:T(8,128)(2,1)S(1)}, u32[]{:S(2)}, u32[]{:S(2)}) collective-permute-start(bf16[128,256]{1,0:T(8,128)(2,1)S(1)} %shard_map.114.refs_0_), channel_id=1, source_target_pairs={{0,3},{1,2},{2,1},{3,0},{4,7},{5,6},{6,5},{7,4},{8,11},{9,10},{10,... | collective-permute-start | bytes 196616 | tf_op jit(solution)/shard_map/ppermute | solution.py:403
  29.4 0.0 collective-permute-done.9.refs_1_
  29.4 0.0 collective-permute-done.10.refs_3_
  29.4 0.3 shard_map.115.base_ref
  29.7 2.6 %collective-permute-done.11.refs_0_ = bf16[128,256]{1,0:T(8,128)(2,1)S(1)} collective-permute-done((bf16[128,256]{1,0:T(8,128)(2,1)S(1)}, bf16[128,256]{1,0:T(8,128)(2,1)S(1)}, u32[]{:S(2)}, u32[]{:S(2)}) %collective-permute-start.11) | collective-permute-done | bytes 65568 | tf_op jit(solution)/shard_map/ppermute | solution.py:403
  32.3 0.8 %collective-permute-done.12.refs_1_ = bf16[128,256]{1,0:T(8,128)(2,1)S(1)} collective-permute-done((bf16[128,256]{1,0:T(8,128)(2,1)S(1)}, bf16[128,256]{1,0:T(8,128)(2,1)S(1)}, u32[]{:S(2)}, u32[]{:S(2)}) %collective-permute-start.12) | collective-permute-done | bytes 65568 | tf_op jit(solution)/shard_map/ppermute | solution.py:403
  33.2 0.0 collective-permute-done.13.refs_3_
  33.2 1.0 %shard_map.116 = bf16[128,1024]{1,0:T(8,128)(2,1)} custom-call(f32[128,1024]{1,0:T(8,128)S(1)} %shard_map.115.base_ref, bf16[128,256]{1,0:T(8,128)(2,1)S(1)} %collective-permute-done.11.refs_0_, bf16[128,256]{1,0:T(8,128)(2,1)S(1)} %collective-permute-done.12.refs_1_, bf16[256,1024]{1,0:T(8,128)(2,1)S(1)} %collective-permute-done.refs_2_, ...), custom_call_target="tpu_custom_call" | custom-call | flops 1 | bytes 1 | tf_op jit(solution)/shard_map/pallas_call | solution.py:139
Async XLA Ops:
  0.0 10.0 %copy-start = (bf16[1024,3,256]{2,0,1:T(8,128)(2,1)S(1)}, bf16[1024,3,256]{2,0,1:T(8,128)(2,1)}, u32[]{:S(2)}) copy-start(bf16[1024,3,256]{2,0,1:T(8,128)(2,1)} %param.13) | copy-start | bytes 4718596
  0.0 14.8 %collective-permute-start.1 = (bf16[512,2,256]{2,1,0:T(2,128)(2,1)}, bf16[512,2,256]{2,1,0:T(2,128)(2,1)S(1)}, u32[]{:S(2)}, u32[]{:S(2)}) collective-permute-start(bf16[512,2,256]{2,1,0:T(2,128)(2,1)} %bitcast.7), channel_id=1, source_target_pairs={{0,4},{1,9},{2,6},{3,11},{4,0},{5,13},{6,2},{7,15},{8,12},{9,1},{1... | collective-permute-start | bytes 1572872 | tf_op jit(solution)/shard_map/ppermute | solution.py:399
  5.3 7.8 %copy-start.1 = (bf16[256,1024]{1,0:T(8,128)(2,1)S(1)}, bf16[256,1024]{1,0:T(8,128)(2,1)}, u32[]{:S(2)}) copy-start(bf16[256,1024]{1,0:T(8,128)(2,1)} %refs_2_) | copy-start | bytes 1572868
  5.3 9.3 %collective-permute-start.3 = (bf16[272,128]{1,0:T(8,128)(2,1)S(1)}, bf16[272,128]{1,0:T(8,128)(2,1)S(1)}, u32[]{:S(2)}, u32[]{:S(2)}) collective-permute-start(bf16[272,128]{1,0:T(8,128)(2,1)S(1)} %get-tuple-element.30.refs_6_.q_ref), channel_id=1, source_target_pairs={{0,16},{1,21},{2,18},{3,23},{4,20},{5,17},{6,22},{7,19},{8,24},{9,... | collective-permute-start | bytes 208904 | tf_op jit(solution)/shard_map/ppermute | solution.py:399
  8.0 6.9 %collective-permute-start.4 = (bf16[272,128]{1,0:T(8,128)(2,1)S(1)}, bf16[272,128]{1,0:T(8,128)(2,1)S(1)}, u32[]{:S(2)}, u32[]{:S(2)}) collective-permute-start(bf16[272,128]{1,0:T(8,128)(2,1)S(1)} %get-tuple-element.30.refs_6_.q_ref), channel_id=1, source_target_pairs={{0,24},{1,17},{2,26},{3,19},{4,28},{5,21},{6,30},{7,23},{8,16},{9,... | collective-permute-start | bytes 208904 | tf_op jit(solution)/shard_map/ppermute | solution.py:399
  9.3 11.6 %collective-permute-start.5 = (bf16[272,128]{1,0:T(8,128)(2,1)S(1)}, bf16[272,128]{1,0:T(8,128)(2,1)S(1)}, u32[]{:S(2)}, u32[]{:S(2)}) collective-permute-start(bf16[272,128]{1,0:T(8,128)(2,1)S(1)} %get-tuple-element.30.refs_6_.q_ref), channel_id=1, source_target_pairs={{0,8},{1,5},{2,10},{3,7},{4,12},{5,1},{6,14},{7,3},{8,0},{9,13},{1... | collective-permute-start | bytes 208904 | tf_op jit(solution)/shard_map/ppermute | solution.py:399
  9.5 3.6 %collective-permute-start.2 = (s32[4,128]{1,0:T(4,128)S(1)}, s32[4,128]{1,0:T(4,128)S(1)}, u32[]{:S(2)}, u32[]{:S(2)}) collective-permute-start(s32[4,128]{1,0:T(4,128)S(1)} %get-tuple-element.33.code_ref), channel_id=1, source_target_pairs={{0,4},{1,9},{2,6},{3,11},{4,0},{5,13},{6,2},{7,15},{8,12},{9,1},{1... | collective-permute-start | bytes 6152 | tf_op jit(solution)/shard_map/ppermute | solution.py:399
  13.1 12.9 %collective-permute-start = (bf16[256,1024]{1,0:T(8,128)(2,1)S(1)}, bf16[256,1024]{1,0:T(8,128)(2,1)S(1)}, u32[]{:S(2)}, u32[]{:S(2)}) collective-permute-start(bf16[256,1024]{1,0:T(8,128)(2,1)S(1)} %copy-done.1), channel_id=1, source_target_pairs={{0,2},{1,3},{2,0},{3,1},{4,6},{5,7},{6,4},{7,5},{8,10},{9,11},{10,... | collective-permute-start | bytes 1572872 | tf_op jit(solution)/shard_map/ppermute | solution.py:403
  16.8 5.9 %collective-permute-start.6 = (bf16[272,128]{1,0:T(8,128)(2,1)S(1)}, bf16[272,128]{1,0:T(8,128)(2,1)S(1)}, u32[]{:S(2)}, u32[]{:S(2)}) collective-permute-start(bf16[272,128]{1,0:T(8,128)(2,1)S(1)} %get-tuple-element.43), channel_id=1, source_target_pairs={{0,16},{1,21},{2,18},{3,23},{4,20},{5,17},{6,22},{7,19},{8,24},{9,... | collective-permute-start | bytes 208904 | tf_op jit(solution)/shard_map/ppermute | solution.py:399
  19.5 6.3 %collective-permute-start.7 = (bf16[272,128]{1,0:T(8,128)(2,1)S(1)}, bf16[272,128]{1,0:T(8,128)(2,1)S(1)}, u32[]{:S(2)}, u32[]{:S(2)}) collective-permute-start(bf16[272,128]{1,0:T(8,128)(2,1)S(1)} %get-tuple-element.44), channel_id=1, source_target_pairs={{0,24},{1,17},{2,26},{3,19},{4,28},{5,21},{6,30},{7,23},{8,16},{9,... | collective-permute-start | bytes 208904 | tf_op jit(solution)/shard_map/ppermute | solution.py:399
  22.6 4.7 %collective-permute-start.8 = (bf16[272,128]{1,0:T(8,128)(2,1)S(1)}, bf16[272,128]{1,0:T(8,128)(2,1)S(1)}, u32[]{:S(2)}, u32[]{:S(2)}) collective-permute-start(bf16[272,128]{1,0:T(8,128)(2,1)S(1)} %get-tuple-element.48), channel_id=1, source_target_pairs={{0,8},{1,5},{2,10},{3,7},{4,12},{5,1},{6,14},{7,3},{8,0},{9,13},{1... | collective-permute-start | bytes 208904 | tf_op jit(solution)/shard_map/ppermute | solution.py:399
  26.0 3.4 %collective-permute-start.10 = (bf16[256,1024]{1,0:T(8,128)(2,1)S(1)}, bf16[256,1024]{1,0:T(8,128)(2,1)S(1)}, u32[]{:S(2)}, u32[]{:S(2)}) collective-permute-start(bf16[256,1024]{1,0:T(8,128)(2,1)S(1)} %copy-done.1), channel_id=1, source_target_pairs={{0,1},{1,0},{2,3},{3,2},{4,5},{5,4},{6,7},{7,6},{8,9},{9,8},{10,11... | collective-permute-start | bytes 1572872 | tf_op jit(solution)/shard_map/ppermute | solution.py:403
  27.0 6.2 %collective-permute-start.13 = (bf16[256,1024]{1,0:T(8,128)(2,1)S(1)}, bf16[256,1024]{1,0:T(8,128)(2,1)S(1)}, u32[]{:S(2)}, u32[]{:S(2)}) collective-permute-start(bf16[256,1024]{1,0:T(8,128)(2,1)S(1)} %collective-permute-done.refs_2_), channel_id=1, source_target_pairs={{0,1},{1,0},{2,3},{3,2},{4,5},{5,4},{6,7},{7,6},{8,9},{9,8},{10,11... | collective-permute-start | bytes 1572872 | tf_op jit(solution)/shard_map/ppermute | solution.py:403
  27.5 1.9 %collective-permute-start.9 = (bf16[128,256]{1,0:T(8,128)(2,1)S(1)}, bf16[128,256]{1,0:T(8,128)(2,1)S(1)}, u32[]{:S(2)}, u32[]{:S(2)}) collective-permute-start(bf16[128,256]{1,0:T(8,128)(2,1)S(1)} %shard_map.114.refs_0_), channel_id=1, source_target_pairs={{0,1},{1,0},{2,3},{3,2},{4,5},{5,4},{6,7},{7,6},{8,9},{9,8},{10,11... | collective-permute-start | bytes 196616 | tf_op jit(solution)/shard_map/ppermute | solution.py:403
  27.7 4.6 %collective-permute-start.11 = (bf16[128,256]{1,0:T(8,128)(2,1)S(1)}, bf16[128,256]{1,0:T(8,128)(2,1)S(1)}, u32[]{:S(2)}, u32[]{:S(2)}) collective-permute-start(bf16[128,256]{1,0:T(8,128)(2,1)S(1)} %shard_map.114.refs_0_), channel_id=1, source_target_pairs={{0,2},{1,3},{2,0},{3,1},{4,6},{5,7},{6,4},{7,5},{8,10},{9,11},{10,... | collective-permute-start | bytes 196616 | tf_op jit(solution)/shard_map/ppermute | solution.py:403
  28.8 4.3 %collective-permute-start.12 = (bf16[128,256]{1,0:T(8,128)(2,1)S(1)}, bf16[128,256]{1,0:T(8,128)(2,1)S(1)}, u32[]{:S(2)}, u32[]{:S(2)}) collective-permute-start(bf16[128,256]{1,0:T(8,128)(2,1)S(1)} %shard_map.114.refs_0_), channel_id=1, source_target_pairs={{0,3},{1,2},{2,1},{3,0},{4,7},{5,6},{6,5},{7,4},{8,11},{9,10},{10,... | collective-permute-start | bytes 196616 | tf_op jit(solution)/shard_map/ppermute | solution.py:403

commit v7 on v6

--- a/solution.py
+++ b/solution.py
@@ -159,14 +159,14 @@
 
 
 def query_kernel(
-    len_ref, tok_hbm, gain_hbm, w_hbm, variate_hbm, path_hbm, bias_hbm, slot_hbm, table_hbm, pool_hbm,
-    msg_ref, normed_ref, rows_ref, tok_ref, pool_ref, code_ref,
+    len_ref, tok_hbm, gain_hbm, w_hbm, variate_hbm, path_hbm, bias_hbm, slot_hbm, table_hbm,
+    msg_ref, normed_ref, rows_ref, tok_ref, code_ref,
     gain_ref, w_ref, variate_ref, path_ref, bias_ref, slot_ref, table_ref, sems,
 ):
     pages, page = slot_ref.shape
     copies = fetch(
         sems, (tok_hbm, tok_ref), (w_hbm.at[0], w_ref), (gain_hbm, gain_ref), (variate_hbm, variate_ref), (path_hbm, path_ref),
-        (bias_hbm, bias_ref), (slot_hbm, slot_ref), (table_hbm, table_ref), (pool_hbm, pool_ref),
+        (bias_hbm, bias_ref), (slot_hbm, slot_ref), (table_hbm, table_ref),
     )
     for copy in copies[2:8]:
         copy.wait()
@@ -190,7 +190,6 @@
     copies[1].wait()
     q = jnp.dot(normed, w_ref[...], preferred_element_type=F32).astype(BF16)
     msg_ref[:cols, :] = (q.astype(F32) * HD ** (-0.5)).T.astype(BF16)
-    copies[8].wait()
 
 
 def split3(x):
@@ -278,10 +277,13 @@
     return q, aux
 
 
-def own_kernel(normed_ref, w_ref, pool_ref, code_ref, k_ref, v_ref, keys_ref, values_ref, terms_ref):
+def own_kernel(normed_ref, w_ref, pool_hbm, code_ref, k_ref, v_ref, keys_ref, values_ref, terms_ref, pool_ref, sem):
+    copy = pltpu.make_async_copy(pool_hbm, pool_ref, sem)
+    copy.start()
     for i, own_ref in ((1, k_ref), (2, v_ref)):
         own = jnp.dot(normed_ref[...], w_ref[i], preferred_element_type=F32).astype(BF16)
         own_ref[...] = own.astype(F32).T.astype(BF16)
+    copy.wait()
     keys_ref[...], values_ref[...], terms_ref[...] = split_pool(pool_ref, code_ref)
 
 
@@ -426,19 +428,18 @@
     pool2 = swap(pool, MATES)
 
     w3 = w_qkv.transpose(1, 0, 2)
-    msg, normed, bias, tok, pool, code = call(
+    msg, normed, bias, tok, code = call(
         query_kernel,
         [
             shape(cols + AUX, rows), shape(rows, width), shape(8 * heads, rows, dtype=F32), shape(rows, width),
-            shape(slots, 2, cols), shape(pages, page, dtype=I32),
+            shape(pages, page, dtype=I32),
         ],
         node_len, tokens, norm_gain[None], w3, query_variate[None], path_nodes.T, head_bias, key_variate, page_table,
-        pool,
-        away=range(1, 10),
+        away=range(1, 9),
         scratch=[
             pltpu.VMEM((1, width), F32), pltpu.VMEM((width, cols), BF16), pltpu.VMEM((1, rows), I32), pltpu.VMEM((3, rows), I32),
             pltpu.VMEM((2, heads), F32), pltpu.VMEM((pages, page), I32), pltpu.SMEM((1, pages), I32),
-            pltpu.SemaphoreType.DMA((9,)),
+            pltpu.SemaphoreType.DMA((8,)),
         ],
     )
     msgs = [msg] + [swap(msg, peer) for peer in PEERS]
@@ -451,6 +452,8 @@
         ],
         normed, w3, pool, code,
         flops=115300000,
+        away=(2,),
+        scratch=[pltpu.VMEM((slots, 2, cols), BF16), pltpu.SemaphoreType.DMA],
     )
     w_far = across(w_out, 2)
     far = len(PEERS) - 1

time: 34.3 us -> 34.4 us (level)
  Pallas kernels: 7.6 us -> 8.67 us
  waiting for transfers between devices: 9.51 us -> 8.46 us
    pallas_call x8, Pallas kernels: 7.6 us -> 8.67 us  [call(): pl.pallas_call(kernel, out_shape=outs, scratch_shapes=scratch, in_specs=[...]
    ppermute x8, waiting for transfers between devices: 6.06 us -> 5 us  [swap(): return lax.ppermute(x, ('seq', 'tp'), pairs)]
  transfers between devices with their start and end apart: 14 -> 14, of which waited for: 6 -> 6; matrix products, arithmetic and copies ran while one was open for 0% -> 0% of each run, Pallas kernels for 19% -> 22%
where the time goes in v7:
time: 34.4 us; the launch traced here: 34.2 us
  starting transfers between devices  16.3 us (47%)
  Pallas kernels  8.67 us (25%)
  waiting for transfers between devices  8.46 us (25%)
  between operations  0.75 us (2%)
    ppermute x8, starting transfers between devices, swap(): return lax.ppermute(x, ('seq', 'tp'), pairs)  11.8 us
    pallas_call x8, Pallas kernels, call(): pl.pallas_call(kernel, out_shape=outs, scratch_shapes=scratch, in_specs=[...  8.67 us
    ppermute x8, waiting for transfers between devices, swap(): return lax.ppermute(x, ('seq', 'tp'), pairs)  5 us
    ppermute x6, starting transfers between devices, across(): lax.ppermute(x, 'tp', [(t, t ^ mask) for t in range(lax.axis_size('tp'))])  4.48 us
    ppermute x6, waiting for transfers between devices, across(): lax.ppermute(x, 'tp', [(t, t ^ mask) for t in range(lax.axis_size('tp'))])  3.46 us
  transfers between devices with their start and end apart: 14, of which 6 were waited for; matrix products, arithmetic and copies ran while one was open for 0% of the time, Pallas kernels for 22%

profile of v7, /device:TPU:0, one launch (start us, length us, event | category | flops | bytes accessed | tf_op | source)
XLA Modules:
  0.0 34.2 jit_solution(12860531909758883951)
XLA Ops:
  0.0 0.0 copy-start
  0.0 3.0 %collective-permute-start.1 = (bf16[512,2,256]{2,1,0:T(2,128)(2,1)}, bf16[512,2,256]{2,1,0:T(2,128)(2,1)S(1)}, u32[]{:S(2)}, u32[]{:S(2)}) collective-permute-start(bf16[512,2,256]{2,1,0:T(2,128)(2,1)} %bitcast.7), channel_id=1, source_target_pairs={{0,4},{1,9},{2,6},{3,11},{4,0},{5,13},{6,2},{7,15},{8,12},{9,1},{1... | collective-permute-start | bytes 1572872 | tf_op jit(solution)/shard_map/ppermute | solution.py:401
  3.6 1.6 %shard_map.109 = (bf16[272,128]{1,0:T(8,128)(2,1)S(1)}, bf16[128,1024]{1,0:T(8,128)(2,1)S(1)}, f32[32,128]{1,0:T(8,128)S(1)}, bf16[128,1024]{1,0:T(8,128)(2,1)S(1)}, s32[4,128]{1,0:T(4,128)S(1)}) custom-call(s32[1]{0:T(128)S(6)} %copy.12.len_ref, bf16[128,1024]{1,0:T(8,128)(2,1)} %tok_hbm.1, f32[1,1024]{1,0:T(1,128)} %bitcast.9, ...), custom_call_target="tpu_custom_call" | custom-call | flops 1 | bytes 1 | tf_op jit(solution)/shard_map/pallas_call | solution.py:139
  5.3 0.0 copy-start.1
  5.3 2.7 %collective-permute-start.3 = (bf16[272,128]{1,0:T(8,128)(2,1)S(1)}, bf16[272,128]{1,0:T(8,128)(2,1)S(1)}, u32[]{:S(2)}, u32[]{:S(2)}) collective-permute-start(bf16[272,128]{1,0:T(8,128)(2,1)S(1)} %get-tuple-element.29.refs_6_.q_ref), channel_id=1, source_target_pairs={{0,16},{1,21},{2,18},{3,23},{4,20},{5,17},{6,22},{7,19},{8,24},{9,... | collective-permute-start | bytes 208904 | tf_op jit(solution)/shard_map/ppermute | solution.py:401
  7.9 1.3 %collective-permute-start.4 = (bf16[272,128]{1,0:T(8,128)(2,1)S(1)}, bf16[272,128]{1,0:T(8,128)(2,1)S(1)}, u32[]{:S(2)}, u32[]{:S(2)}) collective-permute-start(bf16[272,128]{1,0:T(8,128)(2,1)S(1)} %get-tuple-element.29.refs_6_.q_ref), channel_id=1, source_target_pairs={{0,24},{1,17},{2,26},{3,19},{4,28},{5,21},{6,30},{7,23},{8,16},{9,... | collective-permute-start | bytes 208904 | tf_op jit(solution)/shard_map/ppermute | solution.py:401
  9.3 0.2 collective-permute-start.5
  9.5 0.5 %collective-permute-start.2 = (s32[4,128]{1,0:T(4,128)S(1)}, s32[4,128]{1,0:T(4,128)S(1)}, u32[]{:S(2)}, u32[]{:S(2)}) collective-permute-start(s32[4,128]{1,0:T(4,128)S(1)} %get-tuple-element.31.code_ref), channel_id=1, source_target_pairs={{0,4},{1,9},{2,6},{3,11},{4,0},{5,13},{6,2},{7,15},{8,12},{9,1},{1... | collective-permute-start | bytes 6152 | tf_op jit(solution)/shard_map/ppermute | solution.py:401
  10.0 0.0 copy-done
  10.0 1.7 %shard_map.110 = (bf16[256,128]{1,0:T(8,128)(2,1)S(1)}, bf16[256,128]{1,0:T(8,128)(2,1)S(1)}, bf16[512,256]{1,0:T(8,128)(2,1)S(1)}, bf16[256,512]{1,0:T(8,128)(2,1)S(1)}, bf16[512,128]{1,0:T(8,128)(2,1)S(1)}) custom-call(bf16[128,1024]{1,0:T(8,128)(2,1)S(1)} %get-tuple-element.30.normed_ref, bf16[3,1024,256]{2,1,0:T(8,128)(2,1)S(1)} %bitcast.6, ...), custom_call_target="tpu_custom_call" | custom-call | flops 115300000 | bytes 1 | tf_op jit(solution)/shard_map/pallas_call | solution.py:139
  11.7 1.4 %collective-permute-done.2.code_ref = s32[4,128]{1,0:T(4,128)S(1)} collective-permute-done((s32[4,128]{1,0:T(4,128)S(1)}, s32[4,128]{1,0:T(4,128)S(1)}, u32[]{:S(2)}, u32[]{:S(2)}) %collective-permute-start.2) | collective-permute-done | bytes 2080 | tf_op jit(solution)/shard_map/ppermute | solution.py:401
  13.1 0.0 copy-done.1
  13.1 1.5 %collective-permute-start = (bf16[256,1024]{1,0:T(8,128)(2,1)S(1)}, bf16[256,1024]{1,0:T(8,128)(2,1)S(1)}, u32[]{:S(2)}, u32[]{:S(2)}) collective-permute-start(bf16[256,1024]{1,0:T(8,128)(2,1)S(1)} %copy-done.1), channel_id=1, source_target_pairs={{0,2},{1,3},{2,0},{3,1},{4,6},{5,7},{6,4},{7,5},{8,10},{9,11},{10,... | collective-permute-start | bytes 1572872 | tf_op jit(solution)/shard_map/ppermute | solution.py:405
  14.6 0.0 collective-permute-done.3.refs_0_
  14.6 0.2 collective-permute-done.4.refs_1_
  14.8 0.0 collective-permute-done.1.pool_ref
  14.8 2.0 %shard_map.111 = (bf16[272,128]{1,0:T(8,128)(2,1)S(1)}, bf16[272,128]{1,0:T(8,128)(2,1)S(1)}, bf16[512,256]{1,0:T(8,128)(2,1)S(1)}, bf16[256,512]{1,0:T(8,128)(2,1)S(1)}, bf16[512,128]{1,0:T(8,128)(2,1)S(1)}) custom-call(f32[32,128]{1,0:T(8,128)S(1)} %get-tuple-element.28.rows_ref, bf16[512,256]{1,0:T(8,128)(2,1)S(1)} %get-tuple-element.34.keys_ref.refs_0_, ...), custom_call_target="tpu_custom_call" | custom-call | flops 2305999872 | bytes 1 | tf_op jit(solution)/shard_map/pallas_call | solution.py:139
  16.9 2.7 %collective-permute-start.6 = (bf16[272,128]{1,0:T(8,128)(2,1)S(1)}, bf16[272,128]{1,0:T(8,128)(2,1)S(1)}, u32[]{:S(2)}, u32[]{:S(2)}) collective-permute-start(bf16[272,128]{1,0:T(8,128)(2,1)S(1)} %get-tuple-element.41), channel_id=1, source_target_pairs={{0,16},{1,21},{2,18},{3,23},{4,20},{5,17},{6,22},{7,19},{8,24},{9,... | collective-permute-start | bytes 208904 | tf_op jit(solution)/shard_map/ppermute | solution.py:401
  19.5 1.4 %collective-permute-start.7 = (bf16[272,128]{1,0:T(8,128)(2,1)S(1)}, bf16[272,128]{1,0:T(8,128)(2,1)S(1)}, u32[]{:S(2)}, u32[]{:S(2)}) collective-permute-start(bf16[272,128]{1,0:T(8,128)(2,1)S(1)} %get-tuple-element.42), channel_id=1, source_target_pairs={{0,24},{1,17},{2,26},{3,19},{4,28},{5,21},{6,30},{7,23},{8,16},{9,... | collective-permute-start | bytes 208904 | tf_op jit(solution)/shard_map/ppermute | solution.py:401
  20.9 0.0 collective-permute-done.5.refs_7_
  20.9 1.8 %shard_map.112 = (bf16[272,128]{1,0:T(8,128)(2,1)S(1)}, bf16[272,128]{1,0:T(8,128)(2,1)S(1)}) custom-call(f32[32,128]{1,0:T(8,128)S(1)} %get-tuple-element.28.rows_ref, bf16[512,256]{1,0:T(8,128)(2,1)S(1)} %get-tuple-element.34.keys_ref.refs_0_, bf16[256,512]{1,0:T(8,128)(2,1)S(1)} %get-tuple-element.35.values_ref.refs_1_, ...), custom_call_target="tpu_custom_call" | custom-call | flops 2305999872 | bytes 1 | tf_op jit(solution)/shard_map/pallas_call | solution.py:139
  22.6 0.1 collective-permute-start.8
  22.7 0.0 collective-permute-done.6.refs_1_
  22.7 3.1 %collective-permute-done.7.refs_2_ = bf16[272,128]{1,0:T(8,128)(2,1)S(1)} collective-permute-done((bf16[272,128]{1,0:T(8,128)(2,1)S(1)}, bf16[272,128]{1,0:T(8,128)(2,1)S(1)}, u32[]{:S(2)}, u32[]{:S(2)}) %collective-permute-start.7) | collective-permute-done | bytes 69664 | tf_op jit(solution)/shard_map/ppermute | solution.py:401
  25.9 0.1 shard_map.113
  26.0 0.0 collective-permute-done.refs_2_
  26.0 1.0 %collective-permute-start.10 = (bf16[256,1024]{1,0:T(8,128)(2,1)S(1)}, bf16[256,1024]{1,0:T(8,128)(2,1)S(1)}, u32[]{:S(2)}, u32[]{:S(2)}) collective-permute-start(bf16[256,1024]{1,0:T(8,128)(2,1)S(1)} %copy-done.1), channel_id=1, source_target_pairs={{0,1},{1,0},{2,3},{3,2},{4,5},{5,4},{6,7},{7,6},{8,9},{9,8},{10,11... | collective-permute-start | bytes 1572872 | tf_op jit(solution)/shard_map/ppermute | solution.py:405
  27.0 0.1 collective-permute-start.13
  27.1 0.3 collective-permute-done.8.refs_0_
  27.3 0.1 shard_map.114.refs_0_
  27.5 0.2 collective-permute-start.9
  27.7 1.1 %collective-permute-start.11 = (bf16[128,256]{1,0:T(8,128)(2,1)S(1)}, bf16[128,256]{1,0:T(8,128)(2,1)S(1)}, u32[]{:S(2)}, u32[]{:S(2)}) collective-permute-start(bf16[128,256]{1,0:T(8,128)(2,1)S(1)} %shard_map.114.refs_0_), channel_id=1, source_target_pairs={{0,2},{1,3},{2,0},{3,1},{4,6},{5,7},{6,4},{7,5},{8,10},{9,11},{10,... | collective-permute-start | bytes 196616 | tf_op jit(solution)/shard_map/ppermute | solution.py:405
  28.8 0.6 %collective-permute-start.12 = (bf16[128,256]{1,0:T(8,128)(2,1)S(1)}, bf16[128,256]{1,0:T(8,128)(2,1)S(1)}, u32[]{:S(2)}, u32[]{:S(2)}) collective-permute-start(bf16[128,256]{1,0:T(8,128)(2,1)S(1)} %shard_map.114.refs_0_), channel_id=1, source_target_pairs={{0,3},{1,2},{2,1},{3,0},{4,7},{5,6},{6,5},{7,4},{8,11},{9,10},{10,... | collective-permute-start | bytes 196616 | tf_op jit(solution)/shard_map/ppermute | solution.py:405
  29.4 0.0 collective-permute-done.9.refs_1_
  29.4 0.0 collective-permute-done.10.refs_3_
  29.4 0.3 shard_map.115.base_ref
  29.7 2.6 %collective-permute-done.11.refs_0_ = bf16[128,256]{1,0:T(8,128)(2,1)S(1)} collective-permute-done((bf16[128,256]{1,0:T(8,128)(2,1)S(1)}, bf16[128,256]{1,0:T(8,128)(2,1)S(1)}, u32[]{:S(2)}, u32[]{:S(2)}) %collective-permute-start.11) | collective-permute-done | bytes 65568 | tf_op jit(solution)/shard_map/ppermute | solution.py:405
  32.3 0.8 %collective-permute-done.12.refs_1_ = bf16[128,256]{1,0:T(8,128)(2,1)S(1)} collective-permute-done((bf16[128,256]{1,0:T(8,128)(2,1)S(1)}, bf16[128,256]{1,0:T(8,128)(2,1)S(1)}, u32[]{:S(2)}, u32[]{:S(2)}) %collective-permute-start.12) | collective-permute-done | bytes 65568 | tf_op jit(solution)/shard_map/ppermute | solution.py:405
  33.2 0.0 collective-permute-done.13.refs_3_
  33.2 1.0 %shard_map.116 = bf16[128,1024]{1,0:T(8,128)(2,1)} custom-call(f32[128,1024]{1,0:T(8,128)S(1)} %shard_map.115.base_ref, bf16[128,256]{1,0:T(8,128)(2,1)S(1)} %collective-permute-done.11.refs_0_, bf16[128,256]{1,0:T(8,128)(2,1)S(1)} %collective-permute-done.12.refs_1_, bf16[256,1024]{1,0:T(8,128)(2,1)S(1)} %collective-permute-done.refs_2_, ...), custom_call_target="tpu_custom_call" | custom-call | flops 1 | bytes 1 | tf_op jit(solution)/shard_map/pallas_call | solution.py:139
Async XLA Ops:
  0.0 10.0 %copy-start = (bf16[1024,3,256]{2,0,1:T(8,128)(2,1)S(1)}, bf16[1024,3,256]{2,0,1:T(8,128)(2,1)}, u32[]{:S(2)}) copy-start(bf16[1024,3,256]{2,0,1:T(8,128)(2,1)} %param.13) | copy-start | bytes 4718596
  0.0 14.8 %collective-permute-start.1 = (bf16[512,2,256]{2,1,0:T(2,128)(2,1)}, bf16[512,2,256]{2,1,0:T(2,128)(2,1)S(1)}, u32[]{:S(2)}, u32[]{:S(2)}) collective-permute-start(bf16[512,2,256]{2,1,0:T(2,128)(2,1)} %bitcast.7), channel_id=1, source_target_pairs={{0,4},{1,9},{2,6},{3,11},{4,0},{5,13},{6,2},{7,15},{8,12},{9,1},{1... | collective-permute-start | bytes 1572872 | tf_op jit(solution)/shard_map/ppermute | solution.py:401
  5.3 7.8 %copy-start.1 = (bf16[256,1024]{1,0:T(8,128)(2,1)S(1)}, bf16[256,1024]{1,0:T(8,128)(2,1)}, u32[]{:S(2)}) copy-start(bf16[256,1024]{1,0:T(8,128)(2,1)} %refs_2_) | copy-start | bytes 1572868
  5.3 9.3 %collective-permute-start.3 = (bf16[272,128]{1,0:T(8,128)(2,1)S(1)}, bf16[272,128]{1,0:T(8,128)(2,1)S(1)}, u32[]{:S(2)}, u32[]{:S(2)}) collective-permute-start(bf16[272,128]{1,0:T(8,128)(2,1)S(1)} %get-tuple-element.29.refs_6_.q_ref), channel_id=1, source_target_pairs={{0,16},{1,21},{2,18},{3,23},{4,20},{5,17},{6,22},{7,19},{8,24},{9,... | collective-permute-start | bytes 208904 | tf_op jit(solution)/shard_map/ppermute | solution.py:401
  7.9 6.9 %collective-permute-start.4 = (bf16[272,128]{1,0:T(8,128)(2,1)S(1)}, bf16[272,128]{1,0:T(8,128)(2,1)S(1)}, u32[]{:S(2)}, u32[]{:S(2)}) collective-permute-start(bf16[272,128]{1,0:T(8,128)(2,1)S(1)} %get-tuple-element.29.refs_6_.q_ref), channel_id=1, source_target_pairs={{0,24},{1,17},{2,26},{3,19},{4,28},{5,21},{6,30},{7,23},{8,16},{9,... | collective-permute-start | bytes 208904 | tf_op jit(solution)/shard_map/ppermute | solution.py:401
  9.3 11.6 %collective-permute-start.5 = (bf16[272,128]{1,0:T(8,128)(2,1)S(1)}, bf16[272,128]{1,0:T(8,128)(2,1)S(1)}, u32[]{:S(2)}, u32[]{:S(2)}) collective-permute-start(bf16[272,128]{1,0:T(8,128)(2,1)S(1)} %get-tuple-element.29.refs_6_.q_ref), channel_id=1, source_target_pairs={{0,8},{1,5},{2,10},{3,7},{4,12},{5,1},{6,14},{7,3},{8,0},{9,13},{1... | collective-permute-start | bytes 208904 | tf_op jit(solution)/shard_map/ppermute | solution.py:401
  9.5 3.6 %collective-permute-start.2 = (s32[4,128]{1,0:T(4,128)S(1)}, s32[4,128]{1,0:T(4,128)S(1)}, u32[]{:S(2)}, u32[]{:S(2)}) collective-permute-start(s32[4,128]{1,0:T(4,128)S(1)} %get-tuple-element.31.code_ref), channel_id=1, source_target_pairs={{0,4},{1,9},{2,6},{3,11},{4,0},{5,13},{6,2},{7,15},{8,12},{9,1},{1... | collective-permute-start | bytes 6152 | tf_op jit(solution)/shard_map/ppermute | solution.py:401
  13.1 12.9 %collective-permute-start = (bf16[256,1024]{1,0:T(8,128)(2,1)S(1)}, bf16[256,1024]{1,0:T(8,128)(2,1)S(1)}, u32[]{:S(2)}, u32[]{:S(2)}) collective-permute-start(bf16[256,1024]{1,0:T(8,128)(2,1)S(1)} %copy-done.1), channel_id=1, source_target_pairs={{0,2},{1,3},{2,0},{3,1},{4,6},{5,7},{6,4},{7,5},{8,10},{9,11},{10,... | collective-permute-start | bytes 1572872 | tf_op jit(solution)/shard_map/ppermute | solution.py:405
  16.9 5.9 %collective-permute-start.6 = (bf16[272,128]{1,0:T(8,128)(2,1)S(1)}, bf16[272,128]{1,0:T(8,128)(2,1)S(1)}, u32[]{:S(2)}, u32[]{:S(2)}) collective-permute-start(bf16[272,128]{1,0:T(8,128)(2,1)S(1)} %get-tuple-element.41), channel_id=1, source_target_pairs={{0,16},{1,21},{2,18},{3,23},{4,20},{5,17},{6,22},{7,19},{8,24},{9,... | collective-permute-start | bytes 208904 | tf_op jit(solution)/shard_map/ppermute | solution.py:401
  19.5 6.4 %collective-permute-start.7 = (bf16[272,128]{1,0:T(8,128)(2,1)S(1)}, bf16[272,128]{1,0:T(8,128)(2,1)S(1)}, u32[]{:S(2)}, u32[]{:S(2)}) collective-permute-start(bf16[272,128]{1,0:T(8,128)(2,1)S(1)} %get-tuple-element.42), channel_id=1, source_target_pairs={{0,24},{1,17},{2,26},{3,19},{4,28},{5,21},{6,30},{7,23},{8,16},{9,... | collective-permute-start | bytes 208904 | tf_op jit(solution)/shard_map/ppermute | solution.py:401
  22.6 4.7 %collective-permute-start.8 = (bf16[272,128]{1,0:T(8,128)(2,1)S(1)}, bf16[272,128]{1,0:T(8,128)(2,1)S(1)}, u32[]{:S(2)}, u32[]{:S(2)}) collective-permute-start(bf16[272,128]{1,0:T(8,128)(2,1)S(1)} %get-tuple-element.46), channel_id=1, source_target_pairs={{0,8},{1,5},{2,10},{3,7},{4,12},{5,1},{6,14},{7,3},{8,0},{9,13},{1... | collective-permute-start | bytes 208904 | tf_op jit(solution)/shard_map/ppermute | solution.py:401
  26.0 3.4 %collective-permute-start.10 = (bf16[256,1024]{1,0:T(8,128)(2,1)S(1)}, bf16[256,1024]{1,0:T(8,128)(2,1)S(1)}, u32[]{:S(2)}, u32[]{:S(2)}) collective-permute-start(bf16[256,1024]{1,0:T(8,128)(2,1)S(1)} %copy-done.1), channel_id=1, source_target_pairs={{0,1},{1,0},{2,3},{3,2},{4,5},{5,4},{6,7},{7,6},{8,9},{9,8},{10,11... | collective-permute-start | bytes 1572872 | tf_op jit(solution)/shard_map/ppermute | solution.py:405
  27.0 6.2 %collective-permute-start.13 = (bf16[256,1024]{1,0:T(8,128)(2,1)S(1)}, bf16[256,1024]{1,0:T(8,128)(2,1)S(1)}, u32[]{:S(2)}, u32[]{:S(2)}) collective-permute-start(bf16[256,1024]{1,0:T(8,128)(2,1)S(1)} %collective-permute-done.refs_2_), channel_id=1, source_target_pairs={{0,1},{1,0},{2,3},{3,2},{4,5},{5,4},{6,7},{7,6},{8,9},{9,8},{10,11... | collective-permute-start | bytes 1572872 | tf_op jit(solution)/shard_map/ppermute | solution.py:405
  27.5 1.9 %collective-permute-start.9 = (bf16[128,256]{1,0:T(8,128)(2,1)S(1)}, bf16[128,256]{1,0:T(8,128)(2,1)S(1)}, u32[]{:S(2)}, u32[]{:S(2)}) collective-permute-start(bf16[128,256]{1,0:T(8,128)(2,1)S(1)} %shard_map.114.refs_0_), channel_id=1, source_target_pairs={{0,1},{1,0},{2,3},{3,2},{4,5},{5,4},{6,7},{7,6},{8,9},{9,8},{10,11... | collective-permute-start | bytes 196616 | tf_op jit(solution)/shard_map/ppermute | solution.py:405
  27.7 4.6 %collective-permute-start.11 = (bf16[128,256]{1,0:T(8,128)(2,1)S(1)}, bf16[128,256]{1,0:T(8,128)(2,1)S(1)}, u32[]{:S(2)}, u32[]{:S(2)}) collective-permute-start(bf16[128,256]{1,0:T(8,128)(2,1)S(1)} %shard_map.114.refs_0_), channel_id=1, source_target_pairs={{0,2},{1,3},{2,0},{3,1},{4,6},{5,7},{6,4},{7,5},{8,10},{9,11},{10,... | collective-permute-start | bytes 196616 | tf_op jit(solution)/shard_map/ppermute | solution.py:405
  28.8 4.3 %collective-permute-start.12 = (bf16[128,256]{1,0:T(8,128)(2,1)S(1)}, bf16[128,256]{1,0:T(8,128)(2,1)S(1)}, u32[]{:S(2)}, u32[]{:S(2)}) collective-permute-start(bf16[128,256]{1,0:T(8,128)(2,1)S(1)} %shard_map.114.refs_0_), channel_id=1, source_target_pairs={{0,3},{1,2},{2,1},{3,0},{4,7},{5,6},{6,5},{7,4},{8,11},{9,10},{10,... | collective-permute-start | bytes 196616 | tf_op jit(solution)/shard_map/ppermute | solution.py:405

commit v8 on v6

--- a/solution.py
+++ b/solution.py
@@ -379,7 +379,7 @@
 def last_kernel(base_ref, *refs):
     *pairs, out_hbm, out_ref, sems = refs
     half = len(pairs) // 2
-    step = 256
+    step = 512
     copies = []
     for i, at in enumerate(range(0, base_ref.shape[1], step)):
         span = slice(at, at + step)
@@ -476,7 +476,7 @@
     total = call(project_kernel, shape(rows, width, dtype=F32), tok, attn, x_near, w_own, w_near)
     return call(
         last_kernel, shape(rows, width), total, x_far, x_last, w_far, w_last,
-        scratch=[pltpu.VMEM((rows, width), BF16), pltpu.SemaphoreType.DMA((width // 256,))],
+        scratch=[pltpu.VMEM((rows, width), BF16), pltpu.SemaphoreType.DMA((width // 512,))],
         leaves=True,
     )
 

time: 34.3 us -> 34.3 us (level)
  no operation moved by 1% of the time
where the time goes in v8:
time: 34.3 us; the launch traced here: 34.2 us
  starting transfers between devices  16.3 us (48%)
  waiting for transfers between devices  9.51 us (28%)
  Pallas kernels  7.59 us (22%)
  between operations  0.75 us (2%)
    ppermute x8, starting transfers between devices, swap(): return lax.ppermute(x, ('seq', 'tp'), pairs)  11.8 us
    pallas_call x8, Pallas kernels, call(): pl.pallas_call(kernel, out_shape=outs, scratch_shapes=scratch, in_specs=[...  7.59 us
    ppermute x8, waiting for transfers between devices, swap(): return lax.ppermute(x, ('seq', 'tp'), pairs)  6.06 us
    ppermute x6, starting transfers between devices, across(): lax.ppermute(x, 'tp', [(t, t ^ mask) for t in range(lax.axis_size('tp'))])  4.48 us
    ppermute x6, waiting for transfers between devices, across(): lax.ppermute(x, 'tp', [(t, t ^ mask) for t in range(lax.axis_size('tp'))])  3.45 us
  transfers between devices with their start and end apart: 14, of which 6 were waited for; matrix products, arithmetic and copies ran while one was open for 0% of the time, Pallas kernels for 19%

profile of v8, /device:TPU:0, one launch (start us, length us, event | category | flops | bytes accessed | tf_op | source)
XLA Modules:
  0.0 34.2 jit_solution(3800852856507652792)
XLA Ops:
  0.0 0.0 copy-start
  0.0 3.0 %collective-permute-start.1 = (bf16[512,2,256]{2,1,0:T(2,128)(2,1)}, bf16[512,2,256]{2,1,0:T(2,128)(2,1)S(1)}, u32[]{:S(2)}, u32[]{:S(2)}) collective-permute-start(bf16[512,2,256]{2,1,0:T(2,128)(2,1)} %bitcast.7), channel_id=1, source_target_pairs={{0,4},{1,9},{2,6},{3,11},{4,0},{5,13},{6,2},{7,15},{8,12},{9,1},{1... | collective-permute-start | bytes 1572872 | tf_op jit(solution)/shard_map/ppermute | solution.py:399
  3.6 1.7 %shard_map.109 = (bf16[272,128]{1,0:T(8,128)(2,1)S(1)}, bf16[128,1024]{1,0:T(8,128)(2,1)S(1)}, f32[32,128]{1,0:T(8,128)S(1)}, bf16[128,1024]{1,0:T(8,128)(2,1)S(...) custom-call(s32[1]{0:T(128)S(6)} %copy.12.len_ref, bf16[128,1024]{1,0:T(8,128)(2,1)} %tok_hbm.1, ...), custom_call_target="tpu_custom_call" | custom-call | flops 1 | bytes 1 | tf_op jit(solution)/shard_map/pallas_call | solution.py:139
  5.3 0.0 copy-start.1
  5.3 2.7 %collective-permute-start.3 = (bf16[272,128]{1,0:T(8,128)(2,1)S(1)}, bf16[272,128]{1,0:T(8,128)(2,1)S(1)}, u32[]{:S(2)}, u32[]{:S(2)}) collective-permute-start(bf16[272,128]{1,0:T(8,128)(2,1)S(1)} %get-tuple-element.30.refs_6_.q_ref), channel_id=1, source_target_pairs={{0,16},{1,21},{2,18},{3,23},{4,20},{5,17},{6,22},{7,19},{8,24},{9,... | collective-permute-start | bytes 208904 | tf_op jit(solution)/shard_map/ppermute | solution.py:399
  8.0 1.3 %collective-permute-start.4 = (bf16[272,128]{1,0:T(8,128)(2,1)S(1)}, bf16[272,128]{1,0:T(8,128)(2,1)S(1)}, u32[]{:S(2)}, u32[]{:S(2)}) collective-permute-start(bf16[272,128]{1,0:T(8,128)(2,1)S(1)} %get-tuple-element.30.refs_6_.q_ref), channel_id=1, source_target_pairs={{0,24},{1,17},{2,26},{3,19},{4,28},{5,21},{6,30},{7,23},{8,16},{9,... | collective-permute-start | bytes 208904 | tf_op jit(solution)/shard_map/ppermute | solution.py:399
  9.3 0.2 collective-permute-start.5
  9.5 0.5 %collective-permute-start.2 = (s32[4,128]{1,0:T(4,128)S(1)}, s32[4,128]{1,0:T(4,128)S(1)}, u32[]{:S(2)}, u32[]{:S(2)}) collective-permute-start(s32[4,128]{1,0:T(4,128)S(1)} %get-tuple-element.33.code_ref), channel_id=1, source_target_pairs={{0,4},{1,9},{2,6},{3,11},{4,0},{5,13},{6,2},{7,15},{8,12},{9,1},{1... | collective-permute-start | bytes 6152 | tf_op jit(solution)/shard_map/ppermute | solution.py:399
  10.0 0.0 copy-done
  10.0 0.6 %shard_map.110 = (bf16[256,128]{1,0:T(8,128)(2,1)S(1)}, bf16[256,128]{1,0:T(8,128)(2,1)S(1)}, bf16[512,256]{1,0:T(8,128)(2,1)S(1)}, bf16[256,512]{1,0:T(8,128)(2,1)S(1)}, bf16[512,128]{1,0:T(8,128)(2,1)S(1)}) custom-call(bf16[128,1024]{1,0:T(8,128)(2,1)S(1)} %get-tuple-element.31.normed_ref, bf16[3,1024,256]{2,1,0:T(8,128)(2,1)S(1)} %bitcast.6, ...), custom_call_target="tpu_custom_call" | custom-call | flops 115300000 | bytes 1 | tf_op jit(solution)/shard_map/pallas_call | solution.py:139
  10.7 2.4 %collective-permute-done.2.code_ref = s32[4,128]{1,0:T(4,128)S(1)} collective-permute-done((s32[4,128]{1,0:T(4,128)S(1)}, s32[4,128]{1,0:T(4,128)S(1)}, u32[]{:S(2)}, u32[]{:S(2)}) %collective-permute-start.2) | collective-permute-done | bytes 2080 | tf_op jit(solution)/shard_map/ppermute | solution.py:399
  13.1 0.0 copy-done.1
  13.1 1.5 %collective-permute-start = (bf16[256,1024]{1,0:T(8,128)(2,1)S(1)}, bf16[256,1024]{1,0:T(8,128)(2,1)S(1)}, u32[]{:S(2)}, u32[]{:S(2)}) collective-permute-start(bf16[256,1024]{1,0:T(8,128)(2,1)S(1)} %copy-done.1), channel_id=1, source_target_pairs={{0,2},{1,3},{2,0},{3,1},{4,6},{5,7},{6,4},{7,5},{8,10},{9,11},{10,... | collective-permute-start | bytes 1572872 | tf_op jit(solution)/shard_map/ppermute | solution.py:403
  14.6 0.0 collective-permute-done.3.refs_0_
  14.6 0.2 collective-permute-done.4.refs_1_
  14.8 0.0 collective-permute-done.1.pool_ref
  14.8 2.0 %shard_map.111 = (bf16[272,128]{1,0:T(8,128)(2,1)S(1)}, bf16[272,128]{1,0:T(8,128)(2,1)S(1)}, bf16[512,256]{1,0:T(8,128)(2,1)S(1)}, bf16[256,512]{1,0:T(8,128)(2,1)S(1)}, bf16[512,128]{1,0:T(8,128)(2,1)S(1)}) custom-call(f32[32,128]{1,0:T(8,128)S(1)} %get-tuple-element.29.rows_ref, bf16[512,256]{1,0:T(8,128)(2,1)S(1)} %get-tuple-element.36.keys_ref.refs_0_, ...), custom_call_target="tpu_custom_call" | custom-call | flops 2305999872 | bytes 1 | tf_op jit(solution)/shard_map/pallas_call | solution.py:139
  16.8 2.7 %collective-permute-start.6 = (bf16[272,128]{1,0:T(8,128)(2,1)S(1)}, bf16[272,128]{1,0:T(8,128)(2,1)S(1)}, u32[]{:S(2)}, u32[]{:S(2)}) collective-permute-start(bf16[272,128]{1,0:T(8,128)(2,1)S(1)} %get-tuple-element.43), channel_id=1, source_target_pairs={{0,16},{1,21},{2,18},{3,23},{4,20},{5,17},{6,22},{7,19},{8,24},{9,... | collective-permute-start | bytes 208904 | tf_op jit(solution)/shard_map/ppermute | solution.py:399
  19.5 1.4 %collective-permute-start.7 = (bf16[272,128]{1,0:T(8,128)(2,1)S(1)}, bf16[272,128]{1,0:T(8,128)(2,1)S(1)}, u32[]{:S(2)}, u32[]{:S(2)}) collective-permute-start(bf16[272,128]{1,0:T(8,128)(2,1)S(1)} %get-tuple-element.44), channel_id=1, source_target_pairs={{0,24},{1,17},{2,26},{3,19},{4,28},{5,21},{6,30},{7,23},{8,16},{9,... | collective-permute-start | bytes 208904 | tf_op jit(solution)/shard_map/ppermute | solution.py:399
  20.9 0.0 collective-permute-done.5.refs_7_
  20.9 1.7 %shard_map.112 = (bf16[272,128]{1,0:T(8,128)(2,1)S(1)}, bf16[272,128]{1,0:T(8,128)(2,1)S(1)}) custom-call(f32[32,128]{1,0:T(8,128)S(1)} %get-tuple-element.29.rows_ref, bf16[512,256]{1,0:T(8,128)(2,1)S(1)} %get-tuple-element.36.keys_ref.refs_0_, bf16[256,512]{1,0:T(8,128)(2,1)S(1)} %get-tuple-element.37.values_ref.refs_1_, ...), custom_call_target="tpu_custom_call" | custom-call | flops 2305999872 | bytes 1 | tf_op jit(solution)/shard_map/pallas_call | solution.py:139
  22.6 0.1 collective-permute-start.8
  22.7 0.0 collective-permute-done.6.refs_1_
  22.7 3.1 %collective-permute-done.7.refs_2_ = bf16[272,128]{1,0:T(8,128)(2,1)S(1)} collective-permute-done((bf16[272,128]{1,0:T(8,128)(2,1)S(1)}, bf16[272,128]{1,0:T(8,128)(2,1)S(1)}, u32[]{:S(2)}, u32[]{:S(2)}) %collective-permute-start.7) | collective-permute-done | bytes 69664 | tf_op jit(solution)/shard_map/ppermute | solution.py:399
  25.9 0.1 shard_map.113
  26.0 0.0 collective-permute-done.refs_2_
  26.0 1.0 %collective-permute-start.10 = (bf16[256,1024]{1,0:T(8,128)(2,1)S(1)}, bf16[256,1024]{1,0:T(8,128)(2,1)S(1)}, u32[]{:S(2)}, u32[]{:S(2)}) collective-permute-start(bf16[256,1024]{1,0:T(8,128)(2,1)S(1)} %copy-done.1), channel_id=1, source_target_pairs={{0,1},{1,0},{2,3},{3,2},{4,5},{5,4},{6,7},{7,6},{8,9},{9,8},{10,11... | collective-permute-start | bytes 1572872 | tf_op jit(solution)/shard_map/ppermute | solution.py:403
  27.0 0.1 collective-permute-start.13
  27.0 0.3 collective-permute-done.8.refs_0_
  27.3 0.1 shard_map.114.refs_0_
  27.5 0.2 collective-permute-start.9
  27.7 1.1 %collective-permute-start.11 = (bf16[128,256]{1,0:T(8,128)(2,1)S(1)}, bf16[128,256]{1,0:T(8,128)(2,1)S(1)}, u32[]{:S(2)}, u32[]{:S(2)}) collective-permute-start(bf16[128,256]{1,0:T(8,128)(2,1)S(1)} %shard_map.114.refs_0_), channel_id=1, source_target_pairs={{0,2},{1,3},{2,0},{3,1},{4,6},{5,7},{6,4},{7,5},{8,10},{9,11},{10,... | collective-permute-start | bytes 196616 | tf_op jit(solution)/shard_map/ppermute | solution.py:403
  28.8 0.6 %collective-permute-start.12 = (bf16[128,256]{1,0:T(8,128)(2,1)S(1)}, bf16[128,256]{1,0:T(8,128)(2,1)S(1)}, u32[]{:S(2)}, u32[]{:S(2)}) collective-permute-start(bf16[128,256]{1,0:T(8,128)(2,1)S(1)} %shard_map.114.refs_0_), channel_id=1, source_target_pairs={{0,3},{1,2},{2,1},{3,0},{4,7},{5,6},{6,5},{7,4},{8,11},{9,10},{10,... | collective-permute-start | bytes 196616 | tf_op jit(solution)/shard_map/ppermute | solution.py:403
  29.4 0.0 collective-permute-done.9.refs_1_
  29.4 0.0 collective-permute-done.10.refs_3_
  29.4 0.3 shard_map.115.base_ref
  29.7 2.6 %collective-permute-done.11.refs_0_ = bf16[128,256]{1,0:T(8,128)(2,1)S(1)} collective-permute-done((bf16[128,256]{1,0:T(8,128)(2,1)S(1)}, bf16[128,256]{1,0:T(8,128)(2,1)S(1)}, u32[]{:S(2)}, u32[]{:S(2)}) %collective-permute-start.11) | collective-permute-done | bytes 65568 | tf_op jit(solution)/shard_map/ppermute | solution.py:403
  32.3 0.8 %collective-permute-done.12.refs_1_ = bf16[128,256]{1,0:T(8,128)(2,1)S(1)} collective-permute-done((bf16[128,256]{1,0:T(8,128)(2,1)S(1)}, bf16[128,256]{1,0:T(8,128)(2,1)S(1)}, u32[]{:S(2)}, u32[]{:S(2)}) %collective-permute-start.12) | collective-permute-done | bytes 65568 | tf_op jit(solution)/shard_map/ppermute | solution.py:403
  33.2 0.0 collective-permute-done.13.refs_3_
  33.2 1.0 %shard_map.116 = bf16[128,1024]{1,0:T(8,128)(2,1)} custom-call(f32[128,1024]{1,0:T(8,128)S(1)} %shard_map.115.base_ref, bf16[128,256]{1,0:T(8,128)(2,1)S(1)} %collective-permute-done.11.refs_0_, bf16[128,256]{1,0:T(8,128)(2,1)S(1)} %collective-permute-done.12.refs_1_, bf16[256,1024]{1,0:T(8,128)(2,1)S(1)} %collective-permute-done.refs_2_, ...), custom_call_target="tpu_custom_call" | custom-call | flops 1 | bytes 1 | tf_op jit(solution)/shard_map/pallas_call | solution.py:139
Async XLA Ops:
  0.0 10.0 %copy-start = (bf16[1024,3,256]{2,0,1:T(8,128)(2,1)S(1)}, bf16[1024,3,256]{2,0,1:T(8,128)(2,1)}, u32[]{:S(2)}) copy-start(bf16[1024,3,256]{2,0,1:T(8,128)(2,1)} %param.13) | copy-start | bytes 4718596
  0.0 14.8 %collective-permute-start.1 = (bf16[512,2,256]{2,1,0:T(2,128)(2,1)}, bf16[512,2,256]{2,1,0:T(2,128)(2,1)S(1)}, u32[]{:S(2)}, u32[]{:S(2)}) collective-permute-start(bf16[512,2,256]{2,1,0:T(2,128)(2,1)} %bitcast.7), channel_id=1, source_target_pairs={{0,4},{1,9},{2,6},{3,11},{4,0},{5,13},{6,2},{7,15},{8,12},{9,1},{1... | collective-permute-start | bytes 1572872 | tf_op jit(solution)/shard_map/ppermute | solution.py:399
  5.3 7.8 %copy-start.1 = (bf16[256,1024]{1,0:T(8,128)(2,1)S(1)}, bf16[256,1024]{1,0:T(8,128)(2,1)}, u32[]{:S(2)}) copy-start(bf16[256,1024]{1,0:T(8,128)(2,1)} %refs_2_) | copy-start | bytes 1572868
  5.3 9.3 %collective-permute-start.3 = (bf16[272,128]{1,0:T(8,128)(2,1)S(1)}, bf16[272,128]{1,0:T(8,128)(2,1)S(1)}, u32[]{:S(2)}, u32[]{:S(2)}) collective-permute-start(bf16[272,128]{1,0:T(8,128)(2,1)S(1)} %get-tuple-element.30.refs_6_.q_ref), channel_id=1, source_target_pairs={{0,16},{1,21},{2,18},{3,23},{4,20},{5,17},{6,22},{7,19},{8,24},{9,... | collective-permute-start | bytes 208904 | tf_op jit(solution)/shard_map/ppermute | solution.py:399
  8.0 6.9 %collective-permute-start.4 = (bf16[272,128]{1,0:T(8,128)(2,1)S(1)}, bf16[272,128]{1,0:T(8,128)(2,1)S(1)}, u32[]{:S(2)}, u32[]{:S(2)}) collective-permute-start(bf16[272,128]{1,0:T(8,128)(2,1)S(1)} %get-tuple-element.30.refs_6_.q_ref), channel_id=1, source_target_pairs={{0,24},{1,17},{2,26},{3,19},{4,28},{5,21},{6,30},{7,23},{8,16},{9,... | collective-permute-start | bytes 208904 | tf_op jit(solution)/shard_map/ppermute | solution.py:399
  9.3 11.6 %collective-permute-start.5 = (bf16[272,128]{1,0:T(8,128)(2,1)S(1)}, bf16[272,128]{1,0:T(8,128)(2,1)S(1)}, u32[]{:S(2)}, u32[]{:S(2)}) collective-permute-start(bf16[272,128]{1,0:T(8,128)(2,1)S(1)} %get-tuple-element.30.refs_6_.q_ref), channel_id=1, source_target_pairs={{0,8},{1,5},{2,10},{3,7},{4,12},{5,1},{6,14},{7,3},{8,0},{9,13},{1... | collective-permute-start | bytes 208904 | tf_op jit(solution)/shard_map/ppermute | solution.py:399
  9.5 3.6 %collective-permute-start.2 = (s32[4,128]{1,0:T(4,128)S(1)}, s32[4,128]{1,0:T(4,128)S(1)}, u32[]{:S(2)}, u32[]{:S(2)}) collective-permute-start(s32[4,128]{1,0:T(4,128)S(1)} %get-tuple-element.33.code_ref), channel_id=1, source_target_pairs={{0,4},{1,9},{2,6},{3,11},{4,0},{5,13},{6,2},{7,15},{8,12},{9,1},{1... | collective-permute-start | bytes 6152 | tf_op jit(solution)/shard_map/ppermute | solution.py:399
  13.1 12.9 %collective-permute-start = (bf16[256,1024]{1,0:T(8,128)(2,1)S(1)}, bf16[256,1024]{1,0:T(8,128)(2,1)S(1)}, u32[]{:S(2)}, u32[]{:S(2)}) collective-permute-start(bf16[256,1024]{1,0:T(8,128)(2,1)S(1)} %copy-done.1), channel_id=1, source_target_pairs={{0,2},{1,3},{2,0},{3,1},{4,6},{5,7},{6,4},{7,5},{8,10},{9,11},{10,... | collective-permute-start | bytes 1572872 | tf_op jit(solution)/shard_map/ppermute | solution.py:403
  16.8 5.9 %collective-permute-start.6 = (bf16[272,128]{1,0:T(8,128)(2,1)S(1)}, bf16[272,128]{1,0:T(8,128)(2,1)S(1)}, u32[]{:S(2)}, u32[]{:S(2)}) collective-permute-start(bf16[272,128]{1,0:T(8,128)(2,1)S(1)} %get-tuple-element.43), channel_id=1, source_target_pairs={{0,16},{1,21},{2,18},{3,23},{4,20},{5,17},{6,22},{7,19},{8,24},{9,... | collective-permute-start | bytes 208904 | tf_op jit(solution)/shard_map/ppermute | solution.py:399
  19.5 6.3 %collective-permute-start.7 = (bf16[272,128]{1,0:T(8,128)(2,1)S(1)}, bf16[272,128]{1,0:T(8,128)(2,1)S(1)}, u32[]{:S(2)}, u32[]{:S(2)}) collective-permute-start(bf16[272,128]{1,0:T(8,128)(2,1)S(1)} %get-tuple-element.44), channel_id=1, source_target_pairs={{0,24},{1,17},{2,26},{3,19},{4,28},{5,21},{6,30},{7,23},{8,16},{9,... | collective-permute-start | bytes 208904 | tf_op jit(solution)/shard_map/ppermute | solution.py:399
  22.6 4.7 %collective-permute-start.8 = (bf16[272,128]{1,0:T(8,128)(2,1)S(1)}, bf16[272,128]{1,0:T(8,128)(2,1)S(1)}, u32[]{:S(2)}, u32[]{:S(2)}) collective-permute-start(bf16[272,128]{1,0:T(8,128)(2,1)S(1)} %get-tuple-element.48), channel_id=1, source_target_pairs={{0,8},{1,5},{2,10},{3,7},{4,12},{5,1},{6,14},{7,3},{8,0},{9,13},{1... | collective-permute-start | bytes 208904 | tf_op jit(solution)/shard_map/ppermute | solution.py:399
  26.0 3.4 %collective-permute-start.10 = (bf16[256,1024]{1,0:T(8,128)(2,1)S(1)}, bf16[256,1024]{1,0:T(8,128)(2,1)S(1)}, u32[]{:S(2)}, u32[]{:S(2)}) collective-permute-start(bf16[256,1024]{1,0:T(8,128)(2,1)S(1)} %copy-done.1), channel_id=1, source_target_pairs={{0,1},{1,0},{2,3},{3,2},{4,5},{5,4},{6,7},{7,6},{8,9},{9,8},{10,11... | collective-permute-start | bytes 1572872 | tf_op jit(solution)/shard_map/ppermute | solution.py:403
  27.0 6.2 %collective-permute-start.13 = (bf16[256,1024]{1,0:T(8,128)(2,1)S(1)}, bf16[256,1024]{1,0:T(8,128)(2,1)S(1)}, u32[]{:S(2)}, u32[]{:S(2)}) collective-permute-start(bf16[256,1024]{1,0:T(8,128)(2,1)S(1)} %collective-permute-done.refs_2_), channel_id=1, source_target_pairs={{0,1},{1,0},{2,3},{3,2},{4,5},{5,4},{6,7},{7,6},{8,9},{9,8},{10,11... | collective-permute-start | bytes 1572872 | tf_op jit(solution)/shard_map/ppermute | solution.py:403
  27.5 1.9 %collective-permute-start.9 = (bf16[128,256]{1,0:T(8,128)(2,1)S(1)}, bf16[128,256]{1,0:T(8,128)(2,1)S(1)}, u32[]{:S(2)}, u32[]{:S(2)}) collective-permute-start(bf16[128,256]{1,0:T(8,128)(2,1)S(1)} %shard_map.114.refs_0_), channel_id=1, source_target_pairs={{0,1},{1,0},{2,3},{3,2},{4,5},{5,4},{6,7},{7,6},{8,9},{9,8},{10,11... | collective-permute-start | bytes 196616 | tf_op jit(solution)/shard_map/ppermute | solution.py:403
  27.7 4.6 %collective-permute-start.11 = (bf16[128,256]{1,0:T(8,128)(2,1)S(1)}, bf16[128,256]{1,0:T(8,128)(2,1)S(1)}, u32[]{:S(2)}, u32[]{:S(2)}) collective-permute-start(bf16[128,256]{1,0:T(8,128)(2,1)S(1)} %shard_map.114.refs_0_), channel_id=1, source_target_pairs={{0,2},{1,3},{2,0},{3,1},{4,6},{5,7},{6,4},{7,5},{8,10},{9,11},{10,... | collective-permute-start | bytes 196616 | tf_op jit(solution)/shard_map/ppermute | solution.py:403
  28.8 4.3 %collective-permute-start.12 = (bf16[128,256]{1,0:T(8,128)(2,1)S(1)}, bf16[128,256]{1,0:T(8,128)(2,1)S(1)}, u32[]{:S(2)}, u32[]{:S(2)}) collective-permute-start(bf16[128,256]{1,0:T(8,128)(2,1)S(1)} %shard_map.114.refs_0_), channel_id=1, source_target_pairs={{0,3},{1,2},{2,1},{3,0},{4,7},{5,6},{6,5},{7,4},{8,11},{9,10},{10,... | collective-permute-start | bytes 196616 | tf_op jit(solution)/shard_map/ppermute | solution.py:403
